TPU v7x, 32 devices: a whole 2x2x4 slice. The times are simulated.
32 devices in a mesh: rep: 2 (over x), fsdp: 2 (over y), ctx: 8 (over z, core).
Axes of the slice: x: 2, y: 2, z: 4, core: 2. Of those that a mesh axis runs over, the one named last changes fastest.
Arguments:
- tokens: bfloat16 [8, 2048, 1024], P(('rep', 'fsdp'), 'ctx'), may hold values from -6 to 6
- segments: int32 [8, 2048], P(('rep', 'fsdp')), may hold values from 0 to 16, as said below
- expand_weight: bfloat16 [2, 1024, 4384], P(None, 'fsdp'), may hold values from -0.1875 to 0.1875
- reduce_weight: bfloat16 [2, 2048, 1024], P(None, 'fsdp'), may hold values from -0.125 to 0.125
- filter_taps: bfloat16 [2, 4, 2304], P(None, None, 'fsdp'), may hold values from -3 to 3
- filter_offset: bfloat16 [2, 2304], P(None, 'fsdp'), may hold values from -1.5 to 1.5
- step_bias: bfloat16 [2, 32], P(None, 'fsdp'), may hold values from -4 to -2
- decay_rate: bfloat16 [2, 32], P(None, 'fsdp'), may hold values from 0 to 0.25, as said below
- skip_gain: bfloat16 [2, 32], P(None, 'fsdp'), may hold values from 0.5 to 1.5
- norm_gain: bfloat16 [2, 1024], P(None, 'fsdp'), may hold values from 0.5 to 1.5
- gate_gain: bfloat16 [2, 2048], P(None, 'fsdp'), may hold values from 0.5 to 1.5
- cotangent: bfloat16 [8, 2048, 1024], P(('rep', 'fsdp'), 'ctx'), may hold values from -6 to 6
Outputs:
- layer_out: bfloat16 [8, 2048, 1024], P(('rep', 'fsdp'), 'ctx')
- token_grads: bfloat16 [8, 2048, 1024], P(('rep', 'fsdp'), 'ctx')
- expand_grads: float32 [2, 1024, 4384], P(None, 'fsdp')
- reduce_grads: float32 [2, 2048, 1024], P(None, 'fsdp')
- filter_grads: float32 [2, 4, 2304], P(None, None, 'fsdp')
- offset_grads: float32 [2, 2304], P(None, 'fsdp')
- step_grads: float32 [2, 32], P(None, 'fsdp')
- decay_grads: float32 [2, 32], P(None, 'fsdp')
- skip_grads: float32 [2, 32], P(None, 'fsdp')
- norm_grads: float32 [2, 1024], P(None, 'fsdp')
- gating_grads: float32 [2, 2048], P(None, 'fsdp')
Inputs may be any that keep to these rules, and one draw needn't show every extreme that they name: `segments`: along each sequence the ids start at 0 and rise by 0 or 1 from one token to the next; tokens with equal ids form one document. Of each 2 consecutive sequences, one holds exactly 2 documents, the first of which ends within the last 256 tokens, and every other one holds exactly 17 documents. `decay_rate`: Positive.
All inputs are finite; a program needn't handle non-finite values.
Results may differ from a plain program's by a relative error of at most 0.019.
The roundings to bfloat16 on the way count: a program that leaves them out, or rounds other values in their place, can miss the bound.
Values may be sent and summed in bfloat16 or wider, within the bound.
No kernel may reach another device: no remote copies, remote signals or barrier semaphores. Data moves between devices by JAX's collectives and lax.ppermute only.
A program may use at most 448 MiB of HBM per device.

v0:
```python
import jax
import jax.numpy as jnp
from jax import lax
from jax.sharding import PartitionSpec as P

H = 32
P_SIZE = 64
N = 128
CONV = 4
LAYERS = 2
DI = 2048
CH = 2304


EPSILON = 1e-05
FULL_PRECISION = lax.Precision.HIGHEST


def shifted(array, axis, by):
    peers = lax.axis_size(axis)
    pairs = [(i, i + by) for i in range(peers) if 0 <= i + by < peers]
    return lax.ppermute(array, axis, pairs)


def carried_in(value, axis, join, neutral, backward):
    count, mine = (lax.axis_size(axis), lax.axis_index(axis))
    pieces = jax.tree.map(lambda part: lax.all_gather(part, axis), value)
    if backward:
        pieces = jax.tree.map(lambda part: part[::-1], pieces)
        mine = count - 1 - mine
    total = jax.tree.map(
        lambda part, zero: jnp.full_like(part, 0) + jnp.asarray(zero, part.dtype), value, neutral
    )

    def lap(position, total):
        longer = join(total, jax.tree.map(lambda part: part[position], pieces))
        return jax.tree.map(lambda new, old: jnp.where(position < mine, new, old), longer, total)

    return lax.fori_loop(0, count - 1, lap, total)


def rms_scale(values, gain):
    return values * lax.rsqrt(jnp.mean(values * values, axis=-1, keepdims=True) + EPSILON) * gain


def combine_states(earlier, later):
    return (earlier[0] * later[0], later[0][:, :, None, None] * earlier[1] + later[1])


def sequence_front(conv_rows, step_raw, seg_rows, taps, offsets, step_bias, decay_rate, skip_gain):
    block_rows = step_raw.shape[0]
    segment = seg_rows[CONV - 1 :]
    filtered = jnp.broadcast_to(offsets, (block_rows, offsets.shape[0]))
    for tap_index in range(CONV):
        same = (seg_rows[tap_index : tap_index + block_rows] == segment).astype(jnp.float32)
        filtered = (
            filtered
            + taps[tap_index] * conv_rows[tap_index : tap_index + block_rows] * same[:, None]
        )
    active = jax.nn.silu(filtered)
    values = active[:, :DI].reshape(block_rows, H, P_SIZE)
    b_keys = active[:, DI : DI + N]
    c_reads = active[:, DI + N :]
    step_size = jax.nn.softplus(step_raw + step_bias)
    joined = (seg_rows[CONV - 1] == seg_rows[CONV - 2]).astype(jnp.float32)
    log_decay = jnp.cumsum(-(step_size * decay_rate[None, :]), axis=0).T
    row_index = lax.broadcasted_iota(jnp.int32, (block_rows, block_rows), 0)
    col_index = lax.broadcasted_iota(jnp.int32, (block_rows, block_rows), 1)
    causal = (segment[:, None] == segment[None, :]) & (row_index >= col_index)
    gap_logs = log_decay[:, :, None] - log_decay[:, None, :]
    decay_mask = jnp.where(causal[None], jnp.exp(jnp.where(causal[None], gap_logs, 0.0)), 0.0)
    scores = jnp.dot(c_reads, b_keys.T, precision=FULL_PRECISION)
    weights = decay_mask * scores[None] * step_size.T[:, None, :]
    within = jnp.einsum("hts,shp->thp", weights, values, precision=FULL_PRECISION)
    within = (within + values * skip_gain[None, :, None]).reshape(block_rows, DI)
    from_start = jnp.exp(log_decay) * joined * (segment == segment[0]).astype(jnp.float32)[None, :]
    to_end = (
        jnp.exp(log_decay[:, -1:] - log_decay)
        * (segment == segment[-1]).astype(jnp.float32)[None, :]
        * step_size.T
    )
    added_state = jnp.einsum("hs,shp,sn->hpn", to_end, values, b_keys, precision=FULL_PRECISION)
    block_decay = (
        jnp.exp(log_decay[:, -1]) * joined * (segment[-1] == segment[0]).astype(jnp.float32)
    )
    return (block_decay, added_state, within, c_reads, from_start)


def front_all(conv_rows, step_raw, seg_rows, taps, offsets, step_bias, decay_rate, skip_gain):

    def per_sequence(pieces):
        return sequence_front(
            pieces[0], pieces[1], pieces[2], taps, offsets, step_bias, decay_rate, skip_gain
        )

    return lax.map(jax.checkpoint(per_sequence), (conv_rows, step_raw, seg_rows))


def back_part(incoming, within, c_reads, from_start, gate_raw, gate_gain):
    carried = jnp.einsum(
        "stn,shpn,sht->sthp", c_reads, incoming, from_start, precision=FULL_PRECISION
    )
    outputs = within + carried.reshape(within.shape)
    gated = outputs * jax.nn.silu(gate_raw)
    return rms_scale(gated, gate_gain)


def small_float(gathered):
    return tuple((item.astype(jnp.float32) for item in gathered[2:7]))


def layer_forward(resid, gathered, seg_rows):
    expand_full, reduce_full = (gathered[0], gathered[1])
    norm_full, gate_full = (gathered[7], gathered[8])
    seq_count, block_rows, width = resid.shape
    normed = rms_scale(resid, norm_full.astype(jnp.float32)).astype(jnp.bfloat16)
    mixed = jnp.dot(normed.reshape(-1, width), expand_full, preferred_element_type=jnp.float32)
    mixed = mixed.astype(jnp.bfloat16).reshape(seq_count, block_rows, -1)
    rim_rows = mixed[:, block_rows - (CONV - 1) :, DI : DI + CH]
    rim_prev = shifted(rim_rows, "ctx", 1)
    conv_rows = jnp.concatenate([rim_prev, mixed[:, :, DI : DI + CH]], axis=1).astype(jnp.float32)
    step_raw = mixed[:, :, DI + CH :].astype(jnp.float32)
    block_decay, added_state, within, c_reads, from_start = front_all(
        conv_rows, step_raw, seg_rows, *small_float(gathered)
    )
    scanned = carried_in(
        (block_decay, added_state),
        "ctx",
        combine_states,
        (jnp.ones_like(block_decay), jnp.zeros_like(added_state)),
        False,
    )
    incoming = scanned[1]
    out_in = back_part(
        incoming,
        within,
        c_reads,
        from_start,
        mixed[:, :, :DI].astype(jnp.float32),
        gate_full.astype(jnp.float32),
    ).astype(jnp.bfloat16)
    branch = jnp.dot(out_in.reshape(-1, DI), reduce_full, preferred_element_type=jnp.float32)
    return (resid + branch.reshape(resid.shape), (mixed, rim_prev, incoming))


def layer_backward(resid, gradient, gathered, saved, seg_rows):
    expand_full, reduce_full = (gathered[0], gathered[1])
    norm_full, gate_full = (gathered[7], gathered[8])
    mixed, rim_prev, incoming = saved
    seq_count, block_rows, width = resid.shape
    normed_float, norm_pull = jax.vjp(rms_scale, resid, norm_full.astype(jnp.float32))
    normed = normed_float.astype(jnp.bfloat16).reshape(-1, width)
    conv_rows = jnp.concatenate([rim_prev, mixed[:, :, DI : DI + CH]], axis=1).astype(jnp.float32)
    step_raw = mixed[:, :, DI + CH :].astype(jnp.float32)
    gate_raw = mixed[:, :, :DI].astype(jnp.float32)

    def front_local(conv_in, step_in, taps_in, offsets_in, bias_in, rate_in, skip_in):
        return front_all(conv_in, step_in, seg_rows, taps_in, offsets_in, bias_in, rate_in, skip_in)

    front_out, front_pull = jax.vjp(front_local, conv_rows, step_raw, *small_float(gathered))
    block_decay, added_state, within, c_reads, from_start = front_out
    out_in, back_pull = jax.vjp(
        back_part, incoming, within, c_reads, from_start, gate_raw, gate_full.astype(jnp.float32)
    )
    grad_low = gradient.astype(jnp.bfloat16).reshape(-1, width)
    out_low = out_in.astype(jnp.bfloat16).reshape(-1, DI)
    reduce_grad = lax.dot_general(
        out_low, grad_low, (((0,), (0,)), ((), ())), preferred_element_type=jnp.float32
    )
    d_out_in = lax.dot_general(
        grad_low, reduce_full, (((1,), (1,)), ((), ())), preferred_element_type=jnp.float32
    )
    d_incoming, d_within, d_reads, d_start, d_gate, gating_grad = back_pull(
        d_out_in.reshape(seq_count, block_rows, DI)
    )
    later_grads = carried_in(
        (block_decay, d_incoming),
        "ctx",
        combine_states,
        (jnp.ones_like(block_decay), jnp.zeros_like(d_incoming)),
        True,
    )
    after_grad = later_grads[1]
    d_decay = jnp.sum(after_grad * incoming, axis=(2, 3))
    pulled = front_pull((d_decay, after_grad, d_within, d_reads, d_start))
    d_conv, d_step = (pulled[0], pulled[1])
    from_next = shifted(d_conv[:, : CONV - 1].astype(jnp.bfloat16), "ctx", -1).astype(jnp.float32)
    d_own = d_conv[:, CONV - 1 :].at[:, block_rows - (CONV - 1) :].add(from_next)
    d_mixed = (
        jnp.concatenate([d_gate, d_own, d_step], axis=2)
        .astype(jnp.bfloat16)
        .reshape(-1, mixed.shape[2])
    )
    expand_grad = lax.dot_general(
        normed, d_mixed, (((0,), (0,)), ((), ())), preferred_element_type=jnp.float32
    )
    d_normed = lax.dot_general(
        d_mixed, expand_full, (((1,), (1,)), ((), ())), preferred_element_type=jnp.float32
    )
    d_resid, norm_grad = norm_pull(d_normed.reshape(seq_count, block_rows, width))
    layer_grads = (
        expand_grad,
        reduce_grad,
        pulled[2],
        pulled[3],
        pulled[4],
        pulled[5],
        pulled[6],
        norm_grad,
        gating_grad,
    )
    return (gradient + d_resid, layer_grads)


def total_grads(layer_grads):
    (
        expand_grad,
        reduce_grad,
        taps_grad,
        offset_grad,
        bias_grad,
        rate_grad,
        skip_grad,
        norm_grad,
        gating_grad,
    ) = layer_grads
    shards = (
        lax.psum_scatter(
            expand_grad.astype(jnp.bfloat16), "fsdp", scatter_dimension=0, tiled=True
        ).astype(jnp.float32),
        lax.psum_scatter(
            reduce_grad.astype(jnp.bfloat16), "fsdp", scatter_dimension=0, tiled=True
        ).astype(jnp.float32),
        lax.psum_scatter(
            taps_grad.astype(jnp.bfloat16), "fsdp", scatter_dimension=1, tiled=True
        ).astype(jnp.float32),
        lax.psum_scatter(
            offset_grad.astype(jnp.bfloat16), "fsdp", scatter_dimension=0, tiled=True
        ).astype(jnp.float32),
        lax.psum_scatter(
            bias_grad.astype(jnp.bfloat16), "fsdp", scatter_dimension=0, tiled=True
        ).astype(jnp.float32),
        lax.psum_scatter(
            rate_grad.astype(jnp.bfloat16), "fsdp", scatter_dimension=0, tiled=True
        ).astype(jnp.float32),
        lax.psum_scatter(
            skip_grad.astype(jnp.bfloat16), "fsdp", scatter_dimension=0, tiled=True
        ).astype(jnp.float32),
        lax.psum_scatter(
            norm_grad.astype(jnp.bfloat16), "fsdp", scatter_dimension=0, tiled=True
        ).astype(jnp.float32),
        lax.psum_scatter(
            gating_grad.astype(jnp.bfloat16), "fsdp", scatter_dimension=0, tiled=True
        ).astype(jnp.float32),
    )
    totals = lax.psum(
        (
            shards[0],
            shards[1],
            shards[2],
            shards[3],
            shards[4],
            shards[5],
            shards[6],
            shards[7],
            shards[8],
        ),
        ("rep", "ctx"),
    )
    return tuple(totals)


def local(
    tokens,
    segments,
    expand_weight,
    reduce_weight,
    filter_taps,
    filter_offset,
    step_bias,
    decay_rate,
    skip_gain,
    norm_gain,
    gate_gain,
    cotangent,
):
    seq_count, block_rows, width = tokens.shape
    start = lax.axis_index("ctx") * block_rows
    padded_seg = jnp.concatenate([jnp.full((seq_count, CONV - 1), -1, jnp.int32), segments], axis=1)
    seg_rows = lax.dynamic_slice_in_dim(padded_seg, start, block_rows + CONV - 1, 1)
    resid = tokens.astype(jnp.float32)
    stored = []
    for layer_index in range(LAYERS):
        gathered = (
            lax.all_gather(expand_weight[layer_index], "fsdp", axis=0, tiled=True),
            lax.all_gather(reduce_weight[layer_index], "fsdp", axis=0, tiled=True),
            lax.all_gather(filter_taps[layer_index], "fsdp", axis=1, tiled=True),
            lax.all_gather(filter_offset[layer_index], "fsdp", axis=0, tiled=True),
            lax.all_gather(step_bias[layer_index], "fsdp", axis=0, tiled=True),
            lax.all_gather(decay_rate[layer_index], "fsdp", axis=0, tiled=True),
            lax.all_gather(skip_gain[layer_index], "fsdp", axis=0, tiled=True),
            lax.all_gather(norm_gain[layer_index], "fsdp", axis=0, tiled=True),
            lax.all_gather(gate_gain[layer_index], "fsdp", axis=0, tiled=True),
        )
        resid_next, saved = layer_forward(resid, gathered, seg_rows)
        stored.append((resid, gathered, saved))
        resid = resid_next
    layer_out = resid.astype(jnp.bfloat16)
    gradient = cotangent.astype(jnp.float32)
    per_layer = [None] * LAYERS
    for layer_index in reversed(range(LAYERS)):
        resid_in, gathered, saved = stored[layer_index]
        gathered = (
            lax.all_gather(expand_weight[layer_index], "fsdp", axis=0, tiled=True),
            lax.all_gather(reduce_weight[layer_index], "fsdp", axis=0, tiled=True),
            lax.all_gather(filter_taps[layer_index], "fsdp", axis=1, tiled=True),
            lax.all_gather(filter_offset[layer_index], "fsdp", axis=0, tiled=True),
            lax.all_gather(step_bias[layer_index], "fsdp", axis=0, tiled=True),
            lax.all_gather(decay_rate[layer_index], "fsdp", axis=0, tiled=True),
            lax.all_gather(skip_gain[layer_index], "fsdp", axis=0, tiled=True),
            lax.all_gather(norm_gain[layer_index], "fsdp", axis=0, tiled=True),
            lax.all_gather(gate_gain[layer_index], "fsdp", axis=0, tiled=True),
        )
        gradient, layer_grads = layer_backward(resid_in, gradient, gathered, saved, seg_rows)
        per_layer[layer_index] = total_grads(layer_grads)
    stacked = tuple(
        (
            jnp.stack([per_layer[layer_index][member] for layer_index in range(LAYERS)])
            for member in range(9)
        )
    )
    return (
        layer_out,
        gradient.astype(jnp.bfloat16),
        stacked[0],
        stacked[1],
        stacked[2],
        stacked[3],
        stacked[4],
        stacked[5],
        stacked[6],
        stacked[7],
        stacked[8],
    )


def solution(mesh):
    placed = (
        P(("rep", "fsdp"), "ctx", None),
        P(("rep", "fsdp"), None),
        P(None, "fsdp", None),
        P(None, "fsdp", None),
        P(None, None, "fsdp"),
        P(None, "fsdp"),
        P(None, "fsdp"),
        P(None, "fsdp"),
        P(None, "fsdp"),
        P(None, "fsdp"),
        P(None, "fsdp"),
        P(("rep", "fsdp"), "ctx", None),
    )
    return jax.shard_map(
        local,
        mesh=mesh,
        in_specs=placed,
        out_specs=(
            P(("rep", "fsdp"), "ctx", None),
            P(("rep", "fsdp"), "ctx", None),
            P(None, "fsdp", None),
            P(None, "fsdp", None),
            P(None, None, "fsdp"),
            P(None, "fsdp"),
            P(None, "fsdp"),
            P(None, "fsdp"),
            P(None, "fsdp"),
            P(None, "fsdp"),
            P(None, "fsdp"),
        ),
        check_vma=False,
    )
```

profile of v0, /device:TPU:0, one launch (start us, length us, event | category | flops | bytes accessed | tf_op | source)
XLA Modules:
  0.0 2458.1 jit_solution(6322295089633025530)
XLA Ops:
  39.4 91.7 %all-gather.39.cloned.1.call-done = bf16[1,1024,4384]{1,2,0:T(8,128)(2,1)} async-done(((bf16[1,512,4384]{1,2,0:T(8,128)(2,1)}), bf16[1,1024,4384]{1,2,0:T(8,128)(2,1)}) %all-gather.39.cloned.1.call-update) | async-done | bytes 8978448 | tf_op jit(solution)/shard_map/all_gather | solution.py:295
  131.1 10.0 fusion.264
  141.1 10.1 reshape.1634
  172.7 78.7 %while.198 = (s32[]{:T(128)}, f32[2,32]{1,0:T(2,128)S(1)}, f32[2,32,64,128]{3,2,1,0:T(8,128)}, f32[2,256,2048]{2,1,0:T(8,128)}, f32[2,256,128]{2,1,0:T(8,128)S(1...) while((s32[]{:T(128)}, f32[2,32]{1,0:T(2,128)S(1)}, ...), condition=%wide.region_4.5_spmd, body=%wide.region_1.4_spmd.sunk | while | flops 2538908416 | bytes 63260508 | solution.py:96
  189.7 13.0 bitcast_add_fusion.20
  229.0 13.0 bitcast_add_fusion.20
  285.6 100.3 %while.201 = (s32[]{:T(128)}, f32[2,32]{1,0:T(2,128)S(1)}, f32[2,256,2048]{2,1,0:T(8,128)}, f32[2,256,128]{1,2,0:T(8,128)S(1)}, f32[2,32,256]{2,1,0:T(8,128)S(1)...) while((s32[]{:T(128)}, f32[2,32]{1,0:T(2,128)S(1)}, ...), condition=%wide.region_49.51_spmd.clone, body=%wide.region_46.50_spmd.clone.sunk | while | flops 1732995200 | bytes 68302488 | solution.py:96
  315.1 13.0 bitcast_add_fusion.23
  365.2 13.0 bitcast_add_fusion.23
  386.5 12.6 all-gather.26
  403.4 27.1 %while.202 = (s32[]{:T(128)}, f32[2,32,64,128]{3,2,1,0:T(8,128)}, s32[]{:T(128)}, f32[8,2,32]{2,1,0:T(2,128)S(1)}, f32[8,2,32,64,128]{4,3,2,1,0:T(8,128)}, /*index=5*/s32[]{:T(128)}, s32[]{:T(128)}) while((s32[]{:T(128)}, f32[2,32,64,128]{3,2,1,0:T(8,128)}, s32[]{:T(128)}, f32[8,2,32]{2,1,0:T(2,128)S(1)}, ...), condition=%wide.region_6.7_spmd.clone, body=%wide.region_5.6_spmd.clone.sunk | while | flops 2097156 | bytes 6292329 | solution.py:39
  472.8 102.1 %all-gather.45.cloned.1.call-done = bf16[1,1024,4384]{1,2,0:T(8,128)(2,1)} async-done(((bf16[1,512,4384]{1,2,0:T(8,128)(2,1)}), bf16[1,1024,4384]{1,2,0:T(8,128)(2,1)}) %all-gather.45.cloned.1.call-update) | async-done | bytes 8978448 | tf_op jit(solution)/shard_map/all_gather | solution.py:295
  585.0 10.2 reshape.1637
  616.4 79.1 %while.199 = (s32[]{:T(128)}, f32[2,32]{1,0:T(2,128)S(1)}, f32[2,32,64,128]{3,2,1,0:T(8,128)}, f32[2,256,2048]{2,1,0:T(8,128)}, f32[2,256,128]{2,1,0:T(8,128)S(1...) while((s32[]{:T(128)}, f32[2,32]{1,0:T(2,128)S(1)}, ...), condition=%wide.region_12.13_spmd, body=%wide.region_9.12_spmd.sunk | while | flops 2538908416 | bytes 63260508 | solution.py:96
  633.6 13.0 bitcast_add_fusion.21
  673.0 13.0 bitcast_add_fusion.21
  705.5 12.4 all-gather.27
  720.5 101.5 %while.200 = (s32[]{:T(128)}, f32[2,32]{1,0:T(2,128)S(1)}, f32[2,256,2048]{2,1,0:T(8,128)}, f32[2,256,128]{1,2,0:T(8,128)S(1)}, f32[2,32,256]{2,1,0:T(8,128)S(1)...) while((s32[]{:T(128)}, f32[2,32]{1,0:T(2,128)S(1)}, ...), condition=%wide.region_19.20_spmd.clone, body=%wide.region_16.19_spmd.clone.sunk | while | flops 1732995200 | bytes 68302488 | solution.py:96
  750.5 13.1 bitcast_add_fusion.22
  801.2 13.1 bitcast_add_fusion.22
  822.0 25.4 %all-gather.47.cloned.1.call-done = f32[16,32,64,128]{3,2,1,0:T(8,128)} async-done(((f32[2,32,64,128]{3,2,1,0:T(8,128)}), f32[16,32,64,128]{3,2,1,0:T(8,128)}) %all-gather.47.cloned.1.call-update) | async-done | bytes 16777232 | tf_op jit(solution)/shard_map/all_gather | solution.py:27
  847.4 27.3 %while.203 = (s32[]{:T(128)}, f32[2,32,64,128]{3,2,1,0:T(8,128)}, s32[]{:T(128)}, f32[8,2,32]{2,1,0:T(2,128)S(1)}, f32[8,2,32,64,128]{4,3,2,1,0:T(8,128)}, /*index=5*/s32[]{:T(128)}, s32[]{:T(128)}) while((s32[]{:T(128)}, f32[2,32,64,128]{3,2,1,0:T(8,128)}, s32[]{:T(128)}, f32[8,2,32]{2,1,0:T(2,128)S(1)}, ...), condition=%wide.region_14.15_spmd.clone, body=%wide.region_13.14_spmd.clone.sunk | while | flops 2097156 | bytes 6292329 | solution.py:39
  905.7 11.6 multiply_reduce_fusion.20
  935.1 10.3 all-gather.28
  945.4 10.0 fusion.327
  959.4 125.2 %all-gather.51.cloned.1.call-done = f32[16,32,64,128]{3,2,1,0:T(8,128)} async-done(((f32[2,32,64,128]{3,2,1,0:T(8,128)}), f32[16,32,64,128]{3,2,1,0:T(8,128)}) %all-gather.51.cloned.1.call-update) | async-done | bytes 16777232 | tf_op jit(solution)/shard_map/all_gather | solution.py:27
  1084.6 12.0 rev.13
  1096.5 26.6 %while.204 = (s32[]{:T(128)}, f32[2,32,64,128]{3,2,1,0:T(8,128)}, s32[]{:T(128)}, f32[8,2,32]{2,1,0:T(2,128)S(1)}, f32[8,2,32,64,128]{4,3,2,1,0:T(8,128)}, /*index=5*/s32[]{:T(128)}, s32[]{:T(128)}) while((s32[]{:T(128)}, f32[2,32,64,128]{3,2,1,0:T(8,128)}, s32[]{:T(128)}, f32[8,2,32]{2,1,0:T(2,128)S(1)}, ...), condition=%wide.region_23.24_spmd.clone, body=%wide.region_22.23_spmd.clone.sunk | while | flops 2097156 | bytes 6292329 | solution.py:39
  1128.8 195.4 %while.205 = (s32[]{:T(128)}, f32[2304]{0:T(1024)}, f32[4,2304]{1,0:T(4,128)}, f32[32]{0:T(128)}, f32[32]{0:T(128)}, /*index=5*/f32[32]{0:T(128)}, f32[2,259,230...) while((s32[]{:T(128)}, f32[2304]{0:T(1024)}, ...), condition=%wide.region_44.46_spmd.clone, body=%wide.region_25.45_spmd.clone.sunk | while | flops 5210002432 | bytes 210299216 | solution.py:96
  1161.2 16.0 fusion.562
  1258.6 16.0 fusion.562
  1343.5 13.6 scatter-add.6
  1357.1 10.6 multiply_reduce_fusion.28
  1411.3 10.5 all-gather.29
  1435.8 13.7 bitcast_convert_fusion
  1449.6 94.4 %all-gather.53.cloned.1.call-done = f32[16,32,64,128]{3,2,1,0:T(8,128)} async-done(((f32[2,32,64,128]{3,2,1,0:T(8,128)}), f32[16,32,64,128]{3,2,1,0:T(8,128)}) %all-gather.53.cloned.1.call-update) | async-done | bytes 16777232 | tf_op jit(solution)/shard_map/all_gather | solution.py:27
  1543.9 12.1 rev.15
  1556.0 27.0 %while.206 = (s32[]{:T(128)}, f32[2,32,64,128]{3,2,1,0:T(8,128)}, s32[]{:T(128)}, f32[8,2,32]{2,1,0:T(2,128)S(1)}, f32[8,2,32,64,128]{4,3,2,1,0:T(8,128)}, /*index=5*/s32[]{:T(128)}, s32[]{:T(128)}) while((s32[]{:T(128)}, f32[2,32,64,128]{3,2,1,0:T(8,128)}, s32[]{:T(128)}, f32[8,2,32]{2,1,0:T(2,128)S(1)}, ...), condition=%wide.region_53.55_spmd.clone, body=%wide.region_52.54_spmd.clone.sunk | while | flops 2097156 | bytes 6292329 | solution.py:39
  1588.7 194.1 %while.207 = (s32[]{:T(128)}, f32[2304]{0:T(1024)}, f32[4,2304]{1,0:T(4,128)}, f32[32]{0:T(128)}, f32[32]{0:T(128)}, /*index=5*/f32[32]{0:T(128)}, f32[2,259,230...) while((s32[]{:T(128)}, f32[2304]{0:T(1024)}, ...), condition=%wide.region_74.76_spmd.clone, body=%wide.region_55.75_spmd.clone.sunk | while | flops 5210002432 | bytes 209963280 | solution.py:96
  1619.9 15.9 fusion.588
  1716.9 15.9 fusion.588
  1801.1 13.6 scatter-add.9
  1814.7 10.3 bitcast_convert_fusion.1
  1843.5 87.6 %reduce-scatter.11.cloned.1.call-done = bf16[512,4384]{0,1:T(8,128)(2,1)} async-done(((bf16[1024,4384]{0,1:T(8,128)(2,1)}), bf16[512,4384]{0,1:T(8,128)(2,1)}) %reduce-scatter.11.cloned.1.call-update) | async-done | bytes 4489232 | tf_op jit(solution)/shard_map/reduce_scatter | solution.py:228
  1951.5 11.0 fusion.305
  1974.8 63.4 %all-reduce.45 = (f32[1,4,1152]{2,1,0:T(4,128)S(1)}, f32[1,4,1152]{2,1,0:T(4,128)S(1)}, f32[1,1152]{1,0:T(1,128)S(1)}, f32[1,1152]{1,0:T(1,128)S(1)}, f32[1,16]{...) all-reduce(f32[1,4,1152]{2,1,0:T(4,128)S(1)} %bitcast_convert_fusio, ...), channel_id=1, replica_groups=mesh['rep'=2,'fsdp'=2,'ctx'=8] {'rep','ctx'}, use_global_device_ids=true, to_apply=%region_87.89 | all-reduce | flops 14688 | bytes 117504 | tf_op jit(solution)/shard_map/psum | solution.py:256
  2042.4 389.8 %all-reduce.51.cloned.1.call-done = (f32[1,512,4384]{1,2,0:T(8,128)}, f32[1,512,4384]{1,2,0:T(8,128)}, f32[1,1024,1024]{2,1,0:T(8,128)}, f32[1,1024,1024]{2,1,0:T(8,128)}) async-done(((f32[1,512,4384]{1,2,0:T(8,128)}, f32[1,512,4384]{1,2,0:T(8,128)}, f32[1,1024,1024]{2,1,0:T(8,128)}, f32[1,1024,1024]{2,1,0:T(8,128)}), (f32[1,512,4384]{1,2,0:T(8,128)}, f32[1,512,4384]{1,2,0:T(8,128)}, ...) | async-done | bytes 26345488 | tf_op jit(solution)/shard_map/psum | solution.py:256
  2440.9 10.5 pad_maximum_fusion
  (1538 shorter events, 1051.1 us)
Async XLA Ops:
  7.2 123.9 %all-gather.39.cloned.1.call-start = ((), (), s32[]{:S(2)}) async-start(), calls=%async_computation.10 | async-start | bytes 13467648 | tf_op jit(solution)/shard_map/all_gather | solution.py:295
  15.1 18.0 copy-start.184
  15.1 22.5 copy-start.188
  15.1 22.6 copy-start.37
  15.1 388.3 %all-gather.41.cloned.1.call-start = ((), (), s32[]{:S(2)}) async-start(), calls=%async_computation.11 | async-start | bytes 18874368 | tf_op jit(solution)/shard_map/all_gather | solution.py:27
  21.0 120.1 %copy-start.163 = (f32[1,1024]{1,0:T(1,128)}, f32[1,1024]{1,0:T(1,128)S(1)}, u32[]{:S(2)}) copy-start(f32[1,1024]{1,0:T(1,128)S(1)} %convert_element_type.623) | copy-start | bytes 12292
  38.0 103.1 %copy-start.181 = (f32[2,256]{1,0:T(2,128)}, f32[2,256]{1,0:T(2,128)S(1)}, u32[]{:S(2)}) copy-start(f32[2,256]{1,0:T(2,128)S(1)} %fusion.309) | copy-start | bytes 6148
  39.1 102.0 %copy-start.179 = (f32[2,256]{1,0:T(2,128)}, f32[2,256]{1,0:T(2,128)S(1)}, u32[]{:S(2)}) copy-start(f32[2,256]{1,0:T(2,128)S(1)} %fusion.345) | copy-start | bytes 6148
  39.4 101.7 %copy-start.100 = (bf16[2,256,1024]{2,1,0:T(8,128)(2,1)}, bf16[2,256,1024]{2,1,0:T(8,128)(2,1)S(1)}, u32[]{:S(2)}) copy-start(bf16[2,256,1024]{2,1,0:T(8,128)(2,1)S(1)} %fusion.304) | copy-start | bytes 3145732
  155.7 8.5 collective-permute-start
  251.5 212.7 %all-gather.43.cloned.1.call-start = ((), (), s32[]{:S(2)}) async-start(), calls=%async_computation.12 | async-start | bytes 6291456 | tf_op jit(solution)/shard_map/all_gather | solution.py:296
  256.3 318.7 %all-gather.45.cloned.1.call-start = ((), (), s32[]{:S(2)}) async-start(), calls=%async_computation.13 | async-start | bytes 13467648 | tf_op jit(solution)/shard_map/all_gather | solution.py:295
  256.9 21.3 slice-start.6
  256.9 590.5 %all-gather.47.cloned.1.call-start = ((), (), s32[]{:S(2)}) async-start(), calls=%async_computation.14 | async-start | bytes 18874368 | tf_op jit(solution)/shard_map/all_gather | solution.py:27
  261.9 202.3 %copy-start.167 = (f32[1,2048]{1,0:T(1,128)}, f32[1,2048]{1,0:T(1,128)S(1)}, u32[]{:S(2)}) copy-start(f32[1,2048]{1,0:T(1,128)S(1)} %convert_element_type.629) | copy-start | bytes 24580
  285.6 100.9 %copy-start.225 = (f32[2,32]{1,0:T(2,128)S(1)}, f32[2,32]{1,0:T(2,128)}, u32[]{:S(2)}) copy-start(f32[2,32]{1,0:T(2,128)} %copy-done.224) | copy-start | bytes 772
  385.9 17.5 copy-start.51
  385.9 17.5 copy-start.61
  385.9 44.6 %copy-start.82 = (f32[2,256,128]{1,2,0:T(8,128)}, f32[2,256,128]{1,2,0:T(8,128)S(1)}, u32[]{:S(2)}) copy-start(f32[2,256,128]{1,2,0:T(8,128)S(1)} %get-tuple-element.1816) | copy-start | bytes 786436
  385.9 44.6 %copy-start.98 = (f32[2,32,256]{2,1,0:T(8,128)}, f32[2,32,256]{2,1,0:T(8,128)S(1)}, u32[]{:S(2)}) copy-start(f32[2,32,256]{2,1,0:T(8,128)S(1)} %get-tuple-element.1815) | copy-start | bytes 196612
  471.3 113.7 %copy-start.213 = (f32[2,256]{1,0:T(2,128)}, f32[2,256]{1,0:T(2,128)S(1)}, u32[]{:S(2)}) copy-start(f32[2,256]{1,0:T(2,128)S(1)} %get-tuple-element.2941) | copy-start | bytes 6148
  471.3 113.7 %copy-start.186 = (f32[2,256]{1,0:T(2,128)}, f32[2,256]{1,0:T(2,128)S(1)}, u32[]{:S(2)}) copy-start(f32[2,256]{1,0:T(2,128)S(1)} %fusion.346) | copy-start | bytes 6148
  472.8 112.2 %copy-start.101 = (bf16[2,256,1024]{2,1,0:T(8,128)(2,1)}, bf16[2,256,1024]{2,1,0:T(8,128)(2,1)S(1)}, u32[]{:S(2)}) copy-start(bf16[2,256,1024]{2,1,0:T(8,128)(2,1)S(1)} %multiply_convert_fusion.8) | copy-start | bytes 3145732
  599.6 8.2 collective-permute-start.1
  695.5 210.1 %all-gather.49.cloned.1.call-start = ((), (), s32[]{:S(2)}) async-start(), calls=%async_computation.15 | async-start | bytes 6291456 | tf_op jit(solution)/shard_map/all_gather | solution.py:296
  696.1 388.4 %all-gather.51.cloned.1.call-start = ((), (), s32[]{:S(2)}) async-start(), calls=%async_computation.16 | async-start | bytes 18874368 | tf_op jit(solution)/shard_map/all_gather | solution.py:27
  700.8 216.5 %copy-start.169 = (f32[1,2048]{1,0:T(1,128)}, f32[1,2048]{1,0:T(1,128)S(1)}, u32[]{:S(2)}) copy-start(f32[1,2048]{1,0:T(1,128)S(1)} %convert_element_type.636) | copy-start | bytes 24580
  847.4 27.3 %copy-start.143 = (f32[2,32,256]{2,1,0:T(8,128)S(1)}, f32[2,32,256]{2,1,0:T(8,128)}, u32[]{:S(2)}) copy-start(f32[2,32,256]{2,1,0:T(8,128)} %copy-done.142) | copy-start | bytes 196612
  935.0 609.0 %all-gather.53.cloned.1.call-start = ((), (), s32[]{:S(2)}) async-start(), calls=%async_computation.17 | async-start | bytes 18874368 | tf_op jit(solution)/shard_map/all_gather | solution.py:27
  1161.2 16.7 copy-start.35
  1161.2 18.6 copy-start.86
  1258.6 16.7 copy-start.35
  1258.6 18.6 copy-start.86
  1329.8 11.2 collective-permute-start.2
  1393.1 432.0 %reduce-scatter.17.cloned.1.call-start = ((), (), s32[]{:S(2)}) async-start(), calls=%async_computation.9 | async-start | bytes 6291456 | tf_op jit(solution)/shard_map/reduce_scatter | solution.py:231
  1401.4 429.2 %reduce-scatter.15.cloned.1.call-start = ((), (), s32[]{:S(2)}) async-start(), calls=%async_computation.8 | async-start | bytes 6291456 | tf_op jit(solution)/shard_map/reduce_scatter | solution.py:231
  1410.6 424.5 %reduce-scatter.13.cloned.1.call-start = ((), (), s32[]{:S(2)}) async-start(), calls=%async_computation.7 | async-start | bytes 13467648 | tf_op jit(solution)/shard_map/reduce_scatter | solution.py:228
  1449.5 481.6 %reduce-scatter.11.cloned.1.call-start = ((), (), s32[]{:S(2)}) async-start(), calls=%async_computation.6 | async-start | bytes 13467648 | tf_op jit(solution)/shard_map/reduce_scatter | solution.py:228
  1619.9 16.6 copy-start.36
  1619.9 18.6 copy-start.88
  1716.9 16.6 copy-start.36
  1716.9 18.5 copy-start.88
  1788.4 10.3 collective-permute-start.3
  1825.0 125.2 %reduce-scatter.21.cloned.1.call-start = ((), (), s32[]{:S(2)}) async-start(), calls=%async_computation.19 | async-start | bytes 884736
  1830.3 143.4 %reduce-scatter.19.cloned.1.call-start = ((), (), s32[]{:S(2)}) async-start(), calls=%async_computation.18 | async-start | bytes 884736
  1843.4 588.8 %all-reduce.51.cloned.1.call-start = ((), (), s32[]{:S(2)}) async-start(), calls=%async_computation.20 | async-start | bytes 52690944 | tf_op jit(solution)/shard_map/psum | solution.py:256
  1951.5 19.0 copy-start.182
  1951.5 19.0 copy-start.50
  (350 other events, 1794.0 us)
Sparse Core Ops, SparseCore 0:
  15.2 115.7 all-gather.38
  251.6 151.7 all-gather.40
  405.0 54.9 all-gather.42
  462.0 112.9 all-gather.44
  695.7 151.6 all-gather.46
  848.8 54.9 all-gather.48
  935.1 149.4 all-gather.50
  1393.3 150.6 all-gather.52
  1546.2 52.5 reduce-scatter.16
  1601.0 54.3 reduce-scatter.14
  1657.7 105.6 reduce-scatter.12
  1825.1 105.8 reduce-scatter.10
  1933.9 15.2 reduce-scatter.20
  1951.5 15.2 reduce-scatter.18
  1972.0 460.1 all-reduce.50
where the time goes:
time: 2470 us; the launch traced here: 2460 us
  waiting for transfers between devices  922 us (37%)
  local copies, waits for them, and re-layouts  483 us (20%)
  matrix products  454 us (18%)
  other arithmetic  379 us (15%)
  blocking collectives  157 us (6%)
  loops' own time  35.6 us (1%)
    psum x1, waiting for transfers between devices, total_grads(): lax.psum((shards[0], shards[1], shards[2], shards[3], shards[4], shards[5...  390 us
    all_gather x4, waiting for transfers between devices, carried_in(): pieces = jax.tree.map(lambda part: lax.all_gather(part, axis), value)  249 us
    dot_general x16, matrix products, sequence_front(): jnp.einsum('hts,shp->thp', weights, values, precision=FULL_PRECISION)  207 us
    all_gather x2, waiting for transfers between devices, local(): lax.all_gather(expand_weight[layer_index], 'fsdp', axis=0, tiled=True)  194 us
    select_n x28, other arithmetic, lap(): jnp.where(position < mine, new, old)  108 us
    reduce_scatter x2, waiting for transfers between devices, total_grads(): lax.psum_scatter(expand_grad.astype(jnp.bfloat16), 'fsdp', scatter_dimens...  87.6 us
    while x548, local copies, waits for them, and re-layouts  72 us
    psum x1, blocking collectives, total_grads(): lax.psum((shards[0], shards[1], shards[2], shards[3], shards[4], shards[5...  63.4 us
  transfers between devices with their start and end apart: 19, of which 8 were waited for; matrix products, arithmetic and copies ran while one was open for 30% of the time, Pallas kernels for 0%

commit v1 on v0

v1 whole, which is shorter than its diff:
```python
import functools

import jax
import jax.numpy as jnp
from jax import lax
from jax.experimental import pallas as pl
from jax.experimental.pallas import tpu as pltpu
from jax.sharding import Mesh, PartitionSpec as P

H = 32
P_SIZE = 64
N = 128
CONV = 4
LAYERS = 2
DI = 2048
CH = 2304
D = 1024
EPSILON = 1e-05
Q = 128
LANES = 128
PAIRS = DI // LANES
BLOCKS = CH // LANES
KEYS, READS, KEYS_REST, READS_REST = (slice(DI + i * N, DI + (i + 1) * N) for i in range(4))
ACT = DI + 4 * N
FAR = -1e30
F32 = jnp.float32
BF16 = jnp.bfloat16
VMEM_LIMIT = 56 * 1024 * 1024


def dot_nn(a, b):
    return lax.dot_general(a, b, (((1,), (0,)), ((), ())), preferred_element_type=F32)


def dot_nt(a, b):
    return lax.dot_general(a, b, (((1,), (1,)), ((), ())), preferred_element_type=F32)


def dot_tn(a, b):
    return lax.dot_general(a, b, (((0,), (0,)), ((), ())), preferred_element_type=F32)


def dot_full(a, b):
    return lax.dot_general(
        a, b, (((1,), (0,)), ((), ())), precision=lax.Precision.HIGHEST, preferred_element_type=F32
    )


def two_parts(x):
    high = x.astype(BF16)
    return high, (x - high.astype(F32)).astype(BF16)


def low_lanes():
    return lax.broadcasted_iota(jnp.int32, (Q, LANES), 1) < P_SIZE


def spread(table, first, pair, low):
    a = table[:, first + 2 * pair : first + 2 * pair + 1]
    b = table[:, first + 2 * pair + 1 : first + 2 * pair + 2]
    return jnp.where(low, a, b)


def column(table, index):
    return table[:, index : index + 1]


def lanes_of(index):
    return pl.ds(index * LANES, LANES)


def fold_rows(x):
    return jnp.sum(x.reshape(x.shape[0] // 8, 8, x.shape[1]), axis=0)


STEP, LOGS, TO_END, FROM_START = 0, 32, 64, 96


def front_kernel(
    u_ref, s_ref, rim_ref, segx_ref, taps_ref, heads_ref, oht_ref,
    act_ref, slope_ref, aux_ref, lt_ref, drow_ref, sout_ref, msg_ref,
    ubuf, state, decay, xbuf,
):
    c = pl.program_id(0)

    @pl.when(c == 0)
    def _():
        ubuf[0:8, :] = rim_ref[...].astype(F32)
        state[...] = jnp.zeros_like(state)
        decay[...] = jnp.ones_like(decay)

    @pl.when(c > 0)
    def _():
        ubuf[0:8, :] = ubuf[Q : Q + 8, :]

    seg_rows = segx_ref[pl.ds(pl.multiple_of(c * Q, Q), Q + 8), :]
    seg = seg_rows[8:]
    masks = [(seg_rows[5 + k : 5 + k + Q] == seg).astype(F32) for k in range(CONV - 1)]
    for j in range(BLOCKS):
        cols = lanes_of(j)
        ubuf[8 : 8 + Q, cols] = u_ref[:, cols].astype(F32)
        filtered = taps_ref[4:5, cols] + taps_ref[3:4, cols] * ubuf[8 : 8 + Q, cols]
        for k in range(CONV - 1):
            filtered += taps_ref[k : k + 1, cols] * (ubuf[5 + k : 5 + k + Q, cols] * masks[k])
        gate = 1.0 / (1.0 + jnp.exp(-filtered))
        active = filtered * gate
        act_ref[:, cols] = active.astype(BF16)
        if j >= PAIRS:
            act_ref[:, lanes_of(j + 2)] = two_parts(active)[1]
        slope_ref[:, cols] = (gate * (1.0 + filtered - active)).astype(BF16)

    raw = s_ref[...].astype(F32) + heads_ref[0:1, :]
    step = jnp.maximum(raw, 0.0) + jnp.log1p(jnp.exp(-jnp.abs(raw)))
    rows = lax.broadcasted_iota(jnp.int32, (Q, Q), 0)
    lane = lax.broadcasted_iota(jnp.int32, (Q, Q), 1)
    logs = dot_full((rows >= lane).astype(F32), -(step * heads_ref[1:2, :]))
    last = logs[Q - 1 : Q, :]
    joined = (seg_rows[8:9] == seg_rows[7:8]).astype(F32)
    to_end = jnp.exp(last - logs) * (seg == seg[Q - 1 : Q]).astype(F32)
    from_start = jnp.exp(logs) * (joined * (seg == seg[0:1]).astype(F32))
    aux = jnp.where(
        lane < 64, jnp.where(lane < 32, step, logs), jnp.where(lane < 96, to_end, from_start)
    )
    aux_ref[...] = aux
    lt_ref[0] = logs.T[:H, :]
    through = jnp.exp(last) * joined * (seg[Q - 1 : Q] == seg[0:1]).astype(F32)
    before = decay[0:1, :]
    after = before * through
    row16 = lax.broadcasted_iota(jnp.int32, (16, LANES), 0)
    table = jnp.where(row16 == 0, through, jnp.where(row16 == 1, before, after))
    high, rest = two_parts(table)
    drow = dot_nn(high, oht_ref[...]) + dot_nn(rest, oht_ref[...])
    drow_ref[0] = drow[0:8]
    decay[...] = jnp.broadcast_to(after, decay.shape)

    low = low_lanes()
    for j in range(PAIRS):
        scaled = (spread(aux, STEP, j, low) * act_ref[:, lanes_of(j)].astype(F32)).astype(BF16)
        xbuf[:, lanes_of(j)] = (spread(aux, TO_END, j, low) * scaled.astype(F32)).astype(BF16)
    keys = act_ref[:, KEYS].astype(F32).T.astype(BF16)
    held = state[...] * drow[0:1, :] + dot_nn(keys, xbuf[...])
    state[...] = held
    sout_ref[0] = held
    msg_ref[0:N, :] = held
    msg_ref[N : N + 8, :] = jnp.broadcast_to(drow[2:3], (8, DI))


def within_kernel(act_ref, aux_ref, lt_ref, segx_ref, segr_ref, sprev_ref, skip_ref, y_ref):
    c = pl.program_id(0)
    seg = segx_ref[pl.ds(pl.multiple_of(c * Q + 8, 8), Q), :]
    rows = lax.broadcasted_iota(jnp.int32, (Q, Q), 0)
    lane = lax.broadcasted_iota(jnp.int32, (Q, Q), 1)
    bias = jnp.where((rows >= lane) & (seg == segr_ref[0, 0:1, :]), 0.0, FAR)
    reads = act_ref[:, READS]
    reads_both = jnp.concatenate([reads, act_ref[:, READS_REST]], axis=1)
    keys_twice = jnp.concatenate([act_ref[:, KEYS]] * 2, axis=1)
    scores = dot_nt(reads_both, keys_twice) + dot_nt(reads, act_ref[:, KEYS_REST])
    aux = aux_ref[...]
    low = low_lanes()
    has_prev = (c > 0).astype(F32)
    for j in range(PAIRS):
        cols = lanes_of(j)
        weights = [
            (jnp.exp(column(aux, LOGS + h) - lt_ref[0, h : h + 1, :] + bias) * scores).astype(BF16)
            for h in (2 * j, 2 * j + 1)
        ]
        values = act_ref[:, cols].astype(F32)
        scaled = spread(aux, STEP, j, low) * values
        stack = jnp.concatenate(
            [jnp.where(low, scaled, 0.0), jnp.where(low, 0.0, scaled)], axis=0
        ).astype(BF16)
        high, rest = two_parts(sprev_ref[0, :, cols])
        carried = dot_nn(reads_both, jnp.concatenate([high, high], axis=0)) + dot_nn(reads, rest)
        carried *= spread(aux, FROM_START, j, low) * has_prev
        y_ref[:, cols] = (
            dot_nn(jnp.concatenate(weights, axis=1), stack)
            + carried
            + skip_ref[0:1, cols] * values
        )


def gate_kernel(
    yloc_ref, aux_ref, drow_ref, sin_ref, reads_ref, rest_ref, z_ref, gain_ref, y_ref, out_ref, gbuf
):
    aux = aux_ref[...]
    reads = reads_ref[...]
    reads_both = jnp.concatenate([reads, rest_ref[...]], axis=1)
    low = low_lanes()
    total = jnp.zeros((Q, LANES), F32)
    for j in range(PAIRS):
        cols = lanes_of(j)
        high, rest = two_parts(sin_ref[:, cols])
        carried = dot_nn(reads_both, jnp.concatenate([high, high], axis=0)) + dot_nn(reads, rest)
        y = yloc_ref[:, cols] + carried * (spread(aux, FROM_START, j, low) * drow_ref[0, 1:2, cols])
        y_ref[:, cols] = y
        z = z_ref[:, cols].astype(F32)
        gated = y * (z / (1.0 + jnp.exp(-z)))
        gbuf[:, cols] = gated
        total += gated * gated
    scale = lax.rsqrt(jnp.sum(total, axis=1, keepdims=True) * (1.0 / DI) + EPSILON)
    for j in range(PAIRS):
        cols = lanes_of(j)
        out_ref[:, cols] = (gbuf[:, cols] * scale * gain_ref[0:1, cols]).astype(BF16)


def gate_back_kernel(
    dout_ref, y_ref, z_ref, gain_ref, reads_ref, aux_ref, drow_ref,
    dy_ref, rest_ref, dz_ref, ggrad_ref, zloc_ref, gmsg_ref, dsuf_ref,
    gbuf, grad_state, suffix, xbuf,
):
    @pl.when(pl.program_id(0) == 0)
    def _():
        ggrad_ref[...] = jnp.zeros_like(ggrad_ref)
        grad_state[...] = jnp.zeros_like(grad_state)
        suffix[...] = jnp.ones_like(suffix)

    aux = aux_ref[...]
    low = low_lanes()
    total = jnp.zeros((Q, LANES), F32)
    cross = jnp.zeros((Q, LANES), F32)
    for j in range(PAIRS):
        cols = lanes_of(j)
        z = z_ref[:, cols].astype(F32)
        gated = y_ref[:, cols] * (z / (1.0 + jnp.exp(-z)))
        gbuf[:, cols] = gated
        total += gated * gated
        cross += gated * (dout_ref[:, cols] * gain_ref[0:1, cols])
    scale = lax.rsqrt(jnp.sum(total, axis=1, keepdims=True) * (1.0 / DI) + EPSILON)
    pull = jnp.sum(cross, axis=1, keepdims=True) * (scale * scale * scale * (1.0 / DI))
    scale = jnp.broadcast_to(scale, (Q, LANES))
    pull = jnp.broadcast_to(pull, (Q, LANES))
    for j in range(PAIRS):
        cols = lanes_of(j)
        z = z_ref[:, cols].astype(F32)
        gate = 1.0 / (1.0 + jnp.exp(-z))
        gated = gbuf[:, cols]
        scaled = dout_ref[:, cols] * scale
        ggrad_ref[:, cols] += fold_rows(scaled * gated)
        d_gated = scaled * gain_ref[0:1, cols] - gated * pull
        dy, rest = two_parts(d_gated * (z * gate))
        dy_ref[:, cols] = dy
        rest_ref[:, cols] = rest
        dz_ref[:, cols] = (d_gated * y_ref[:, cols] * (gate * (1.0 + z * (1.0 - gate)))).astype(BF16)
        xbuf[:, cols] = (dy.astype(F32) * spread(aux, FROM_START, j, low)).astype(BF16)
    zloc_ref[0] = grad_state[...].astype(BF16)
    dsuf_ref[0] = suffix[...]
    reads = reads_ref[...].astype(F32).T.astype(BF16)
    through = drow_ref[0, 0:1, :]
    grad_state[...] = grad_state[...] * through + dot_nn(reads, xbuf[...])
    suffix[...] = suffix[...] * through
    gmsg_ref[...] = grad_state[...].astype(BF16)


def within_back_kernel(
    act_ref, aux_ref, lt_ref, segx_ref, segr_ref, dy_ref, rest_ref, sprev_ref, drow_ref, sin_ref, zloc_ref,
    dxs_ref, dbc_ref, wbuf, wrest, ibuf, irest, ebuf,
):
    c = pl.program_id(0)
    seg = segx_ref[pl.ds(pl.multiple_of(c * Q + 8, 8), Q), :]
    rows = lax.broadcasted_iota(jnp.int32, (Q, Q), 0)
    lane = lax.broadcasted_iota(jnp.int32, (Q, Q), 1)
    bias = jnp.where((rows <= lane) & (seg == segr_ref[0, 0:1, :]), 0.0, FAR)
    keys, reads = act_ref[:, KEYS], act_ref[:, READS]
    scores = dot_nt(
        jnp.concatenate([keys, keys], axis=1), jnp.concatenate([reads, act_ref[:, READS_REST]], axis=1)
    ) + dot_nt(act_ref[:, KEYS_REST], reads)
    aux = aux_ref[...]
    low = low_lanes()
    has_prev = (c > 0).astype(F32)
    d_scores = jnp.zeros((Q, Q), F32)
    for j in range(PAIRS):
        cols = lanes_of(j)
        fades = [
            jnp.exp(lt_ref[0, h : h + 1, :] - column(aux, LOGS + h) + bias)
            for h in (2 * j, 2 * j + 1)
        ]
        weights = jnp.concatenate([(fade * scores).astype(BF16) for fade in fades], axis=1)
        dy = dy_ref[:, cols]
        dy_wide = dy.astype(F32)
        dy_rest = rest_ref[:, cols]
        stack = jnp.concatenate(
            [jnp.where(low, dy_wide, 0.0), jnp.where(low, 0.0, dy_wide)], axis=0
        ).astype(BF16)
        scaled = (spread(aux, STEP, j, low) * act_ref[:, cols].astype(F32)).astype(BF16).astype(F32)
        both = jnp.concatenate(
            [jnp.where(low, scaled, 0.0), jnp.where(low, 0.0, scaled)], axis=0
        ).astype(BF16)
        d_weights = dot_nt(
            jnp.concatenate([both, both], axis=1), jnp.concatenate([dy, dy_rest], axis=1)
        )
        d_scores += d_weights[:Q] * fades[0] + d_weights[Q:] * fades[1]
        to_end = spread(aux, TO_END, j, low)
        dxs_ref[:, cols] = dot_nn(weights, stack) + to_end * dot_nn(keys, zloc_ref[0, :, cols])
        wbuf[:, cols], wrest[:, cols] = two_parts(
            (dy_wide + dy_rest.astype(F32)) * spread(aux, FROM_START, j, low)
        )
        ebuf[:, cols] = (to_end * scaled).astype(BF16)
        ibuf[:, cols], irest[:, cols] = two_parts(
            drow_ref[0, 1:2, cols] * sin_ref[:, cols] + has_prev * sprev_ref[0, :, cols]
        )
    dbc_ref[:, 0:N] = dot_nn(d_scores.astype(BF16), reads) + dot_nt(ebuf[...], zloc_ref[0])
    high, rest = two_parts(d_scores.T)
    dbc_ref[:, N:] = (
        dot_nn(high, keys)
        + dot_nn(rest, keys)
        + dot_nt(wbuf[...], ibuf[...])
        + dot_nt(wrest[...], ibuf[...])
        + dot_nt(wbuf[...], irest[...])
    )


def last_kernel(
    act_ref, aux_ref, slope_ref, u_ref, s_ref, rim_ref, segx_ref, taps_ref, heads_ref, skip_ref,
    oh_ref, dy_ref, y_ref, dxs_ref, dbc_ref, sout_ref, drow_ref, sin_ref, zloc_ref, dsuf_ref, zdev_ref,
    du_ref, ds_ref, tail_ref, rimout_ref, tgrad_ref, hgrad_ref,
    dbuf, qhigh, qrest, vhigh, vrest, ebuf, sums, skips,
):
    i = pl.program_id(0)
    count = pl.num_programs(0)
    c = count - 1 - i

    @pl.when(i == 0)
    def _():
        dbuf[Q : Q + 8, :] = jnp.zeros((8, CH), F32)
        tgrad_ref[...] = jnp.zeros_like(tgrad_ref)
        hgrad_ref[...] = jnp.zeros_like(hgrad_ref)
        skips[...] = jnp.zeros_like(skips)

    @pl.when(i > 0)
    def _():
        dbuf[Q : Q + 8, :] = dbuf[0:8, :]

    aux = aux_ref[...]
    low = low_lanes()
    keys = act_ref[:, KEYS]
    for j in range(PAIRS):
        cols = lanes_of(j)
        dy = dy_ref[:, cols].astype(F32)
        values = act_ref[:, cols].astype(F32)
        step = spread(aux, STEP, j, low)
        scaled = (step * values).astype(BF16).astype(F32)
        reach = spread(aux, TO_END, j, low) * dsuf_ref[0, 0:1, cols]
        dxs = dxs_ref[:, cols] + reach * dot_nn(keys, zdev_ref[:, cols])
        ebuf[:, cols] = (reach * scaled).astype(BF16)
        skip = skip_ref[0:1, cols]
        dbuf[0:Q, cols] = (step * dxs + skip * dy) * slope_ref[:, cols].astype(F32)
        qhigh[:, cols], qrest[:, cols] = two_parts(dy * (y_ref[:, cols] - skip * values) - scaled * dxs)
        vhigh[:, cols], vrest[:, cols] = two_parts(values * dxs)
        skips[:, cols] += fold_rows(values * dy)
        arrived = zloc_ref[0, :, cols].astype(F32) + dsuf_ref[0, 0:1, cols] * zdev_ref[:, cols].astype(F32)
        leaving = sout_ref[0, :, cols] + drow_ref[0, 2:3, cols] * sin_ref[:, cols]
        sums[:, cols] = fold_rows(arrived * leaving)
    d_keys = dbc_ref[:, 0:N] + dot_nt(ebuf[...], zdev_ref[...])
    dbuf[0:Q, DI : DI + N] = d_keys * slope_ref[:, DI : DI + N].astype(F32)
    dbuf[0:Q, DI + N :] = dbc_ref[:, N:] * slope_ref[:, DI + N :].astype(F32)

    hot = oh_ref[...]

    def by_head(x):
        high, rest = two_parts(x)
        return dot_nn(high, hot) + dot_nn(rest, hot)

    d_logs = dot_nn(qhigh[...], hot) + dot_nn(qrest[...], hot)
    d_last = jnp.sum(by_head(sums[...]), axis=0, keepdims=True)
    rows = lax.broadcasted_iota(jnp.int32, (Q, Q), 0)
    lane = lax.broadcasted_iota(jnp.int32, (Q, Q), 1)
    d_decay = dot_full((rows <= lane).astype(F32), d_logs) + d_last
    raw = s_ref[...].astype(F32) + heads_ref[0:1, :]
    step = jnp.maximum(raw, 0.0) + jnp.log1p(jnp.exp(-jnp.abs(raw)))
    d_step = dot_nn(vhigh[...], hot) + dot_nn(vrest[...], hot) - heads_ref[1:2, :] * d_decay
    d_raw = d_step / (1.0 + jnp.exp(-raw))
    ds_ref[...] = d_raw.astype(BF16)
    hgrad_ref[0:8, :] += fold_rows(d_raw)
    hgrad_ref[8:16, :] += fold_rows(-(step * d_decay))

    @pl.when(i == count - 1)
    def _():
        hgrad_ref[16:24, :] = by_head(skips[...])

    seg_rows = segx_ref[pl.ds(pl.multiple_of(c * Q + 8, 8), Q + 8), :]
    seg = seg_rows[:Q]
    masks = [(seg_rows[m : m + Q] == seg).astype(F32) for m in range(1, CONV)]
    for j in range(BLOCKS):
        cols = lanes_of(j)
        d_filtered = dbuf[0:Q, cols]
        u = u_ref[:, cols].astype(F32)
        du = taps_ref[3:4, cols] * d_filtered
        tgrad_ref[24:32, cols] += fold_rows(u * d_filtered)
        tgrad_ref[32:40, cols] += fold_rows(d_filtered)
        for m in range(1, CONV):
            later = dbuf[m : m + Q, cols] * masks[m - 1]
            du += taps_ref[3 - m : 4 - m, cols] * later
            tgrad_ref[8 * (3 - m) : 8 * (4 - m), cols] += fold_rows(u * later)
        du_ref[:, cols] = du.astype(BF16)

        @pl.when(i == 0)
        def _():
            tail_ref[:, cols] = du[Q - 8 :]

    @pl.when(i == count - 1)
    def _():
        near = segx_ref[0:16, :]
        rim_masks = [(near[m : m + 8] == near[0:8]).astype(F32) for m in range(1, CONV)]
        for j in range(BLOCKS):
            cols = lanes_of(j)
            edge = jnp.concatenate([jnp.zeros((8, LANES), F32), dbuf[0:8, cols]], axis=0)
            u = rim_ref[:, cols].astype(F32)
            out = jnp.zeros((8, LANES), F32)
            for m in range(1, CONV):
                later = edge[m : m + 8] * rim_masks[m - 1]
                out += taps_ref[3 - m : 4 - m, cols] * later
                tgrad_ref[8 * (3 - m) : 8 * (4 - m), cols] += u * later
            rimout_ref[:, cols] = out.astype(BF16)


def whole(shape):
    return pl.BlockSpec(shape, lambda i: (0,) * len(shape))


def by_rows(shape, count=None):
    if count is None:
        return pl.BlockSpec(shape, lambda i: (i,) + (0,) * (len(shape) - 1))
    return pl.BlockSpec(shape, lambda i: (count - 1 - i,) + (0,) * (len(shape) - 1))


def struct(shape, dtype):
    return jax.ShapeDtypeStruct(shape, dtype)


def call(kernel, grid, in_specs, out_specs, out_shape, scratch, flops, moved, name):
    return pl.pallas_call(
        kernel,
        grid=(grid,),
        in_specs=in_specs,
        out_specs=out_specs,
        out_shape=out_shape,
        scratch_shapes=scratch,
        compiler_params=pltpu.CompilerParams(
            dimension_semantics=("arbitrary",), vmem_limit_bytes=VMEM_LIMIT
        ),
        cost_estimate=pl.CostEstimate(flops=flops, bytes_accessed=moved, transcendentals=0),
        name=name,
    )


MIB = 1 << 20


def ssd_front(u, s4, rim, segx, taps, heads, oht):
    T = u.shape[0]
    nc = T // Q
    return call(
        front_kernel, nc,
        [by_rows((Q, CH)), by_rows((Q, LANES)), whole((8, CH)), whole(segx.shape), whole(taps.shape),
         whole(heads.shape), whole(oht.shape)],
        [by_rows((Q, ACT)), by_rows((Q, CH)), by_rows((Q, LANES)), by_rows((1, H, Q)),
         by_rows((1, 8, DI)), by_rows((1, N, DI)), whole((N + 8, DI))],
        [struct((T, ACT), BF16), struct((T, CH), BF16), struct((T, LANES), F32), struct((nc, H, Q), F32),
         struct((nc, 8, DI), F32), struct((nc, N, DI), F32), struct((N + 8, DI), F32)],
        [pltpu.VMEM((Q + 8, CH), F32), pltpu.VMEM((N, DI), F32), pltpu.VMEM((8, LANES), F32),
         pltpu.VMEM((Q, DI), BF16)],
        2_000_000_000, 12 * MIB, "ssd_front",
    )(u, s4, rim, segx, taps, heads, oht)


def previous(shape):
    return pl.BlockSpec(shape, lambda i: (jnp.maximum(i - 1, 0), 0, 0))


def ssd_within(act, aux, lt, segx, segr, sout, skip):
    T = act.shape[0]
    nc = T // Q
    return call(
        within_kernel, nc,
        [by_rows((Q, ACT)), by_rows((Q, LANES)), by_rows((1, H, Q)), whole(segx.shape),
         by_rows((1, 8, LANES)), previous((1, N, DI)), whole(skip.shape)],
        by_rows((Q, DI)), struct((T, DI), F32), [],
        4_000_000_000, 10 * MIB, "ssd_within",
    )(act, aux, lt, segx, segr, sout, skip)


def ssd_gate(yloc, aux, drow, s_in, act, z, gain):
    T = yloc.shape[0]
    nc = T // Q
    reads = pl.BlockSpec((Q, N), lambda i: (i, READS.start // N))
    rest = pl.BlockSpec((Q, N), lambda i: (i, READS_REST.start // N))
    return call(
        gate_kernel, nc,
        [by_rows((Q, DI)), by_rows((Q, LANES)), by_rows((1, 8, DI)), whole((N, DI)), reads,
         rest, by_rows((Q, DI)), whole(gain.shape)],
        [by_rows((Q, DI)), by_rows((Q, DI))],
        [struct((T, DI), F32), struct((T, DI), BF16)],
        [pltpu.VMEM((Q, DI), F32)],
        2_000_000_000, 14 * MIB, "ssd_gate",
    )(yloc, aux, drow, s_in, act, act, z, gain)


def gate_back(dout, y, z, gain, act, aux, drow):
    T = y.shape[0]
    nc = T // Q
    reads = pl.BlockSpec((Q, N), lambda i: (nc - 1 - i, READS.start // N))
    return call(
        gate_back_kernel, nc,
        [by_rows((Q, DI), nc), by_rows((Q, DI), nc), by_rows((Q, DI), nc), whole(gain.shape), reads,
         by_rows((Q, LANES), nc), by_rows((1, 8, DI), nc)],
        [by_rows((Q, DI), nc)] * 3 + [whole((8, DI)), by_rows((1, N, DI), nc),
         whole((N, DI)), by_rows((1, 8, DI), nc)],
        [struct((T, DI), BF16)] * 3 + [struct((8, DI), F32), struct((nc, N, DI), BF16),
         struct((N, DI), BF16), struct((nc, 8, DI), F32)],
        [pltpu.VMEM((Q, DI), F32), pltpu.VMEM((N, DI), F32), pltpu.VMEM((8, DI), F32),
         pltpu.VMEM((Q, DI), BF16)],
        3_000_000_000, 18 * MIB, "gate_back",
    )(dout, y, z, gain, act, aux, drow)


def within_back(act, aux, lt, segx, segr, dy, rest, sout, drow, s_in, zloc):
    T = act.shape[0]
    nc = T // Q
    return call(
        within_back_kernel, nc,
        [by_rows((Q, ACT)), by_rows((Q, LANES)), by_rows((1, H, Q)), whole(segx.shape),
         by_rows((1, 8, LANES)), by_rows((Q, DI)), by_rows((Q, DI)), previous((1, N, DI)), by_rows((1, 8, DI)),
         whole((N, DI)), by_rows((1, N, DI))],
        [by_rows((Q, DI)), by_rows((Q, 2 * N))],
        [struct((T, DI), F32), struct((T, 2 * N), F32)],
        [pltpu.VMEM((Q, DI), BF16)] * 5,
        8_000_000_000, 16 * MIB, "within_back",
    )(act, aux, lt, segx, segr, dy, rest, sout, drow, s_in, zloc)


def ssd_last(act, aux, slope, u, s4, rim, segx, taps, heads, skip, oh, dy, y, dxs, dbc, sout, drow, s_in,
             zloc, dsuf, zdev):
    T = act.shape[0]
    nc = T // Q
    return call(
        last_kernel, nc,
        [by_rows((Q, ACT), nc), by_rows((Q, LANES), nc), by_rows((Q, CH), nc), by_rows((Q, CH), nc),
         by_rows((Q, LANES), nc), whole((8, CH)), whole(segx.shape), whole(taps.shape),
         whole(heads.shape), whole(skip.shape), whole(oh.shape), by_rows((Q, DI), nc),
         by_rows((Q, DI), nc), by_rows((Q, DI), nc), by_rows((Q, 2 * N), nc), by_rows((1, N, DI), nc),
         by_rows((1, 8, DI), nc), whole((N, DI)), by_rows((1, N, DI), nc), by_rows((1, 8, DI), nc),
         whole((N, DI))],
        [by_rows((Q, CH), nc), by_rows((Q, LANES), nc), whole((8, CH)), whole((8, CH)), whole((40, CH)),
         whole((24, LANES))],
        [struct((T, CH), BF16), struct((T, LANES), BF16), struct((8, CH), F32), struct((8, CH), BF16),
         struct((40, CH), F32), struct((24, LANES), F32)],
        [pltpu.VMEM((Q + 8, CH), F32), pltpu.VMEM((Q, DI), BF16), pltpu.VMEM((Q, DI), BF16),
         pltpu.VMEM((Q, DI), BF16), pltpu.VMEM((Q, DI), BF16), pltpu.VMEM((Q, DI), BF16),
         pltpu.VMEM((8, DI), F32), pltpu.VMEM((8, DI), F32)],
        6_000_000_000, 24 * MIB, "ssd_last",
    )(act, aux, slope, u, s4, rim, segx, taps, heads, skip, oh, dy, y, dxs, dbc, sout, drow, s_in,
      zloc, dsuf, zdev)


def swap(value, axis):
    return lax.ppermute(value, axis, [(0, 1), (1, 0)])


def flip(value, axis, bit):
    size = lax.axis_size(axis)
    return lax.ppermute(value, axis, [(i, i ^ bit) for i in range(size)])


def ordered(index, mine, other, axis):
    return jnp.where(
        index == 0, jnp.concatenate([mine, other], axis), jnp.concatenate([other, mine], axis)
    )


CTX = ("zz", "core")


def routes():
    n = lax.axis_size("zz") * lax.axis_size("core")
    half = n // 2
    first = [(i, i // 2 + (half if i % 2 else 0)) for i in range(n)]
    second = [(i, i // 2 + (0 if i % 2 else half)) for i in range(n)]
    return half, first, second


def gather_tokens(x):
    half, first, second = routes()
    me = lax.axis_index(CTX)
    even = me % 2 == 0
    a = lax.ppermute(jnp.where(even, x[0], x[1]), CTX, first)
    b = lax.ppermute(jnp.where(even, x[1], x[0]), CTX, second)
    early = me < half
    return jnp.concatenate([jnp.where(early, a, b), jnp.where(early, b, a)], axis=0)


def scatter_tokens(x):
    half, first, second = routes()
    me = lax.axis_index(CTX)
    early = me < half
    rows = x.shape[0] // 2
    x0, x1 = x[:rows], x[rows:]
    a = lax.ppermute(jnp.where(early, x0, x1), CTX, [(d, s) for s, d in first])
    b = lax.ppermute(jnp.where(early, x1, x0), CTX, [(d, s) for s, d in second])
    even = me % 2 == 0
    return jnp.stack([jnp.where(even, a, b), jnp.where(even, b, a)])


def next_piece(value, backward=False):
    n = lax.axis_size("zz") * lax.axis_size("core")
    half = n // 2
    pairs = [(i, i + 1) for i in range(n - 1) if i + 1 != half]
    if backward:
        pairs = [(d, s) for s, d in pairs]
    return lax.ppermute(value, CTX, pairs)


def after(value, earlier):
    value, _ = lax.optimization_barrier((value, earlier))
    return value


def fetch_peer(own, core, earlier=None):
    rows = own.shape[0] // 2
    part = lax.dynamic_slice_in_dim(own, core * rows, rows, 0)
    if earlier is not None:
        part = after(part, earlier)
    got = swap(part, "fsdp")
    return ordered(core, got, swap(got, "core"), 0), got


def carry_forward(core, msg):
    other = swap(msg, "core")

    s_mine, d_mine = msg[:N], msg[N : N + 1]
    s_other, d_other = other[:N], other[N : N + 1]
    lead = core == 0
    s_first, d_first = jnp.where(lead, s_mine, s_other), jnp.where(lead, d_mine, d_other)
    s_second, d_second = jnp.where(lead, s_other, s_mine), jnp.where(lead, d_other, d_mine)
    total = d_second * s_first + s_second
    through = d_first * d_second
    chips = lax.axis_size("zz") // 2
    total = halves(total, core, 0)[0]
    prefix = jnp.zeros_like(total)
    for hop in range(1, chips):
        sent = total if hop == 1 else through * prefix + total
        pairs = [(hop - 1, hop), (chips + hop - 1, chips + hop)]
        prefix = prefix + lax.ppermute(sent, "zz", pairs)
    prefix = ordered(core, prefix, swap(prefix, "core"), 0)
    incoming = jnp.where(lead, prefix, d_first * prefix + s_first)
    return incoming, (d_first, d_second)


def carry_backward(core, msg, decays):
    other = swap(msg, "core")
    d_first, d_second = decays
    lead = core == 0
    g_first = jnp.where(lead, msg, other).astype(F32)
    g_second = jnp.where(lead, other, msg).astype(F32)
    total = g_first + d_first * g_second
    through = d_first * d_second
    chips = lax.axis_size("zz") // 2
    suffix = jnp.zeros_like(total)
    for hop in range(1, chips):
        sent = total if hop == 1 else through * suffix + total
        pairs = [(chips - hop, chips - hop - 1), (2 * chips - hop, 2 * chips - hop - 1)]
        suffix = suffix + lax.ppermute(sent.astype(BF16), "zz", pairs).astype(F32)
    arriving = jnp.where(lead, g_second + d_second * suffix, suffix)
    return arriving.astype(BF16)


def rms_parts(values):
    return lax.rsqrt(jnp.mean(values * values, axis=-1, keepdims=True) + EPSILON)


def halves(array, index, axis):
    size = array.shape[axis] // 2
    mine = lax.dynamic_slice_in_dim(array, index * size, size, axis)
    other = lax.dynamic_slice_in_dim(array, (1 - index) * size, size, axis)
    return mine, other


def levels():
    out = [("rep", 1)]
    bit = 1
    while bit < lax.axis_size("zz"):
        out.append(("zz", bit))
        bit *= 2
    return out


def sum_shards(partial, fsdp):
    mine, other = halves(partial, fsdp, 0)
    total = mine + swap(other.astype(BF16), "fsdp").astype(F32)
    steps = levels()
    for axis, bit in steps:
        which = (lax.axis_index(axis) // bit) % 2
        mine, other = halves(total, which, 0)
        total = mine + flip(other.astype(BF16), axis, bit).astype(F32)
    total = total.astype(BF16)
    for axis, bit in reversed(steps):
        which = (lax.axis_index(axis) // bit) % 2
        total = ordered(which, total, flip(total, axis, bit), 0)
    return total


def sum_small(packed):
    packed = packed + swap(packed, "core")
    packed = packed + swap(packed, "fsdp")
    for axis, bit in levels():
        packed = packed + flip(packed, axis, bit)
    return packed


def local(
    tokens,
    segments,
    expand_weight,
    reduce_weight,
    filter_taps,
    filter_offset,
    step_bias,
    decay_rate,
    skip_gain,
    norm_gain,
    gate_gain,
    cotangent,
):
    rows = tokens.shape[1]
    T = 2 * rows
    fsdp = lax.axis_index("fsdp")
    core = lax.axis_index("core")
    me = lax.axis_index(CTX)
    n = lax.axis_size("zz") * lax.axis_size("core")
    half = n // 2

    def pad(x, width):
        return jnp.pad(x, ((0, 0), (0, 0), (0, width - x.shape[-1])))

    heads_packed = jnp.concatenate([step_bias, decay_rate, skip_gain], axis=-1)
    own = jnp.concatenate(
        [filter_taps, filter_offset[:, None], pad(norm_gain[:, None], CH // 2),
         pad(gate_gain[:, None], CH // 2), pad(heads_packed[:, None], CH // 2)], axis=1
    )
    other = swap(own, "fsdp")
    lead = fsdp == 0
    low_half = jnp.where(lead, own, other).astype(F32)
    high_half = jnp.where(lead, other, own).astype(F32)

    def joined(row, start, size):
        return jnp.concatenate(
            [low_half[:, row, start : start + size], high_half[:, row, start : start + size]], axis=-1
        )

    taps_all = jnp.concatenate([low_half[:, :5], high_half[:, :5]], axis=-1)
    taps_all = jnp.pad(taps_all, ((0, 0), (0, 3), (0, 0)))
    norm_all, gate_all = joined(5, 0, D // 2), joined(6, 0, DI // 2)
    bias_all, rate_all, skip_all = joined(7, 0, H // 2), joined(7, H // 2, H // 2), joined(7, H, H // 2)
    heads_all = jnp.pad(
        jnp.stack([jnp.tile(bias_all, (1, 4)), jnp.tile(rate_all, (1, 4))], axis=1), ((0, 0), (0, 6), (0, 0))
    )
    skip_rows = jnp.repeat(skip_all, P_SIZE, axis=-1)

    hot = (
        lax.broadcasted_iota(jnp.int32, (DI, LANES), 0) // P_SIZE
        == lax.broadcasted_iota(jnp.int32, (DI, LANES), 1)
    ).astype(BF16)
    hot_t = (
        lax.broadcasted_iota(jnp.int32, (LANES, DI), 1) // P_SIZE
        == lax.broadcasted_iota(jnp.int32, (LANES, DI), 0)
    ).astype(BF16)

    seq = (me >= half).astype(jnp.int32)
    padded = jnp.pad(segments, ((0, 0), (8, 8)), constant_values=-1)
    seg_line = lax.dynamic_slice(padded, (seq, (me % half) * T), (1, T + 16))[0].astype(F32)
    segx = jnp.broadcast_to(seg_line[:, None], (T + 16, LANES))
    segr = jnp.broadcast_to(seg_line[8 : 8 + T].reshape(T // Q, 1, Q), (T // Q, 8, Q))

    weights = []
    earlier = None
    for layer in range(LAYERS):
        expand_peer, earlier = fetch_peer(expand_weight[layer], core, earlier)
        reduce_peer, earlier = fetch_peer(reduce_weight[layer], core, earlier)
        weights.append(
            (ordered(fsdp, expand_weight[layer], expand_peer, 0),
             ordered(fsdp, reduce_weight[layer], reduce_peer, 0))
        )

    resid = gather_tokens(tokens).astype(F32)
    saved = []
    for layer in range(LAYERS):
        expand, reduce = weights[layer]
        normed = (resid * rms_parts(resid) * norm_all[layer]).astype(BF16)
        mixed = dot_nn(normed, expand).astype(BF16)
        z, u, s = mixed[:, :DI], mixed[:, DI : DI + CH], mixed[:, DI + CH :]
        s4 = jnp.tile(s, (1, LANES // H))
        rim = next_piece(u[T - 8 :])
        taps, heads = taps_all[layer], heads_all[layer]
        skip = skip_rows[layer][None]
        act, slope, aux, lt, drow, sout, msg = ssd_front(u, s4, rim, segx, taps, heads, hot_t)
        s_in, decays = carry_forward(core, msg)
        yloc = ssd_within(act, aux, lt, segx, segr, sout, skip)
        gain = gate_all[layer][None]
        y, out_in = ssd_gate(yloc, aux, drow, s_in, act, z, gain)
        normed_both = jnp.concatenate([normed, swap(normed, "core")], axis=0)
        out_both = jnp.concatenate([out_in, swap(out_in, "core")], axis=0)
        saved.append((resid, normed_both, z, u, s4, rim, act, slope, aux, lt, drow, sout, s_in, decays, y, out_both))
        resid = resid + dot_nn(out_in, reduce)
    layer_out = scatter_tokens(resid.astype(BF16))

    grad = gather_tokens(cotangent).astype(F32)
    expand_z, expand_u, reduce_g, small = [None] * 2, [None] * 2, [None] * 2, [None] * 2
    for layer in reversed(range(LAYERS)):
        expand, reduce = weights[layer]
        (resid_in, normed_both, z, u, s4, rim, act, slope, aux, lt, drow, sout, s_in, decays, y, out_both) = saved[layer]
        taps, heads = taps_all[layer], heads_all[layer]
        skip = skip_rows[layer][None]
        gain = gate_all[layer][None]
        grad_low = grad.astype(BF16)
        dout = dot_nt(grad_low, reduce)
        low_mine, low_other = halves(grad_low, core, 1)
        low_both = jnp.concatenate([low_mine, swap(low_other, "core")], axis=0)
        reduce_g[layer] = sum_shards(dot_tn(out_both, low_both), fsdp)
        dy, dy_rest, dz, ggrad, zloc, gmsg, dsuf = gate_back(dout, y, z, gain, act, aux, drow)
        zdev = carry_backward(core, gmsg, decays)
        dz_mine, dz_other = halves(dz, core, 1)
        dz_both = jnp.concatenate([dz_mine, swap(dz_other, "core")], axis=0)
        expand_z[layer] = sum_shards(dot_tn(normed_both, dz_both), fsdp)
        dxs, dbc = within_back(act, aux, lt, segx, segr, dy, dy_rest, sout, drow, s_in, zloc)
        du, ds, tail, rimout, tgrad, hgrad = ssd_last(
            act, aux, slope, u, s4, rim, segx, taps, heads, skip, hot, dy, y, dxs, dbc, sout, drow, s_in,
            zloc, dsuf, zdev
        )
        tail = (tail + next_piece(rimout, True).astype(F32)).astype(BF16)
        du = lax.dynamic_update_slice(du, tail, (T - 8, 0))
        ds = ds[:, :H]
        du_mine, du_other = halves(du, core, 1)
        us_both = jnp.concatenate(
            [jnp.concatenate([du_mine, ds], axis=1),
             swap(jnp.concatenate([du_other, ds], axis=1), "core")], axis=0
        )
        expand_u[layer] = sum_shards(dot_tn(normed_both, us_both), fsdp)
        d_mixed = jnp.concatenate([dz, du, ds], axis=1)
        d_normed = dot_nt(d_mixed, expand)
        scale = rms_parts(resid_in)
        unit = resid_in * scale
        pulled = d_normed * norm_all[layer]
        grad = grad + scale * (pulled - unit * jnp.mean(pulled * unit, axis=-1, keepdims=True))
        norm_grad = jnp.sum(d_normed * unit, axis=0)
        tgrad = jnp.sum(tgrad.reshape(5, 8, CH), axis=1).reshape(-1)
        hgrad = jnp.sum(hgrad.reshape(3, 8, LANES), axis=1)[:, :H].reshape(-1)
        small[layer] = jnp.concatenate([tgrad, jnp.sum(ggrad, axis=0), norm_grad, hgrad])

    token_grads = scatter_tokens(grad.astype(BF16))
    size = small[0].shape[0]
    padded_size = -(-size // 1024) * 1024
    packed = jnp.pad(jnp.stack(small), ((0, 0), (0, padded_size - size)))
    packed = sum_small(packed.reshape(-1, LANES)).reshape(LAYERS, padded_size)

    def own_half(x):
        return halves(x, fsdp, x.ndim - 1)[0]

    tap_grads = own_half(packed[:, : 4 * CH].reshape(LAYERS, 4, CH))
    offset_grads = own_half(packed[:, 4 * CH : 5 * CH])
    at = 5 * CH
    gating_grads = own_half(packed[:, at : at + DI])
    at += DI
    norm_grads = own_half(packed[:, at : at + D])
    at += D
    step_grads = own_half(packed[:, at : at + H])
    decay_grads = own_half(packed[:, at + H : at + 2 * H])
    skip_grads = own_half(packed[:, at + 2 * H : at + 3 * H])

    expand_grads, reduce_grads = [], []
    for layer in range(LAYERS):
        zg = ordered(core, expand_z[layer], swap(expand_z[layer], "core"), 1)
        ug = expand_u[layer]
        sg = ug[:, CH // 2 :]
        ug = ug[:, : CH // 2]
        ug = ordered(core, ug, swap(ug, "core"), 1)
        expand_grads.append(jnp.concatenate([zg, ug, sg], axis=1).astype(F32))
        reduce_grads.append(ordered(core, reduce_g[layer], swap(reduce_g[layer], "core"), 1).astype(F32))
    return (
        layer_out,
        token_grads,
        jnp.stack(expand_grads),
        jnp.stack(reduce_grads),
        tap_grads,
        offset_grads,
        step_grads,
        decay_grads,
        skip_grads,
        norm_grads,
        gating_grads,
    )


def solution(mesh):
    rep, fsdp, ctx = (mesh.shape[name] for name in ("rep", "fsdp", "ctx"))
    inner = Mesh(mesh.devices.reshape(rep, fsdp, ctx // 2, 2), ("rep", "fsdp", "zz", "core"))
    tokens = P(("rep", "fsdp"), ("zz", "core"), None)
    first, last = P(None, "fsdp"), P(None, None, "fsdp")
    return jax.shard_map(
        local,
        mesh=inner,
        in_specs=(
            tokens, P(("rep", "fsdp"), None), P(None, "fsdp", None), P(None, "fsdp", None), last,
            first, first, first, first, first, first, tokens,
        ),
        out_specs=(
            tokens, tokens, P(None, "fsdp", None), P(None, "fsdp", None), last,
            first, first, first, first, first, first,
        ),
        check_vma=False,
    )
```

time: 2470 us -> 905 us (0.37)
  waiting for transfers between devices: 922 us -> 318 us
  local copies, waits for them, and re-layouts: 483 us -> 91.8 us
  matrix products: 454 us -> 105 us
  other arithmetic: 379 us -> 119 us
  Pallas kernels: 0 us -> 170 us
  blocking collectives: 157 us -> 0 us
  starting transfers between devices: 7.29 us -> 87.5 us
  loops' own time: 35.6 us -> 0 us
    all_gather x8 -> x0, waiting for transfers between devices: 443 us -> none  [the longest x4 249 us: carried_in(): pieces = jax.tree.map(lambda part: lax.all_gather(part, axis), value)]
    psum x1 -> x0, waiting for transfers between devices: 390 us -> none  [total_grads(): lax.psum((shards[0], shards[1], shards[2], shards[3], shards[4], shards[5...]
    dot_general x68 -> x14, matrix products: 454 us -> 105 us  [the longest x4 43.2 us: dot_nt(): lax.dot_general(a, b, (((1,), (1,)), ((), ())), preferred_element_type=F32)]
    ppermute x4 -> x94, waiting for transfers between devices: 0.01 us -> 318 us  [the longest x39 148 us: flip(): return lax.ppermute(value, axis, [(i, i ^ bit) for i in range(size)])]
    pallas_call x0 -> x12, Pallas kernels: none -> 170 us  [the longest x2 46.8 us: ssd_last(): call(last_kernel, nc, [by_rows((Q, ACT), nc), by_rows((Q, LANES), nc), by...]
    slice x82 -> x24, local copies, waits for them, and re-layouts: 108 us -> 13 us  [the longest x8 10.4 us: local(): z, u, s = (mixed[:, :DI], mixed[:, DI:DI + CH], mixed[:, DI + CH:])]
    while x552 -> x0, local copies, waits for them, and re-layouts: 89.8 us -> none
    reduce_scatter x4 -> x0, waiting for transfers between devices: 87.6 us -> none  [the longest x2 87.6 us: total_grads(): lax.psum_scatter(expand_grad.astype(jnp.bfloat16), 'fsdp', scatter_dimens...]
  transfers between devices with their start and end apart: 19 -> 94, of which waited for: 8 -> 37; matrix products, arithmetic and copies ran while one was open for 30% -> 28% of each run, Pallas kernels for 0% -> 16%
where the time goes in v1:
time: 905 us; the launch traced here: 894 us
  waiting for transfers between devices  318 us (35%)
  Pallas kernels  170 us (19%)
  other arithmetic  119 us (13%)
  matrix products  105 us (12%)
  local copies, waits for them, and re-layouts  91.8 us (10%)
  starting transfers between devices  87.5 us (10%)
    ppermute x39, waiting for transfers between devices, flip(): return lax.ppermute(value, axis, [(i, i ^ bit) for i in range(size)])  148 us
    ppermute x39, waiting for transfers between devices, swap(): return lax.ppermute(value, axis, [(0, 1), (1, 0)])  139 us
    pallas_call x2, Pallas kernels, ssd_last(): call(last_kernel, nc, [by_rows((Q, ACT), nc), by_rows((Q, LANES), nc), by...  46.8 us
    dot_general x4, matrix products, dot_nt(): lax.dot_general(a, b, (((1,), (1,)), ((), ())), preferred_element_type=F32)  43.2 us
    pallas_call x2, Pallas kernels, within_back(): call(within_back_kernel, nc, [by_rows((Q, ACT)), by_rows((Q, LANES)), by_...  35.8 us
    dot_general x4, matrix products, dot_nn(): lax.dot_general(a, b, (((1,), (0,)), ((), ())), preferred_element_type=F32)  34.7 us
    select_n x24, other arithmetic, ordered(): jnp.where(index == 0, jnp.concatenate([mine, other], axis), jnp.concatena...  29.8 us
    ppermute x39, starting transfers between devices, flip(): return lax.ppermute(value, axis, [(i, i ^ bit) for i in range(size)])  27.8 us
  transfers between devices with their start and end apart: 94, of which 37 were waited for; matrix products, arithmetic and copies ran while one was open for 28% of the time, Pallas kernels for 16%

profile of v1, /device:TPU:0, one launch (start us, length us, event | category | flops | bytes accessed | tf_op | source)
XLA Modules:
  0.0 894.4 jit_solution(17956068888433387840)
XLA Ops:
  14.4 8.8 slice_bitcast_fusion.15
  26.8 5.5 slice_bitcast_fusion.13
  33.9 43.1 %collective-permute-done.3 = bf16[256,4384]{0,1:T(8,128)(2,1)} collective-permute-done((bf16[256,4384]{0,1:T(8,128)(2,1)}, bf16[256,4384]{0,1:T(8,128)(2,1)}, u32[]{:S(2)}, u32[]{:S(2)}) %collective-permute-start.3) | collective-permute-done | bytes 2244640 | tf_op jit(solution)/shard_map/ppermute | solution.py:556
  86.5 12.3 %convolution_convert_fusion.1 = bf16[512,4384]{1,0:T(8,128)(2,1)S(1)} fusion(bf16[512,1024]{1,0:T(8,128)(2,1)} %fusion.38, bf16[512,4384]{0,1:T(8,128)(2,1)} %maximum_select_fusion.2, bf16[512,4384]{0,1:T(8,128)(2,1)} %get-tuple-element.122, pred[]{:T(512)S(6)} %eq.108), kind=kOutput, calls=%fused_computation.4 | convolution fusion | flops 4639604736 | bytes 14516225 | tf_op jit(solution)/shard_map/dot_general | solution.py:32
  105.6 13.0 %ssd_front.2 = (bf16[512,2560]{1,0:T(8,128)(2,1)}, bf16[512,2304]{1,0:T(8,128)(2,1)}, f32[512,128]{1,0:T(8,128)}, f32[4,32,128]{2,1,0:T(8,128)}, f32[4,8,2048]{2...) custom-call(bf16[512,2304]{1,0:T(8,128)(2,1)} %slice.299.u_ref, bf16[512,128]{1,0:T(8,128)(2,1)} %copy.51.s_ref, ...), custom_call_target="tpu_custom_call" | custom-call | flops 2000000000 | bytes 12582912 | tf_op jit(solution)/shard_map/ssd_front/pallas_call | solution.py:452
  124.3 21.6 %collective-permute-done.9 = bf16[512,1024]{1,0:T(8,128)(2,1)} collective-permute-done((bf16[512,1024]{1,0:T(8,128)(2,1)}, bf16[512,1024]{1,0:T(8,128)(2,1)}, u32[]{:S(2)}, u32[]{:S(2)}) %collective-permute-start.9) | collective-permute-done | bytes 1048608 | tf_op jit(solution)/shard_map/ppermute | solution.py:556
  154.5 10.5 %collective-permute-done.7 = f32[64,2048]{1,0:T(8,128)S(1)} collective-permute-done((f32[64,2048]{1,0:T(8,128)}, f32[64,2048]{1,0:T(8,128)S(1)}, u32[]{:S(2)}, u32[]{:S(2)}) %collective-permute-start.7) | collective-permute-done | bytes 524320 | tf_op jit(solution)/shard_map/ppermute | solution.py:642
  172.3 23.9 %collective-permute-done.11 = bf16[256,4384]{0,1:T(8,128)(2,1)} collective-permute-done((bf16[256,4384]{0,1:T(8,128)(2,1)}, bf16[256,4384]{0,1:T(8,128)(2,1)}, u32[]{:S(2)}, u32[]{:S(2)}) %collective-permute-start.11) | collective-permute-done | bytes 2244640 | tf_op jit(solution)/shard_map/ppermute | solution.py:556
  196.8 10.9 %ssd_within.2.yloc_ref = f32[512,2048]{1,0:T(8,128)} custom-call(bf16[512,2560]{1,0:T(8,128)(2,1)} %get-tuple-element.62.act_ref.reads_ref.rest_ref, f32[512,128]{1,0:T(8,128)} %get-tuple-element.63.aux_ref, f32[4,32,128]{2,1,0:T(8,128)} %get-tuple-element.64.lt_ref, f32[528,128]{1,0:T(8,128)} %broadcast_in_dim.44.segx_ref, ...), custom_call_target="tpu_custom_call" | custom-call | flops 4000000000 | bytes 10485760 | tf_op jit(solution)/shard_map/ssd_within/pallas_call | solution.py:473
  208.7 8.2 ssd_gate.2
  228.1 12.1 %convolution_convert_fusion = bf16[512,4384]{1,0:T(8,128)(2,1)S(1)} fusion(bf16[512,1024]{1,0:T(8,128)(2,1)} %multiply_convert_fusion, bf16[512,4384]{0,1:T(8,128)(2,1)} %maximum_select_fusion.3, bf16[512,4384]{0,1:T(8,128)(2,1)} %get-tuple-element.121, pred[]{:T(512)S(6)} %eq.108), kind=kOutput, calls=%fused_computation.3 | convolution fusion | flops 4639604736 | bytes 14516225 | tf_op jit(solution)/shard_map/dot_general | solution.py:32
  246.2 13.2 %ssd_front.3 = (bf16[512,2560]{1,0:T(8,128)(2,1)}, bf16[512,2304]{1,0:T(8,128)(2,1)}, f32[512,128]{1,0:T(8,128)}, f32[4,32,128]{2,1,0:T(8,128)}, f32[4,8,2048]{2...) custom-call(bf16[512,2304]{1,0:T(8,128)(2,1)} %slice.320.u_ref, bf16[512,128]{1,0:T(8,128)(2,1)} %copy.54.s_ref, ...), custom_call_target="tpu_custom_call" | custom-call | flops 2000000000 | bytes 12582912 | tf_op jit(solution)/shard_map/ssd_front/pallas_call | solution.py:452
  262.1 5.4 collective-permute-start.21
  270.8 15.0 %collective-permute-done.17 = bf16[512,1024]{1,0:T(8,128)(2,1)} collective-permute-done((bf16[512,1024]{1,0:T(8,128)(2,1)S(1)}, bf16[512,1024]{1,0:T(8,128)(2,1)}, u32[]{:S(2)}, u32[]{:S(2)}) %collective-permute-start.17) | collective-permute-done | bytes 1048608 | tf_op jit(solution)/shard_map/ppermute | solution.py:556
  296.8 6.5 collective-permute-done.15
  310.9 10.9 %ssd_within.3.yloc_ref = f32[512,2048]{1,0:T(8,128)} custom-call(bf16[512,2560]{1,0:T(8,128)(2,1)} %get-tuple-element.71.act_ref.reads_ref.rest_ref, f32[512,128]{1,0:T(8,128)} %get-tuple-element.72.aux_ref, f32[4,32,128]{2,1,0:T(8,128)} %get-tuple-element.73.lt_ref, f32[528,128]{1,0:T(8,128)} %broadcast_in_dim.44.segx_ref, ...), custom_call_target="tpu_custom_call" | custom-call | flops 4000000000 | bytes 10485760 | tf_op jit(solution)/shard_map/ssd_within/pallas_call | solution.py:473
  322.9 8.2 ssd_gate.3
  331.2 5.2 add_convert_fusion
  337.4 5.3 collective-permute-start.19
  342.9 11.4 %gate_back.2 = (bf16[512,2048]{1,0:T(8,128)(2,1)}, bf16[512,2048]{1,0:T(8,128)(2,1)}, bf16[512,2048]{1,0:T(8,128)(2,1)}, f32[8,2048]{1,0:T(8,128)}, bf16[4,128,2...) custom-call(f32[512,2048]{1,0:T(8,128)} %fusion.70.dout_ref, ...), custom_call_target="tpu_custom_call" | custom-call | flops 3000000000 | bytes 18874368 | tf_op jit(solution)/shard_map/gate_back/pallas_call | solution.py:502
  358.0 17.7 %within_back.2 = (f32[512,2048]{1,0:T(8,128)}, f32[512,256]{1,0:T(8,128)}) custom-call(bf16[512,2560]{1,0:T(8,128)(2,1)} %get-tuple-element.71.act_ref.reads_ref.rest_ref, f32[512,128]{1,0:T(8,128)} %get-tuple-element.72.aux_ref, f32[4,32,128]{2,1,0:T(8,128)} %get-tuple-element.73.lt_ref, f32[528,128]{1,0:T(8,128)} %broadcast_in_dim.44.segx_ref, ...), custom_call_target="tpu_custom_call" | custom-call | flops 8000000000 | bytes 16777216 | tf_op jit(solution)/shard_map/within_back/pallas_call | solution.py:519
  389.3 5.4 collective-permute-done.24
  396.8 23.4 %ssd_last.2 = (bf16[512,2304]{1,0:T(8,128)(2,1)}, bf16[512,128]{1,0:T(8,128)(2,1)}, f32[8,2304]{1,0:T(8,128)}, bf16[8,2304]{1,0:T(8,128)(2,1)}, f32[40,2304]{1,0:T(8,128)}, /*index=5*/f32[24,128]{1,0:T(8,128)}) custom-call(bf16[512,2560]{1,0:T(8,128)(2,1)} %get-tuple-element.71.act_ref.reads_ref.rest_ref, f32[512,128]{1,0:T(8,128)} %get-tuple-element.72.aux_ref, ...), custom_call_target="tpu_custom_call" | custom-call | flops 6000000000 | bytes 25165824 | tf_op jit(solution)/shard_map/ssd_last/pallas_call | solution.py:535
  425.2 15.1 %multiply_reduce_fusion = (f32[1024]{0:T(1024)S(1)}, f32[512]{0:T(512)S(1)}, f32[512,1024]{1,0:T(8,128)S(1)}) fusion(f32[512,1024]{1,0:T(8,128)S(1)} %get-tuple-element.189, f32[512]{0:T(512)S(1)} %add_rsqrt_fusion, f32[1024]{0:T(1024)S(1)} %bitcast.133, bf16[512,4384]{0,1:T(8,128)(2,1)} %maximum_select_fusion.3, bf16[512,4384]{0,1:T(8,128)(2,1)} %get-tuple-element.121, ...), kind=kOutput, calls=%fused_computation.85 | convolution fusion | flops 4653971968 | bytes 17674240 | tf_op jit(solution)/shard_map/dot_general | solution.py:36
  443.2 7.3 fusion.71.dout_ref
  450.6 11.5 %gate_back.3 = (bf16[512,2048]{1,0:T(8,128)(2,1)}, bf16[512,2048]{1,0:T(8,128)(2,1)}, bf16[512,2048]{1,0:T(8,128)(2,1)}, f32[8,2048]{1,0:T(8,128)}, bf16[4,128,2...) custom-call(f32[512,2048]{1,0:T(8,128)} %fusion.71.dout_ref, ...), custom_call_target="tpu_custom_call" | custom-call | flops 3000000000 | bytes 18874368 | tf_op jit(solution)/shard_map/gate_back/pallas_call | solution.py:502
  465.8 18.1 %within_back.3 = (f32[512,2048]{1,0:T(8,128)}, f32[512,256]{1,0:T(8,128)}) custom-call(bf16[512,2560]{1,0:T(8,128)(2,1)} %get-tuple-element.62.act_ref.reads_ref.rest_ref, f32[512,128]{1,0:T(8,128)} %get-tuple-element.63.aux_ref, f32[4,32,128]{2,1,0:T(8,128)} %get-tuple-element.64.lt_ref, f32[528,128]{1,0:T(8,128)} %broadcast_in_dim.44.segx_ref, ...), custom_call_target="tpu_custom_call" | custom-call | flops 8000000000 | bytes 16777216 | tf_op jit(solution)/shard_map/within_back/pallas_call | solution.py:519
  495.2 17.2 %collective-permute-done.52 = bf16[512,1024]{1,0:T(8,128)(2,1)S(1)} collective-permute-done((bf16[512,1024]{1,0:T(8,128)(2,1)S(1)}, bf16[512,1024]{1,0:T(8,128)(2,1)S(1)}, u32[]{:S(2)}, u32[]{:S(2)}) %collective-permute-start.52) | collective-permute-done | bytes 1048608 | tf_op jit(solution)/shard_map/ppermute | solution.py:556
  532.3 23.4 %ssd_last.3 = (bf16[512,2304]{1,0:T(8,128)(2,1)}, bf16[512,128]{1,0:T(8,128)(2,1)}, f32[8,2304]{1,0:T(8,128)}, bf16[8,2304]{1,0:T(8,128)(2,1)}, f32[40,2304]{1,0:T(8,128)}, /*index=5*/f32[24,128]{1,0:T(8,128)}) custom-call(bf16[512,2560]{1,0:T(8,128)(2,1)} %get-tuple-element.62.act_ref.reads_ref.rest_ref, f32[512,128]{1,0:T(8,128)} %get-tuple-element.63.aux_ref, ...), custom_call_target="tpu_custom_call" | custom-call | flops 6000000000 | bytes 25165824 | tf_op jit(solution)/shard_map/ssd_last/pallas_call | solution.py:535
  560.7 16.4 %fusion.44 = (f32[1024]{0:T(1024)S(1)}, f32[512]{0:T(512)S(1)}, f32[512,1024]{1,0:T(8,128)}) fusion(f32[512]{0:T(512)S(1)} %copy-done.54, bf16[256,1024]{1,0:T(8,128)(2,1)S(1)} %copy-done.3, bf16[256,1024]{1,0:T(8,128)(2,1)S(1)} %copy-done.1, f32[1024]{0:T(1024)S(1)} %bitcast.136, bf16[512,4384]{0,1:T(8,128)(2,1)} %maximum_select_fusion.2, ...), kind=kOutput, calls=%fused_computation.65 | convolution fusion | flops 4656069120 | bytes 16625665 | tf_op jit(solution)/shard_map/dot_general | solution.py:36
  594.7 5.1 fusion.30
  599.8 18.2 %collective-permute-done.90 = f32[240,128]{1,0:T(8,128)S(1)} collective-permute-done((f32[240,128]{1,0:T(8,128)S(1)}, f32[240,128]{1,0:T(8,128)S(1)}, u32[]{:S(2)}, u32[]{:S(2)}) %collective-permute-start.90) | collective-permute-done | bytes 122912 | tf_op jit(solution)/shard_map/ppermute | solution.py:556
  640.5 8.0 collective-permute-done.30
  649.6 8.4 collective-permute-done.93
  660.2 6.5 collective-permute-done.54
  669.1 7.1 collective-permute-done.55
  677.6 6.1 collective-permute-done.56
  691.9 6.8 collective-permute-done.72
  726.2 6.1 collective-permute-done.58
  737.0 6.9 collective-permute-done.84
  744.4 10.7 %collective-permute-done.36 = bf16[64,1024]{1,0:T(8,128)(2,1)S(1)} collective-permute-done((bf16[64,1024]{1,0:T(8,128)(2,1)S(1)}, bf16[64,1024]{1,0:T(8,128)(2,1)S(1)}, u32[]{:S(2)}, u32[]{:S(2)}) %collective-permute-start.36) | collective-permute-done | bytes 131104 | tf_op jit(solution)/shard_map/ppermute | solution.py:561
  765.1 7.9 collective-permute-done.63
  782.9 6.3 collective-permute-done.64
  796.4 7.4 collective-permute-done.65
  815.2 7.4 collective-permute-done.45
  825.7 13.3 %collective-permute-done.46 = bf16[64,1184]{0,1:T(8,128)(2,1)S(1)} collective-permute-done((bf16[64,1184]{0,1:T(8,128)(2,1)S(1)}, bf16[64,1184]{0,1:T(8,128)(2,1)S(1)}, u32[]{:S(2)}, u32[]{:S(2)}) %collective-permute-start.46) | collective-permute-done | bytes 151584 | tf_op jit(solution)/shard_map/ppermute | solution.py:561
  851.4 12.2 %collective-permute-done.48 = bf16[256,1184]{0,1:T(8,128)(2,1)S(1)} collective-permute-done((bf16[256,1184]{0,1:T(8,128)(2,1)S(1)}, bf16[256,1184]{0,1:T(8,128)(2,1)S(1)}, u32[]{:S(2)}, u32[]{:S(2)}) %collective-permute-start.48) | collective-permute-done | bytes 606240 | tf_op jit(solution)/shard_map/ppermute | solution.py:561
  880.7 13.4 %maximum_convert_fusion = f32[2,512,4384]{1,2,0:T(8,128)} fusion(bf16[1,512,32]{1,2,0:T(8,128)(2,1)S(1)} %slice_bitcast_fusion.2, bf16[1,512,2304]{1,2,0:T(8,128)(2,1)S(1)} %fusion.37, bf16[1,512,2048]{1,2,0:T(8,128)(2,1)S(1)} %copy.62, bf16[1,512,32]{1,2,0:T(8,128)(2,1)S(1)} %slice_bitcast_fusion.3, bf16[1,512,2304]{1,2,0:T(8,128)(2,1)S(1)} %fusion.36, ...), kind=kLoop, calls=%fused_computation.2 | loop fusion | flops 53870592 | bytes 26935296 | tf_op jit(solution)/shard_map/stack | solution.py:880
  (510 shorter events, 327.1 us)
Async XLA Ops:
  4.3 29.1 %collective-permute-start.2 = (bf16[2,8,1152]{2,0,1:T(2,128)(2,1)S(1)}, bf16[2,8,1152]{2,0,1:T(2,128)(2,1)S(1)}, u32[]{:S(2)}, u32[]{:S(2)}) collective-permute-start(bf16[2,8,1152]{2,0,1:T(2,128)(2,1)S(1)} %constant_dynamic-update-slice_fusion), channel_id=1, source_target_pairs={{0,8},{8,0},{1,9},{9,1},{2,10},{10,2},{3,11},{11,3},{4,12},{12,4},... | collective-permute-start | bytes 110600 | tf_op jit(solution)/shard_map/ppermute | solution.py:556
  9.4 68.4 %collective-permute-start = (bf16[256,1024]{1,0:T(8,128)(2,1)}, bf16[256,1024]{1,0:T(8,128)(2,1)S(1)}, u32[]{:S(2)}, u32[]{:S(2)}) collective-permute-start(bf16[256,1024]{1,0:T(8,128)(2,1)} %get-tuple-element.165), channel_id=1, source_target_pairs={{0,0},{1,4},{2,1},{3,5},{4,2},{5,6},{6,3},{7,7},{8,8},{9,12},{10,9... | collective-permute-start | bytes 1572872 | tf_op jit(solution)/shard_map/ppermute | solution.py:585
  11.0 67.5 %collective-permute-start.1 = (bf16[256,1024]{1,0:T(8,128)(2,1)S(1)}, bf16[256,1024]{1,0:T(8,128)(2,1)}, u32[]{:S(2)}, u32[]{:S(2)}) collective-permute-start(bf16[256,1024]{1,0:T(8,128)(2,1)S(1)} %get-tuple-element.166), channel_id=1, source_target_pairs={{0,4},{1,0},{2,5},{3,1},{4,6},{5,2},{6,7},{7,3},{8,12},{9,8},{10,1... | collective-permute-start | bytes 1572872 | tf_op jit(solution)/shard_map/ppermute | solution.py:586
  26.3 50.7 %collective-permute-start.3 = (bf16[256,4384]{0,1:T(8,128)(2,1)}, bf16[256,4384]{0,1:T(8,128)(2,1)}, u32[]{:S(2)}, u32[]{:S(2)}) collective-permute-start(bf16[256,4384]{0,1:T(8,128)(2,1)} %dynamic-slice_bitcast_fusion.1), channel_id=1, source_target_pairs={{0,8},{8,0},{1,9},{9,1},{2,10},{10,2},{3,11},{11,3},{4,12},{12,4},... | collective-permute-start | bytes 6733832 | tf_op jit(solution)/shard_map/ppermute | solution.py:556
  118.6 27.9 %collective-permute-start.6 = (f32[136,2048]{1,0:T(8,128)}, f32[136,2048]{1,0:T(8,128)}, u32[]{:S(2)}, u32[]{:S(2)}) collective-permute-start(f32[136,2048]{1,0:T(8,128)} %get-tuple-element.67), channel_id=1, source_target_pairs={{0,1},{1,0},{2,3},{3,2},{4,5},{5,4},{6,7},{7,6},{8,9},{9,8},{10,11... | collective-permute-start | bytes 3342344 | tf_op jit(solution)/shard_map/ppermute | solution.py:556
  120.6 25.4 %collective-permute-start.9 = (bf16[512,1024]{1,0:T(8,128)(2,1)}, bf16[512,1024]{1,0:T(8,128)(2,1)}, u32[]{:S(2)}, u32[]{:S(2)}) collective-permute-start(bf16[512,1024]{1,0:T(8,128)(2,1)} %dynamic-slice_bitcast_fusion.3), channel_id=1, source_target_pairs={{0,8},{8,0},{1,9},{9,1},{2,10},{10,2},{3,11},{11,3},{4,12},{12,4},... | collective-permute-start | bytes 3145736 | tf_op jit(solution)/shard_map/ppermute | solution.py:556
  146.0 50.2 %collective-permute-start.11 = (bf16[256,4384]{0,1:T(8,128)(2,1)}, bf16[256,4384]{0,1:T(8,128)(2,1)}, u32[]{:S(2)}, u32[]{:S(2)}) collective-permute-start(bf16[256,4384]{0,1:T(8,128)(2,1)} %dynamic-slice_bitcast_fusion), channel_id=1, source_target_pairs={{0,8},{8,0},{1,9},{9,1},{2,10},{10,2},{3,11},{11,3},{4,12},{12,4},... | collective-permute-start | bytes 6733832 | tf_op jit(solution)/shard_map/ppermute | solution.py:556
  165.0 42.7 %collective-permute-start.8 = (f32[64,2048]{1,0:T(8,128)S(1)}, f32[64,2048]{1,0:T(8,128)S(1)}, u32[]{:S(2)}, u32[]{:S(2)}) collective-permute-start(f32[64,2048]{1,0:T(8,128)S(1)} %collective-permute-done.7), channel_id=1, source_target_pairs={{0,1},{1,0},{2,3},{3,2},{4,5},{5,4},{6,7},{7,6},{8,9},{9,8},{10,11... | collective-permute-start | bytes 1572872 | tf_op jit(solution)/shard_map/ppermute | solution.py:556
  196.2 27.2 %collective-permute-start.12 = (bf16[256,4384]{0,1:T(8,128)(2,1)}, bf16[256,4384]{0,1:T(8,128)(2,1)S(1)}, u32[]{:S(2)}, u32[]{:S(2)}) collective-permute-start(bf16[256,4384]{0,1:T(8,128)(2,1)} %collective-permute-done.11), channel_id=1, source_target_pairs={{0,1},{1,0},{2,3},{3,2},{4,5},{5,4},{6,7},{7,6},{8,9},{9,8},{10,11... | collective-permute-start | bytes 6733832 | tf_op jit(solution)/shard_map/ppermute | solution.py:556
  259.4 26.3 %collective-permute-start.14 = (f32[136,2048]{1,0:T(8,128)}, f32[136,2048]{1,0:T(8,128)}, u32[]{:S(2)}, u32[]{:S(2)}) collective-permute-start(f32[136,2048]{1,0:T(8,128)} %get-tuple-element.76), channel_id=1, source_target_pairs={{0,1},{1,0},{2,3},{3,2},{4,5},{5,4},{6,7},{7,6},{8,9},{9,8},{10,11... | collective-permute-start | bytes 3342344 | tf_op jit(solution)/shard_map/ppermute | solution.py:556
  260.5 25.3 %collective-permute-start.17 = (bf16[512,1024]{1,0:T(8,128)(2,1)S(1)}, bf16[512,1024]{1,0:T(8,128)(2,1)}, u32[]{:S(2)}, u32[]{:S(2)}) collective-permute-start(bf16[512,1024]{1,0:T(8,128)(2,1)S(1)} %dynamic-slice_bitcast_fusion.2), channel_id=1, source_target_pairs={{0,8},{8,0},{1,9},{9,1},{2,10},{10,2},{3,11},{11,3},{4,12},{12,4},... | collective-permute-start | bytes 3145736 | tf_op jit(solution)/shard_map/ppermute | solution.py:556
  262.1 29.4 %collective-permute-start.21 = (bf16[256,1024]{1,0:T(8,128)(2,1)}, bf16[256,1024]{1,0:T(8,128)(2,1)}, u32[]{:S(2)}, u32[]{:S(2)}) collective-permute-start(bf16[256,1024]{1,0:T(8,128)(2,1)} %get-tuple-element.157), channel_id=1, source_target_pairs={{0,0},{1,4},{2,1},{3,5},{4,2},{5,6},{6,3},{7,7},{8,8},{9,12},{10,9... | collective-permute-start | bytes 1572872 | tf_op jit(solution)/shard_map/ppermute | solution.py:585
  267.5 24.0 %collective-permute-start.22 = (bf16[256,1024]{1,0:T(8,128)(2,1)}, bf16[256,1024]{1,0:T(8,128)(2,1)}, u32[]{:S(2)}, u32[]{:S(2)}) collective-permute-start(bf16[256,1024]{1,0:T(8,128)(2,1)} %get-tuple-element.158), channel_id=1, source_target_pairs={{0,4},{1,0},{2,5},{3,1},{4,6},{5,2},{6,7},{7,3},{8,12},{9,8},{10,1... | collective-permute-start | bytes 1572872 | tf_op jit(solution)/shard_map/ppermute | solution.py:586
  293.9 87.8 %collective-permute-start.50 = (bf16[512,1024]{1,0:T(8,128)(2,1)}, bf16[512,1024]{1,0:T(8,128)(2,1)}, u32[]{:S(2)}, u32[]{:S(2)}) collective-permute-start(bf16[512,1024]{1,0:T(8,128)(2,1)} %multiply_convert_fusion), channel_id=1, source_target_pairs={{0,1},{1,0},{2,3},{3,2},{4,5},{5,4},{6,7},{7,6},{8,9},{9,8},{10,11... | collective-permute-start | bytes 3145736 | tf_op jit(solution)/shard_map/ppermute | solution.py:556
  337.4 39.9 %collective-permute-start.19 = (bf16[256,1024]{1,0:T(8,128)(2,1)}, bf16[256,1024]{1,0:T(8,128)(2,1)}, u32[]{:S(2)}, u32[]{:S(2)}) collective-permute-start(bf16[256,1024]{1,0:T(8,128)(2,1)} %get-tuple-element.161), channel_id=1, source_target_pairs={{0,0},{4,1},{1,2},{5,3},{2,4},{6,5},{3,6},{7,7},{8,8},{12,9},{9,10... | collective-permute-start | bytes 1572872 | tf_op jit(solution)/shard_map/ppermute | solution.py:597
  342.8 35.1 %collective-permute-start.20 = (bf16[256,1024]{1,0:T(8,128)(2,1)}, bf16[256,1024]{1,0:T(8,128)(2,1)}, u32[]{:S(2)}, u32[]{:S(2)}) collective-permute-start(bf16[256,1024]{1,0:T(8,128)(2,1)} %get-tuple-element.162), channel_id=1, source_target_pairs={{4,0},{0,1},{5,2},{1,3},{6,4},{2,5},{7,6},{3,7},{12,8},{8,9},{13,1... | collective-permute-start | bytes 1572872 | tf_op jit(solution)/shard_map/ppermute | solution.py:598
  357.5 24.4 %collective-permute-start.51 = (bf16[512,1024]{1,0:T(8,128)(2,1)}, bf16[512,1024]{1,0:T(8,128)(2,1)}, u32[]{:S(2)}, u32[]{:S(2)}) collective-permute-start(bf16[512,1024]{1,0:T(8,128)(2,1)} %get-tuple-element.140), channel_id=1, source_target_pairs={{0,1},{1,0},{2,3},{3,2},{4,5},{5,4},{6,7},{7,6},{8,9},{9,8},{10,11... | collective-permute-start | bytes 3145736 | tf_op jit(solution)/shard_map/ppermute | solution.py:556
  375.7 146.0 %collective-permute-start.31 = (bf16[512,1024]{1,0:T(8,128)(2,1)}, bf16[512,1024]{1,0:T(8,128)(2,1)}, u32[]{:S(2)}, u32[]{:S(2)}) collective-permute-start(bf16[512,1024]{1,0:T(8,128)(2,1)} %fusion.38), channel_id=1, source_target_pairs={{0,1},{1,0},{2,3},{3,2},{4,5},{5,4},{6,7},{7,6},{8,9},{9,8},{10,11... | collective-permute-start | bytes 3145736 | tf_op jit(solution)/shard_map/ppermute | solution.py:556
  377.3 108.8 %collective-permute-start.69 = (bf16[512,2048]{1,0:T(8,128)(2,1)}, bf16[512,2048]{1,0:T(8,128)(2,1)}, u32[]{:S(2)}, u32[]{:S(2)}) collective-permute-start(bf16[512,2048]{1,0:T(8,128)(2,1)} %get-tuple-element.68), channel_id=1, source_target_pairs={{0,1},{1,0},{2,3},{3,2},{4,5},{5,4},{6,7},{7,6},{8,9},{9,8},{10,11... | collective-permute-start | bytes 6291464 | tf_op jit(solution)/shard_map/ppermute | solution.py:556
  381.7 133.5 %collective-permute-start.79 = (bf16[512,2048]{1,0:T(8,128)(2,1)}, bf16[512,2048]{1,0:T(8,128)(2,1)}, u32[]{:S(2)}, u32[]{:S(2)}) collective-permute-start(bf16[512,2048]{1,0:T(8,128)(2,1)} %get-tuple-element.77), channel_id=1, source_target_pairs={{0,1},{1,0},{2,3},{3,2},{4,5},{5,4},{6,7},{7,6},{8,9},{9,8},{10,11... | collective-permute-start | bytes 6291464 | tf_op jit(solution)/shard_map/ppermute | solution.py:556
  462.1 29.9 %collective-permute-start.26 = (bf16[128,2048]{1,0:T(8,128)(2,1)}, bf16[128,2048]{1,0:T(8,128)(2,1)}, u32[]{:S(2)}, u32[]{:S(2)}) collective-permute-start(bf16[128,2048]{1,0:T(8,128)(2,1)} %get-tuple-element.102), channel_id=1, source_target_pairs={{0,1},{1,0},{2,3},{3,2},{4,5},{5,4},{6,7},{7,6},{8,9},{9,8},{10,11... | collective-permute-start | bytes 1572872 | tf_op jit(solution)/shard_map/ppermute | solution.py:556
  486.7 27.1 %collective-permute-start.80 = (bf16[512,512]{1,0:T(8,128)(2,1)S(1)}, bf16[512,512]{1,0:T(8,128)(2,1)S(1)}, u32[]{:S(2)}, u32[]{:S(2)}) collective-permute-start(bf16[512,512]{1,0:T(8,128)(2,1)S(1)} %copy-done.40), channel_id=1, source_target_pairs={{0,1},{1,0},{2,3},{3,2},{4,5},{5,4},{6,7},{7,6},{8,9},{9,8},{10,11... | collective-permute-start | bytes 1572872 | tf_op jit(solution)/shard_map/ppermute | solution.py:556
  487.1 25.3 %collective-permute-start.52 = (bf16[512,1024]{1,0:T(8,128)(2,1)S(1)}, bf16[512,1024]{1,0:T(8,128)(2,1)S(1)}, u32[]{:S(2)}, u32[]{:S(2)}) collective-permute-start(bf16[512,1024]{1,0:T(8,128)(2,1)S(1)} %copy-done.37), channel_id=1, source_target_pairs={{0,8},{8,0},{1,9},{9,1},{2,10},{10,2},{3,11},{11,3},{4,12},{12,4},... | collective-permute-start | bytes 3145736 | tf_op jit(solution)/shard_map/ppermute | solution.py:556
  492.0 31.3 %collective-permute-start.32 = (bf16[512,1024]{1,0:T(8,128)(2,1)S(1)}, bf16[512,1024]{1,0:T(8,128)(2,1)S(1)}, u32[]{:S(2)}, u32[]{:S(2)}) collective-permute-start(bf16[512,1024]{1,0:T(8,128)(2,1)S(1)} %get-tuple-element.138), channel_id=1, source_target_pairs={{0,1},{1,0},{2,3},{3,2},{4,5},{5,4},{6,7},{7,6},{8,9},{9,8},{10,11... | collective-permute-start | bytes 3145736 | tf_op jit(solution)/shard_map/ppermute | solution.py:556
  512.4 78.3 %collective-permute-start.60 = (bf16[512,1184]{0,1:T(8,128)(2,1)}, bf16[512,1184]{0,1:T(8,128)(2,1)}, u32[]{:S(2)}, u32[]{:S(2)}) collective-permute-start(bf16[512,1184]{0,1:T(8,128)(2,1)} %copy.60), channel_id=1, source_target_pairs={{0,1},{1,0},{2,3},{3,2},{4,5},{5,4},{6,7},{7,6},{8,9},{9,8},{10,11... | collective-permute-start | bytes 3637256 | tf_op jit(solution)/shard_map/ppermute | solution.py:556
  515.3 112.2 %collective-permute-start.71 = (bf16[1024,512]{1,0:T(8,128)(2,1)}, bf16[1024,512]{1,0:T(8,128)(2,1)}, u32[]{:S(2)}, u32[]{:S(2)}) collective-permute-start(bf16[1024,512]{1,0:T(8,128)(2,1)} %dynamic-slice_convert_fusion.3), channel_id=1, source_target_pairs={{0,8},{8,0},{1,9},{9,1},{2,10},{10,2},{3,11},{11,3},{4,12},{12,4},... | collective-permute-start | bytes 3145736 | tf_op jit(solution)/shard_map/ppermute | solution.py:556
  521.8 103.0 %collective-permute-start.53 = (bf16[256,1024]{1,0:T(8,128)(2,1)}, bf16[256,1024]{1,0:T(8,128)(2,1)}, u32[]{:S(2)}, u32[]{:S(2)}) collective-permute-start(bf16[256,1024]{1,0:T(8,128)(2,1)} %dynamic-slice_convert_fusion.10), channel_id=1, source_target_pairs={{0,16},{16,0},{1,17},{17,1},{2,18},{18,2},{3,19},{19,3},{4,20},{20... | collective-permute-start | bytes 1572872 | tf_op jit(solution)/shard_map/ppermute | solution.py:561
  523.3 161.0 %collective-permute-start.81 = (bf16[1024,512]{1,0:T(8,128)(2,1)}, bf16[1024,512]{1,0:T(8,128)(2,1)}, u32[]{:S(2)}, u32[]{:S(2)}) collective-permute-start(bf16[1024,512]{1,0:T(8,128)(2,1)} %dynamic-slice_convert_fusion.2), channel_id=1, source_target_pairs={{0,8},{8,0},{1,9},{9,1},{2,10},{10,2},{3,11},{11,3},{4,12},{12,4},... | collective-permute-start | bytes 3145736 | tf_op jit(solution)/shard_map/ppermute | solution.py:556
  590.2 97.6 %collective-permute-start.33 = (bf16[512,1024]{1,0:T(8,128)(2,1)}, bf16[512,1024]{1,0:T(8,128)(2,1)}, u32[]{:S(2)}, u32[]{:S(2)}) collective-permute-start(bf16[512,1024]{1,0:T(8,128)(2,1)} %dynamic-slice_convert_fusion.5), channel_id=1, source_target_pairs={{0,8},{8,0},{1,9},{9,1},{2,10},{10,2},{3,11},{11,3},{4,12},{12,4},... | collective-permute-start | bytes 3145736 | tf_op jit(solution)/shard_map/ppermute | solution.py:556
  590.7 27.4 %collective-permute-start.90 = (f32[240,128]{1,0:T(8,128)S(1)}, f32[240,128]{1,0:T(8,128)S(1)}, u32[]{:S(2)}, u32[]{:S(2)}) collective-permute-start(f32[240,128]{1,0:T(8,128)S(1)} %add.430), channel_id=1, source_target_pairs={{0,8},{8,0},{1,9},{9,1},{2,10},{10,2},{3,11},{11,3},{4,12},{12,4},... | collective-permute-start | bytes 368648 | tf_op jit(solution)/shard_map/ppermute | solution.py:556
  624.8 23.7 %collective-permute-start.30 = (bf16[256,1024]{1,0:T(8,128)(2,1)}, bf16[256,1024]{1,0:T(8,128)(2,1)S(1)}, u32[]{:S(2)}, u32[]{:S(2)}) collective-permute-start(bf16[256,1024]{1,0:T(8,128)(2,1)} %get-tuple-element.154), channel_id=1, source_target_pairs={{4,0},{0,1},{5,2},{1,3},{6,4},{2,5},{7,6},{3,7},{12,8},{8,9},{13,1... | collective-permute-start | bytes 1572872 | tf_op jit(solution)/shard_map/ppermute | solution.py:598
  636.2 63.3 %collective-permute-start.41 = (bf16[512,1184]{0,1:T(8,128)(2,1)}, bf16[512,1184]{0,1:T(8,128)(2,1)}, u32[]{:S(2)}, u32[]{:S(2)}) collective-permute-start(bf16[512,1184]{0,1:T(8,128)(2,1)} %copy.57), channel_id=1, source_target_pairs={{0,1},{1,0},{2,3},{3,2},{4,5},{5,4},{6,7},{7,6},{8,9},{9,8},{10,11... | collective-permute-start | bytes 3637256 | tf_op jit(solution)/shard_map/ppermute | solution.py:556
  640.0 70.2 %collective-permute-start.61 = (bf16[512,1184]{0,1:T(8,128)(2,1)}, bf16[512,1184]{0,1:T(8,128)(2,1)}, u32[]{:S(2)}, u32[]{:S(2)}) collective-permute-start(bf16[512,1184]{0,1:T(8,128)(2,1)} %dynamic-slice_convert_fusion), channel_id=1, source_target_pairs={{0,8},{8,0},{1,9},{9,1},{2,10},{10,2},{3,11},{11,3},{4,12},{12,4},... | collective-permute-start | bytes 3637256 | tf_op jit(solution)/shard_map/ppermute | solution.py:556
  687.8 31.5 %collective-permute-start.82 = (bf16[512,512]{1,0:T(8,128)(2,1)}, bf16[512,512]{1,0:T(8,128)(2,1)}, u32[]{:S(2)}, u32[]{:S(2)}) collective-permute-start(bf16[512,512]{1,0:T(8,128)(2,1)} %dynamic-slice_convert_fusion.8), channel_id=1, source_target_pairs={{0,16},{16,0},{1,17},{17,1},{2,18},{18,2},{3,19},{19,3},{4,20},{20... | collective-permute-start | bytes 1572872 | tf_op jit(solution)/shard_map/ppermute | solution.py:561
  698.7 22.8 %collective-permute-start.34 = (bf16[256,1024]{1,0:T(8,128)(2,1)}, bf16[256,1024]{1,0:T(8,128)(2,1)}, u32[]{:S(2)}, u32[]{:S(2)}) collective-permute-start(bf16[256,1024]{1,0:T(8,128)(2,1)} %dynamic-slice_convert_fusion.11), channel_id=1, source_target_pairs={{0,16},{16,0},{1,17},{17,1},{2,18},{18,2},{3,19},{19,3},{4,20},{20... | collective-permute-start | bytes 1572872 | tf_op jit(solution)/shard_map/ppermute | solution.py:561
  706.7 66.6 %collective-permute-start.42 = (bf16[512,1184]{0,1:T(8,128)(2,1)S(1)}, bf16[512,1184]{0,1:T(8,128)(2,1)S(1)}, u32[]{:S(2)}, u32[]{:S(2)}) collective-permute-start(bf16[512,1184]{0,1:T(8,128)(2,1)S(1)} %dynamic-slice_convert_fusion.1), channel_id=1, source_target_pairs={{0,8},{8,0},{1,9},{9,1},{2,10},{10,2},{3,11},{11,3},{4,12},{12,4},... | collective-permute-start | bytes 3637256 | tf_op jit(solution)/shard_map/ppermute | solution.py:556
  708.5 23.9 %collective-permute-start.58 = (bf16[256,1024]{1,0:T(8,128)(2,1)S(1)}, bf16[256,1024]{1,0:T(8,128)(2,1)S(1)}, u32[]{:S(2)}, u32[]{:S(2)}) collective-permute-start(bf16[256,1024]{1,0:T(8,128)(2,1)S(1)} %maximum_select_fusion.33), channel_id=1, source_target_pairs={{0,16},{16,0},{1,17},{17,1},{2,18},{18,2},{3,19},{19,3},{4,20},{20... | collective-permute-start | bytes 1572872 | tf_op jit(solution)/shard_map/ppermute | solution.py:561
  719.3 35.9 %collective-permute-start.62 = (bf16[256,1184]{0,1:T(8,128)(2,1)S(1)}, bf16[256,1184]{0,1:T(8,128)(2,1)S(1)}, u32[]{:S(2)}, u32[]{:S(2)}) collective-permute-start(bf16[256,1184]{0,1:T(8,128)(2,1)S(1)} %dynamic-slice_convert_fusion.6), channel_id=1, source_target_pairs={{0,16},{16,0},{1,17},{17,1},{2,18},{18,2},{3,19},{19,3},{4,20},{20... | collective-permute-start | bytes 1818632 | tf_op jit(solution)/shard_map/ppermute | solution.py:561
  732.4 26.0 %collective-permute-start.76 = (bf16[256,512]{1,0:T(8,128)(2,1)S(1)}, bf16[256,512]{1,0:T(8,128)(2,1)S(1)}, u32[]{:S(2)}, u32[]{:S(2)}) collective-permute-start(bf16[256,512]{1,0:T(8,128)(2,1)S(1)} %maximum_select_fusion.40), channel_id=1, source_target_pairs={{0,2},{2,0},{4,6},{6,4},{1,3},{3,1},{5,7},{7,5},{8,10},{10,8},{12,... | collective-permute-start | bytes 786440 | tf_op jit(solution)/shard_map/ppermute | solution.py:561
  732.9 72.4 %collective-permute-start.59 = (bf16[512,1024]{1,0:T(8,128)(2,1)S(1)}, bf16[512,1024]{1,0:T(8,128)(2,1)S(1)}, u32[]{:S(2)}, u32[]{:S(2)}) collective-permute-start(bf16[512,1024]{1,0:T(8,128)(2,1)S(1)} %maximum_select_fusion.23), channel_id=1, source_target_pairs={{0,1},{1,0},{2,3},{3,2},{4,5},{5,4},{6,7},{7,6},{8,9},{9,8},{10,11... | collective-permute-start | bytes 3145736 | tf_op jit(solution)/shard_map/ppermute | solution.py:556
  761.7 32.4 %collective-permute-start.77 = (bf16[512,512]{1,0:T(8,128)(2,1)S(1)}, bf16[512,512]{1,0:T(8,128)(2,1)S(1)}, u32[]{:S(2)}, u32[]{:S(2)}) collective-permute-start(bf16[512,512]{1,0:T(8,128)(2,1)S(1)} %maximum_select_fusion.34), channel_id=1, source_target_pairs={{0,16},{16,0},{1,17},{17,1},{2,18},{18,2},{3,19},{19,3},{4,20},{20... | collective-permute-start | bytes 1572872 | tf_op jit(solution)/shard_map/ppermute | solution.py:561
  781.6 31.7 %collective-permute-start.87 = (bf16[512,512]{1,0:T(8,128)(2,1)}, bf16[512,512]{1,0:T(8,128)(2,1)}, u32[]{:S(2)}, u32[]{:S(2)}) collective-permute-start(bf16[512,512]{1,0:T(8,128)(2,1)} %maximum_select_fusion.35), channel_id=1, source_target_pairs={{0,16},{16,0},{1,17},{17,1},{2,18},{18,2},{3,19},{19,3},{4,20},{20... | collective-permute-start | bytes 1572872 | tf_op jit(solution)/shard_map/ppermute | solution.py:561
  789.3 50.2 %collective-permute-start.39 = (bf16[256,1024]{1,0:T(8,128)(2,1)}, bf16[256,1024]{1,0:T(8,128)(2,1)}, u32[]{:S(2)}, u32[]{:S(2)}) collective-permute-start(bf16[256,1024]{1,0:T(8,128)(2,1)} %maximum_select_fusion.32), channel_id=1, source_target_pairs={{0,16},{16,0},{1,17},{17,1},{2,18},{18,2},{3,19},{19,3},{4,20},{20... | collective-permute-start | bytes 1572872 | tf_op jit(solution)/shard_map/ppermute | solution.py:561
  803.9 37.7 %collective-permute-start.78 = (bf16[1024,512]{1,0:T(8,128)(2,1)S(1)}, bf16[1024,512]{1,0:T(8,128)(2,1)}, u32[]{:S(2)}, u32[]{:S(2)}) collective-permute-start(bf16[1024,512]{1,0:T(8,128)(2,1)S(1)} %maximum_select_fusion.24), channel_id=1, source_target_pairs={{0,1},{1,0},{2,3},{3,2},{4,5},{5,4},{6,7},{7,6},{8,9},{9,8},{10,11... | collective-permute-start | bytes 3145736 | tf_op jit(solution)/shard_map/ppermute | solution.py:556
  815.2 35.6 %collective-permute-start.88 = (bf16[1024,512]{1,0:T(8,128)(2,1)S(1)}, bf16[1024,512]{1,0:T(8,128)(2,1)S(1)}, u32[]{:S(2)}, u32[]{:S(2)}) collective-permute-start(bf16[1024,512]{1,0:T(8,128)(2,1)S(1)} %maximum_select_fusion.25), channel_id=1, source_target_pairs={{0,1},{1,0},{2,3},{3,2},{4,5},{5,4},{6,7},{7,6},{8,9},{9,8},{10,11... | collective-permute-start | bytes 3145736 | tf_op jit(solution)/shard_map/ppermute | solution.py:556
  825.2 24.1 %collective-permute-start.67 = (bf16[256,1184]{0,1:T(8,128)(2,1)S(1)}, bf16[256,1184]{0,1:T(8,128)(2,1)S(1)}, u32[]{:S(2)}, u32[]{:S(2)}) collective-permute-start(bf16[256,1184]{0,1:T(8,128)(2,1)S(1)} %maximum_select_fusion.31), channel_id=1, source_target_pairs={{0,16},{16,0},{1,17},{17,1},{2,18},{18,2},{3,19},{19,3},{4,20},{20... | collective-permute-start | bytes 1818632 | tf_op jit(solution)/shard_map/ppermute | solution.py:561
  841.5 27.6 %collective-permute-start.40 = (bf16[512,1024]{1,0:T(8,128)(2,1)S(1)}, bf16[512,1024]{1,0:T(8,128)(2,1)S(1)}, u32[]{:S(2)}, u32[]{:S(2)}) collective-permute-start(bf16[512,1024]{1,0:T(8,128)(2,1)S(1)} %maximum_select_fusion.22), channel_id=1, source_target_pairs={{0,1},{1,0},{2,3},{3,2},{4,5},{5,4},{6,7},{7,6},{8,9},{9,8},{10,11... | collective-permute-start | bytes 3145736 | tf_op jit(solution)/shard_map/ppermute | solution.py:556
  850.8 24.3 %collective-permute-start.68 = (bf16[512,1152]{0,1:T(8,128)(2,1)}, bf16[512,1152]{0,1:T(8,128)(2,1)}, u32[]{:S(2)}, u32[]{:S(2)}) collective-permute-start(bf16[512,1152]{0,1:T(8,128)(2,1)} %slice.334), channel_id=1, source_target_pairs={{0,1},{1,0},{2,3},{3,2},{4,5},{5,4},{6,7},{7,6},{8,9},{9,8},{10,11... | collective-permute-start | bytes 3538952 | tf_op jit(solution)/shard_map/ppermute | solution.py:556
  (105 other events, 1377.6 us)

commit v2 on v1

--- a/solution.py
+++ b/solution.py
@@ -22,6 +22,11 @@
 BLOCKS = CH // LANES
 KEYS, READS, KEYS_REST, READS_REST = (slice(DI + i * N, DI + (i + 1) * N) for i in range(4))
 ACT = DI + 4 * N
+E = DI + CH + H
+US = CH + H
+HALF = CH // 2 + LANES
+WIDE = 512
+FAR_MID, NEAR_MID = DI // 2, 768
 FAR = -1e30
 F32 = jnp.float32
 BF16 = jnp.bfloat16
@@ -77,7 +82,7 @@
 
 
 def front_kernel(
-    u_ref, s_ref, rim_ref, segx_ref, taps_ref, heads_ref, oht_ref,
+    us_ref, rim_ref, segx_ref, taps_ref, heads_ref, oht_ref, copies_ref,
     act_ref, slope_ref, aux_ref, lt_ref, drow_ref, sout_ref, msg_ref,
     ubuf, state, decay, xbuf,
 ):
@@ -98,7 +103,7 @@
     masks = [(seg_rows[5 + k : 5 + k + Q] == seg).astype(F32) for k in range(CONV - 1)]
     for j in range(BLOCKS):
         cols = lanes_of(j)
-        ubuf[8 : 8 + Q, cols] = u_ref[:, cols].astype(F32)
+        ubuf[8 : 8 + Q, cols] = us_ref[:, cols].astype(F32)
         filtered = taps_ref[4:5, cols] + taps_ref[3:4, cols] * ubuf[8 : 8 + Q, cols]
         for k in range(CONV - 1):
             filtered += taps_ref[k : k + 1, cols] * (ubuf[5 + k : 5 + k + Q, cols] * masks[k])
@@ -109,7 +114,7 @@
             act_ref[:, lanes_of(j + 2)] = two_parts(active)[1]
         slope_ref[:, cols] = (gate * (1.0 + filtered - active)).astype(BF16)
 
-    raw = s_ref[...].astype(F32) + heads_ref[0:1, :]
+    raw = dot_nn(us_ref[:, CH:], copies_ref[...]) + heads_ref[0:1, :]
     step = jnp.maximum(raw, 0.0) + jnp.log1p(jnp.exp(-jnp.abs(raw)))
     rows = lax.broadcasted_iota(jnp.int32, (Q, Q), 0)
     lane = lax.broadcasted_iota(jnp.int32, (Q, Q), 1)
@@ -180,8 +185,11 @@
 
 
 def gate_kernel(
-    yloc_ref, aux_ref, drow_ref, sin_ref, reads_ref, rest_ref, z_ref, gain_ref, y_ref, out_ref, gbuf
+    offs_ref, yloc_ref, aux_ref, drow_ref, sin_ref, reads_ref, rest_ref, z_ref, gain_ref, resid_ref,
+    own_ref, *others
 ):
+    pieces, (y_ref, mine_ref, other_ref, next_ref, gbuf, obuf) = others[:-6], others[-6:]
+    i = pl.program_id(0)
     aux = aux_ref[...]
     reads = reads_ref[...]
     reads_both = jnp.concatenate([reads, rest_ref[...]], axis=1)
@@ -198,22 +206,59 @@
         gbuf[:, cols] = gated
         total += gated * gated
     scale = lax.rsqrt(jnp.sum(total, axis=1, keepdims=True) * (1.0 / DI) + EPSILON)
+    rows = pl.ds(pl.multiple_of(i * Q, Q), Q)
     for j in range(PAIRS):
         cols = lanes_of(j)
-        out_ref[:, cols] = (gbuf[:, cols] * scale * gain_ref[0:1, cols]).astype(BF16)
+        obuf[rows, cols] = (gbuf[:, cols] * scale * gain_ref[0:1, cols]).astype(BF16)
+
+    @pl.when(i == pl.num_programs(0) - 1)
+    def _():
+        half, quarter = DI // 2, DI // 4
+        core = offs_ref[7]
+
+        def taken(start, width):
+            return obuf[:, pl.ds(pl.multiple_of(start, quarter), width)]
+
+        for k, start in enumerate((offs_ref[0], half - offs_ref[0])):
+            cols = slice(k * quarter, (k + 1) * quarter)
+            mine_ref[:, cols] = taken(start + core * quarter, quarter)
+            other_ref[:, cols] = taken(start + (1 - core) * quarter, quarter)
+        left = jnp.concatenate(
+            [taken(offs_ref[0], half)] + [taken(offs_ref[k + 1], quarter) for k in range(len(pieces))], axis=1
+        )
+        for j in range(D // 256):
+            cols = pl.ds(j * 256, 256)
+            right = jnp.concatenate([own_ref[0, :, cols]] + [p[:, cols] for p in pieces], axis=0)
+            next_ref[:, cols] = resid_ref[:, cols] + dot_nn(left, right)
 
 
 def gate_back_kernel(
-    dout_ref, y_ref, z_ref, gain_ref, reads_ref, aux_ref, drow_ref,
-    dy_ref, rest_ref, dz_ref, ggrad_ref, zloc_ref, gmsg_ref, dsuf_ref,
-    gbuf, grad_state, suffix, xbuf,
+    offs_ref, grad_ref, y_ref, z_ref, gain_ref, reads_ref, aux_ref, drow_ref, own_ref, *others
 ):
-    @pl.when(pl.program_id(0) == 0)
+    pieces, others = others[:-15], others[-15:]
+    (dy_ref, rest_ref, dzm_ref, dzo_ref, ggrad_ref, zloc_ref, gmsg_ref, dsuf_ref, low_ref,
+     gbuf, grad_state, suffix, xbuf, dout, zbuf) = others
+    i = pl.program_id(0)
+
+    @pl.when(i == 0)
     def _():
+        low_ref[...] = grad_ref[...].astype(BF16)
+        left = low_ref[...]
+        for j in range(DI // 512):
+            right = own_ref[0, 256 * j : 256 * (j + 1), :]
+            cols = pl.ds(pl.multiple_of(offs_ref[0] + 256 * j, 256), 256)
+            dout[:, cols] = dot_nt(left, right)
+        quarter = DI // 4
+        for k, p in enumerate(pieces):
+            for j in range(quarter // 256):
+                right = p[256 * j : 256 * (j + 1), :]
+                cols = pl.ds(pl.multiple_of(offs_ref[k + 1] + 256 * j, 256), 256)
+                dout[:, cols] = dot_nt(left, right)
         ggrad_ref[...] = jnp.zeros_like(ggrad_ref)
         grad_state[...] = jnp.zeros_like(grad_state)
         suffix[...] = jnp.ones_like(suffix)
 
+    rows = pl.ds(pl.multiple_of((pl.num_programs(0) - 1 - i) * Q, Q), Q)
     aux = aux_ref[...]
     low = low_lanes()
     total = jnp.zeros((Q, LANES), F32)
@@ -224,7 +269,7 @@
         gated = y_ref[:, cols] * (z / (1.0 + jnp.exp(-z)))
         gbuf[:, cols] = gated
         total += gated * gated
-        cross += gated * (dout_ref[:, cols] * gain_ref[0:1, cols])
+        cross += gated * (dout[rows, cols] * gain_ref[0:1, cols])
     scale = lax.rsqrt(jnp.sum(total, axis=1, keepdims=True) * (1.0 / DI) + EPSILON)
     pull = jnp.sum(cross, axis=1, keepdims=True) * (scale * scale * scale * (1.0 / DI))
     scale = jnp.broadcast_to(scale, (Q, LANES))
@@ -234,14 +279,17 @@
         z = z_ref[:, cols].astype(F32)
         gate = 1.0 / (1.0 + jnp.exp(-z))
         gated = gbuf[:, cols]
-        scaled = dout_ref[:, cols] * scale
+        scaled = dout[rows, cols] * scale
         ggrad_ref[:, cols] += fold_rows(scaled * gated)
         d_gated = scaled * gain_ref[0:1, cols] - gated * pull
         dy, rest = two_parts(d_gated * (z * gate))
         dy_ref[:, cols] = dy
         rest_ref[:, cols] = rest
-        dz_ref[:, cols] = (d_gated * y_ref[:, cols] * (gate * (1.0 + z * (1.0 - gate)))).astype(BF16)
+        zbuf[:, cols] = (d_gated * y_ref[:, cols] * (gate * (1.0 + z * (1.0 - gate)))).astype(BF16)
         xbuf[:, cols] = (dy.astype(F32) * spread(aux, FROM_START, j, low)).astype(BF16)
+    half, core = DI // 2, offs_ref[7]
+    dzm_ref[...] = zbuf[:, pl.ds(pl.multiple_of(core * half, half), half)]
+    dzo_ref[...] = zbuf[:, pl.ds(pl.multiple_of((1 - core) * half, half), half)]
     zloc_ref[0] = grad_state[...].astype(BF16)
     dsuf_ref[0] = suffix[...]
     reads = reads_ref[...].astype(F32).T.astype(BF16)
@@ -310,10 +358,10 @@
 
 
 def last_kernel(
-    act_ref, aux_ref, slope_ref, u_ref, s_ref, rim_ref, segx_ref, taps_ref, heads_ref, skip_ref,
-    oh_ref, dy_ref, y_ref, dxs_ref, dbc_ref, sout_ref, drow_ref, sin_ref, zloc_ref, dsuf_ref, zdev_ref,
-    du_ref, ds_ref, tail_ref, rimout_ref, tgrad_ref, hgrad_ref,
-    dbuf, qhigh, qrest, vhigh, vrest, ebuf, sums, skips,
+    offs_ref, act_ref, aux_ref, slope_ref, us_ref, rim_ref, segx_ref, taps_ref, heads_ref, skip_ref,
+    oh_ref, copies_ref, dy_ref, y_ref, dxs_ref, dbc_ref, sout_ref, drow_ref, sin_ref, zloc_ref, dsuf_ref, zdev_ref,
+    dum_ref, duo_ref, tail_ref, rimout_ref, tgrad_ref, hgrad_ref,
+    dubuf, dbuf, qhigh, qrest, vhigh, vrest, ebuf, sums, skips,
 ):
     i = pl.program_id(0)
     count = pl.num_programs(0)
@@ -365,11 +413,13 @@
     rows = lax.broadcasted_iota(jnp.int32, (Q, Q), 0)
     lane = lax.broadcasted_iota(jnp.int32, (Q, Q), 1)
     d_decay = dot_full((rows <= lane).astype(F32), d_logs) + d_last
-    raw = s_ref[...].astype(F32) + heads_ref[0:1, :]
+    raw = dot_nn(us_ref[:, CH:], copies_ref[...]) + heads_ref[0:1, :]
     step = jnp.maximum(raw, 0.0) + jnp.log1p(jnp.exp(-jnp.abs(raw)))
     d_step = dot_nn(vhigh[...], hot) + dot_nn(vrest[...], hot) - heads_ref[1:2, :] * d_decay
     d_raw = d_step / (1.0 + jnp.exp(-raw))
-    ds_ref[...] = d_raw.astype(BF16)
+    d_raw = jnp.where(lane < H, d_raw, 0.0).astype(BF16)
+    dum_ref[:, CH // 2 :] = d_raw
+    duo_ref[:, CH // 2 :] = d_raw
     hgrad_ref[0:8, :] += fold_rows(d_raw)
     hgrad_ref[8:16, :] += fold_rows(-(step * d_decay))
 
@@ -383,7 +433,7 @@
     for j in range(BLOCKS):
         cols = lanes_of(j)
         d_filtered = dbuf[0:Q, cols]
-        u = u_ref[:, cols].astype(F32)
+        u = us_ref[:, cols].astype(F32)
         du = taps_ref[3:4, cols] * d_filtered
         tgrad_ref[24:32, cols] += fold_rows(u * d_filtered)
         tgrad_ref[32:40, cols] += fold_rows(d_filtered)
@@ -391,11 +441,15 @@
             later = dbuf[m : m + Q, cols] * masks[m - 1]
             du += taps_ref[3 - m : 4 - m, cols] * later
             tgrad_ref[8 * (3 - m) : 8 * (4 - m), cols] += fold_rows(u * later)
-        du_ref[:, cols] = du.astype(BF16)
+        dubuf[:, cols] = du.astype(BF16)
 
         @pl.when(i == 0)
         def _():
             tail_ref[:, cols] = du[Q - 8 :]
+
+    half, core = CH // 2, offs_ref[7]
+    dum_ref[:, :half] = dubuf[:, pl.ds(pl.multiple_of(core * half, LANES), half)]
+    duo_ref[:, :half] = dubuf[:, pl.ds(pl.multiple_of((1 - core) * half, LANES), half)]
 
     @pl.when(i == count - 1)
     def _():
@@ -413,6 +467,215 @@
             rimout_ref[:, cols] = out.astype(BF16)
 
 
+def expand_first_kernel(offs_ref, resid_ref, gain_ref, own_ref, *others):
+    pieces, (out_ref, normed_ref, left) = others[:-3], others[-3:]
+    half = D // 2
+
+    @pl.when(pl.program_id(0) == 0)
+    def _():
+        x = resid_ref[...]
+        scale = lax.rsqrt(jnp.mean(x * x, axis=1, keepdims=True) + EPSILON)
+        left[...] = (x * scale * gain_ref[...]).astype(BF16)
+        own = left[:, pl.ds(pl.multiple_of(offs_ref[0], half), half)]
+        normed_ref[:, half:] = left[:, pl.ds(pl.multiple_of(half - offs_ref[0], half), half)]
+        normed_ref[:, :half] = own
+
+    out_ref[...] = expand_block(offs_ref, normed_ref, own_ref, pieces).astype(BF16)
+
+
+def expand_block(offs_ref, normed_ref, own_ref, pieces):
+    half = D // 2
+    parts = [normed_ref[:, :half]]
+    for k, p in enumerate(pieces):
+        at = half + lax.rem(offs_ref[k + 1], half)
+        parts.append(normed_ref[:, pl.ds(pl.multiple_of(at, LANES), p.shape[1])])
+    right = jnp.concatenate([own_ref[0]] + [p[...] for p in pieces], axis=1)
+    return dot_nt(jnp.concatenate(parts, axis=1), right)
+
+
+def expand_rest_kernel(offs_ref, normed_ref, own_ref, *others):
+    pieces, out_ref = others[:-1], others[-1]
+    out_ref[...] = expand_block(offs_ref, normed_ref, own_ref, pieces).astype(BF16)
+
+
+def input_back_kernel(
+    count, layer, offs_ref, dzm_ref, dzo_ref, dum_ref, duo_ref, gain_ref, resid_ref, grad_ref, own_ref, *others
+):
+    near, far = others[:count], others[count : 2 * count]
+    (next_ref, ngrad_ref, own, *bufs), (dn, sems) = others[2 * count : -2], others[-2:]
+    near_bufs, far_bufs = bufs[:count], bufs[count:]
+    moves = [(own_ref.at[layer], own)] + list(zip(near, near_bufs))
+    moves += list(zip(far, far_bufs))
+    copies = [pltpu.make_async_copy(src, dst, sems.at[k]) for k, (src, dst) in enumerate(moves)]
+    for copy in copies:
+        copy.start()
+    copies[0].wait()
+    core, zs, us = offs_ref[7], DI // 2, CH // 2
+    parts = [
+        (dzm_ref[...], 0, core * zs), (dzo_ref[...], 0, (1 - core) * zs),
+        (dum_ref[:, :us], DI, core * us), (duo_ref[:, :us], DI, (1 - core) * us), (dum_ref[:, us : us + H], DI + CH, 0),
+    ]
+
+    def down(part, buf, base):
+        left, start, at = part
+        if not isinstance(at, int):
+            at = pl.multiple_of(at, LANES)
+        return dot_nn(left, buf[pl.ds(start - base + at, left.shape[1]), base_cols])
+
+    for j in range(D // 2 // 256):
+        base_cols = slice(j * 256, (j + 1) * 256)
+        cols = pl.ds(pl.multiple_of(offs_ref[0] + j * 256, 256), 256)
+        dn[:, cols] = sum(down(part, own, 0) for part in parts)
+    base_cols = slice(None)
+    for k in range(count):
+        copies[1 + k].wait()
+        copies[1 + count + k].wait()
+        cols = pl.ds(pl.multiple_of(offs_ref[k + 1], LANES), near_bufs[k].shape[1])
+        dn[:, cols] = sum(down(part, far_bufs[k], 0) for part in parts[:2]) + sum(
+            down(part, near_bufs[k], DI) for part in parts[2:]
+        )
+    ngrad = jnp.zeros((8, D), F32)
+    for i in range(dzm_ref.shape[0] // Q):
+        rows = slice(i * Q, (i + 1) * Q)
+        x = resid_ref[rows, :]
+        scale = lax.rsqrt(jnp.mean(x * x, axis=1, keepdims=True) + EPSILON)
+        unit = x * scale
+        down = dn[rows, :]
+        ngrad += fold_rows(down * unit)
+        pulled = down * gain_ref[...]
+        mean = jnp.mean(pulled * unit, axis=1, keepdims=True)
+        next_ref[rows, :] = grad_ref[rows, :] + scale * (pulled - unit * mean)
+    ngrad_ref[...] = ngrad
+
+
+def rows_at(which, size, base=0):
+    return pl.ds(pl.multiple_of(base + which * size, 16), size)
+
+
+def weight_grads(i, count, offs_ref, left, right, away_left, away_right, own_ref, away_ref, near_ref, far_ref):
+    size, width = own_ref.shape
+    first = near_ref.shape[0] // size
+    mine = dot_tn(left, right).astype(BF16)
+    away = dot_tn(away_left, away_right).astype(BF16)
+    own_ref[...] = mine
+    away_ref[...] = away
+
+    @pl.when(i < first)
+    def _():
+        near_ref[rows_at(i, size), :] = away
+
+    start = first + (1 - offs_ref[6]) * (far_ref.shape[0] // size)
+
+    @pl.when((i >= start) & (i < start + far_ref.shape[0] // size))
+    def _():
+        far_ref[rows_at(i - start, size), :width] = mine
+        far_ref[rows_at(i - start, size), width:] = away
+
+
+def both_of(pair, lanes):
+    return jnp.concatenate([ref[:, lanes] for ref in pair], axis=0)
+
+
+def far_grads_kernel(offs_ref, dzm, dzr, nm, nr, om, orr, lm, lr, *outs):
+    i = pl.program_id(0)
+    half, size = D // 2, 256
+
+    @pl.when(i < 4)
+    def _():
+        left = both_of((dzm, dzr), pl.ds(pl.multiple_of(i * size, size), size))
+        weight_grads(
+            i, 8, offs_ref, left, both_of((nm, nr), slice(0, half)), left, both_of((nm, nr), slice(half, D)), *outs
+        )
+
+    @pl.when(i >= 4)
+    def _():
+        at = lax.rem(i, 2) * size
+        right = both_of((lm, lr), pl.ds(pl.multiple_of((i - 4) // 2 * half, half), half))
+        left = both_of((om, orr), pl.ds(pl.multiple_of(at, size), size))
+        away = both_of((om, orr), pl.ds(pl.multiple_of(half + at, size), size))
+        weight_grads(i, 8, offs_ref, left, right, away, right, *outs)
+
+
+def near_grads_kernel(offs_ref, dum, dur, nm, nr, *outs):
+    i = pl.program_id(0)
+    half, size = D // 2, 256
+    left = both_of((dum, dur), pl.ds(pl.multiple_of(i * size, size), size))
+    weight_grads(
+        i, 5, offs_ref, left, both_of((nm, nr), slice(0, half)), left, both_of((nm, nr), slice(half, D)), *outs
+    )
+
+
+def rows_at(which, size, base=0):
+    return pl.ds(pl.multiple_of(base + which * size, LANES), size)
+
+
+def cross_kernel(offs_ref, own_ref, away_ref, near_ref, far_ref, keep_ref, to_rep_ref, to_fsdp_ref):
+    mid, width = near_ref.shape
+    first, second, rep = to_rep_ref.shape[0], to_fsdp_ref.shape[0], offs_ref[6]
+    for ref, which in ((keep_ref, rep), (to_rep_ref, 1 - rep)):
+        rows = rows_at(which, first)
+        total = own_ref[rows, :].astype(F32) + near_ref[rows, :].astype(F32)
+        ref[:first, :] = total.astype(ref.dtype)
+    rows = rows_at(rep, second, mid)
+    keep_ref[first:, :] = own_ref[rows, :].astype(F32) + far_ref[:, :width].astype(F32)
+    to_fsdp_ref[...] = (away_ref[rows, :].astype(F32) + far_ref[:, width:].astype(F32)).astype(BF16)
+
+
+def meet_kernel(keep_ref, a_ref, b_ref, out_ref):
+    size = a_ref.shape[0]
+    out_ref[:size, :] = (keep_ref[:size, :] + a_ref[...].astype(F32)).astype(BF16)
+    out_ref[size:, :] = (keep_ref[size:, :] + b_ref[...].astype(F32)).astype(BF16)
+
+
+def take_kernel(lanes, offs_ref, src_ref, out_ref):
+    rows, width = out_ref.shape
+    core = offs_ref[7]
+    if lanes:
+        out_ref[...] = src_ref[0, :, pl.ds(pl.multiple_of(core * width, width), width)]
+    else:
+        out_ref[...] = src_ref[0, rows_at(core, rows), :]
+
+
+def reduce_kernel(parts_ref, out_ref):
+    count, rows = parts_ref.shape[0], parts_ref.shape[1]
+    total = parts_ref[0].astype(F32)
+    for k in range(1, count):
+        total += parts_ref[k].astype(F32)
+    total = total.astype(BF16)
+    for k in range(count):
+        out_ref[k * rows : (k + 1) * rows, :] = total
+
+
+def final_kernel(layer, count, offs_ref, *others):
+    far, near = others[:count], others[count : 2 * count]
+    expand_ref, reduce_ref, zbuf, ubuf, sbuf, rbuf, sems = others[-7:]
+    core, rep, zs, us, rs = offs_ref[7], offs_ref[6], DI // 2, CH // 2, DI // 4
+    copies = []
+
+    def put(src, ref, start, size):
+        copy = pltpu.make_async_copy(src, ref.at[layer, pl.ds(start, size)], sems.at[len(copies)])
+        copy.start()
+        copies.append(copy)
+
+    for k in range(2):
+        which = core if k == 0 else 1 - core
+        for h in range(2):
+            at = rep if h == 0 else 1 - rep
+            for buf, part, mid in ((zbuf, far[2 * k + h], FAR_MID), (ubuf, near[2 * k + h], NEAR_MID)):
+                size = mid // 2
+                buf[k, rows_at(at, size), :] = part[:size, :].astype(F32)
+                buf[k, rows_at(at, part.shape[0] - size, mid), :] = part[size:, :].astype(F32)
+        for q in range(2):
+            rbuf[k, :, 512 * q : 512 * (q + 1)] = zbuf[k, zs + rs * q : zs + rs * (q + 1), :]
+        put(rbuf.at[k], reduce_ref, pl.multiple_of(which * rs, LANES), rs)
+        put(zbuf.at[k, pl.ds(0, zs)], expand_ref, pl.multiple_of(which * zs, LANES), zs)
+        put(ubuf.at[k, pl.ds(0, us)], expand_ref, pl.multiple_of(DI + which * us, LANES), us)
+    sbuf[...] = ubuf[0, us : us + H, :]
+    put(sbuf, expand_ref, DI + CH, H)
+    for copy in copies:
+        copy.wait()
+
+
 def whole(shape):
     return pl.BlockSpec(shape, lambda i: (0,) * len(shape))
 
@@ -427,47 +690,175 @@
     return jax.ShapeDtypeStruct(shape, dtype)
 
 
-def call(kernel, grid, in_specs, out_specs, out_shape, scratch, flops, moved, name):
-    return pl.pallas_call(
-        kernel,
+SCALARS = pl.BlockSpec(memory_space=pltpu.SMEM)
+ANYWHERE = pl.BlockSpec(memory_space=pl.ANY)
+
+
+COST = {
+    "expand_first": 8, "ssd_front": 13, "expand_rest": 6, "ssd_within": 11, "ssd_gate": 13, "gate_back": 15,
+    "within_back": 17, "ssd_last": 24, "input_back": 16, "far_grads": 12, "near_grads": 6, "take": 1, "cross": 4, "meet": 3, "reduce_parts": 2,
+    "final_grads": 8,
+}
+
+
+def call(kernel, grid, in_specs, out_specs, out_shape, scratch, name, deps=(), aliases=None):
+    n, m = len(in_specs), len(deps)
+
+    def body(*refs):
+        kernel(*refs[:n], *refs[n + m :])
+
+    run = pl.pallas_call(
+        body,
         grid=(grid,),
-        in_specs=in_specs,
+        in_specs=list(in_specs) + [ANYWHERE] * m,
         out_specs=out_specs,
         out_shape=out_shape,
         scratch_shapes=scratch,
+        input_output_aliases=aliases or {},
         compiler_params=pltpu.CompilerParams(
             dimension_semantics=("arbitrary",), vmem_limit_bytes=VMEM_LIMIT
         ),
-        cost_estimate=pl.CostEstimate(flops=flops, bytes_accessed=moved, transcendentals=0),
+        cost_estimate=pl.CostEstimate(
+            flops=int(COST[name] * 1.1e9), bytes_accessed=1000, transcendentals=0
+        ),
         name=name,
     )
-
-
-MIB = 1 << 20
-
-
-def ssd_front(u, s4, rim, segx, taps, heads, oht):
-    T = u.shape[0]
+    return lambda *args: run(*args, *deps)
+
+
+def expand_first(offs, resid, gain, own, pieces, layer):
+    T = resid.shape[0]
+    first = DI // WIDE
+    return call(
+        expand_first_kernel, -(-US // WIDE),
+        [SCALARS, whole((T, D)), whole((1, D)),
+         pl.BlockSpec((1, WIDE, D // 2), lambda i: (layer, first + i, 0))]
+        + [pl.BlockSpec((WIDE, p.shape[1]), lambda i: (i, 0)) for p in pieces],
+        [pl.BlockSpec((T, WIDE), lambda i: (0, i)), whole((T, D))],
+        [struct((T, US), BF16), struct((T, D), BF16)],
+        [pltpu.VMEM((T, D), BF16)],
+        "expand_first",
+    )(offs, resid, gain, own, *pieces)
+
+
+def expand_rest(offs, normed, own, pieces, layer, deps=()):
+    T = normed.shape[0]
+    return call(
+        expand_rest_kernel, DI // WIDE,
+        [SCALARS, whole((T, D)), pl.BlockSpec((1, WIDE, D // 2), lambda i: (layer, i, 0))]
+        + [pl.BlockSpec((WIDE, p.shape[1]), lambda i: (i, 0)) for p in pieces],
+        pl.BlockSpec((T, WIDE), lambda i: (0, i)),
+        struct((T, DI), BF16), [],
+        "expand_rest", deps,
+    )(offs, normed, own, *pieces)
+
+
+def input_back(offs, dzm, dzo, dum, duo, gain, resid, grad, own, near, far, layer, deps=()):
+    T = dzm.shape[0]
+    count = len(near)
+    return call(
+        functools.partial(input_back_kernel, count, layer), 1,
+        [SCALARS] + [whole(a.shape) for a in (dzm, dzo, dum, duo)]
+        + [whole((1, D)), whole((T, D)), whole((T, D)), ANYWHERE] + [ANYWHERE] * (2 * count),
+        [whole((T, D)), whole((8, D))],
+        [struct((T, D), F32), struct((8, D), F32)],
+        [pltpu.VMEM((E, D // 2), BF16)] + [pltpu.VMEM((US, p.shape[1]), BF16) for p in near]
+        + [pltpu.VMEM((DI, p.shape[1]), BF16) for p in far]
+        + [pltpu.VMEM((T, D), F32), pltpu.SemaphoreType.DMA((1 + 2 * count,))],
+        "input_back", deps,
+    )(offs, dzm, dzo, dum, duo, gain, resid, grad, own, *near, *far)
+
+
+def final_grads(offs, far, near, layer, held, deps=()):
+    n = 1 + len(far) + len(near)
+    return call(
+        functools.partial(final_kernel, layer, len(far)), 1,
+        [SCALARS] + [whole(p.shape) for p in (*far, *near)] + [ANYWHERE] * len(held),
+        [ANYWHERE, ANYWHERE],
+        [struct((LAYERS, E, D // 2), F32), struct((LAYERS, DI // 2, D), F32)],
+        [pltpu.VMEM((2, DI, D // 2), F32), pltpu.VMEM((2, HALF, D // 2), F32),
+         pltpu.VMEM((H, D // 2), F32), pltpu.VMEM((2, DI // 4, D), F32), pltpu.SemaphoreType.DMA((7,))],
+        "final_grads", deps,
+        aliases={n + k: k for k in range(len(held))},
+    )(offs, *far, *near, *held)
+
+
+class Sum:
+    def __init__(self, offs, name, kernel, args, mid, deps=()):
+        rows, width, size = (DI if name == "far_grads" else HALF), D // 2, 256
+        block = by_rows((size, width))
+        shapes = [(rows, width), (rows, width), (mid, width), ((rows - mid) // 2, 2 * width)]
+        self.offs = offs
+        self.own, self.away, near, far = call(
+            kernel, rows // size, [SCALARS] + [whole(a.shape) for a in args],
+            [block, block] + [whole(shape) for shape in shapes[2:]], [struct(shape, BF16) for shape in shapes],
+            [], name, deps,
+        )(offs, *args)
+        self.near, self.far = swap(near, "fsdp"), swap(far, "rep")
+
+    def cross(self, deps=()):
+        mid, width = self.near.shape
+        first, second = mid // 2, self.far.shape[0]
+        shapes = [(first + second, width), (first, width), (second, width)]
+        args = (self.own, self.away, self.near, self.far)
+        self.keep, to_rep, to_fsdp = call(
+            cross_kernel, 1, [SCALARS] + [whole(a.shape) for a in args], [whole(shape) for shape in shapes],
+            [struct(shapes[0], F32)] + [struct(shape, BF16) for shape in shapes[1:]], [], "cross", deps,
+        )(self.offs, *args)
+        self.a, self.b = swap(to_rep, "rep"), swap(to_fsdp, "fsdp")
+        return (to_rep,)
+
+    def meet(self, deps=()):
+        args = (self.keep, self.a, self.b)
+        total = call(
+            meet_kernel, 1, [whole(a.shape) for a in args], whole(self.keep.shape), struct(self.keep.shape, BF16),
+            [], "meet", deps,
+        )(*args)
+        self.parts = lax.all_to_all(total, "zz", 0, 0, tiled=True)
+        return (total,)
+
+    def reduce(self, deps=()):
+        rows, width = self.parts.shape
+        count = lax.axis_size("zz")
+        copies = reduce_parts(self.parts.reshape(count, rows // count, width), deps)
+        self.mine = lax.all_to_all(copies, "zz", 0, 0, tiled=True)
+        return (copies,)
+
+    def spread(self, other=None):
+        parts = [self.mine, swap(self.mine, "rep") if other is None else other]
+        return parts + [swap(p, "core") for p in parts]
+
+
+def reduce_parts(parts, deps):
+    count, rows, width = parts.shape
+    return call(
+        reduce_kernel, 1, [whole(parts.shape)], whole((count * rows, width)),
+        struct((count * rows, width), BF16), [], "reduce_parts", deps,
+    )(parts)
+
+
+def ssd_front(us, rim, segx, taps, heads, oht, copies, deps=()):
+    T = us.shape[0]
     nc = T // Q
     return call(
         front_kernel, nc,
-        [by_rows((Q, CH)), by_rows((Q, LANES)), whole((8, CH)), whole(segx.shape), whole(taps.shape),
-         whole(heads.shape), whole(oht.shape)],
+        [by_rows((Q, US)), whole((8, CH)), whole(segx.shape), whole(taps.shape),
+         whole(heads.shape), whole(oht.shape), whole(copies.shape)],
         [by_rows((Q, ACT)), by_rows((Q, CH)), by_rows((Q, LANES)), by_rows((1, H, Q)),
          by_rows((1, 8, DI)), by_rows((1, N, DI)), whole((N + 8, DI))],
         [struct((T, ACT), BF16), struct((T, CH), BF16), struct((T, LANES), F32), struct((nc, H, Q), F32),
          struct((nc, 8, DI), F32), struct((nc, N, DI), F32), struct((N + 8, DI), F32)],
         [pltpu.VMEM((Q + 8, CH), F32), pltpu.VMEM((N, DI), F32), pltpu.VMEM((8, LANES), F32),
          pltpu.VMEM((Q, DI), BF16)],
-        2_000_000_000, 12 * MIB, "ssd_front",
-    )(u, s4, rim, segx, taps, heads, oht)
+        "ssd_front", deps,
+    )(us, rim, segx, taps, heads, oht, copies)
 
 
 def previous(shape):
     return pl.BlockSpec(shape, lambda i: (jnp.maximum(i - 1, 0), 0, 0))
 
 
-def ssd_within(act, aux, lt, segx, segr, sout, skip):
+def ssd_within(act, aux, lt, segx, segr, sout, skip, deps=()):
     T = act.shape[0]
     nc = T // Q
     return call(
@@ -475,45 +866,48 @@
         [by_rows((Q, ACT)), by_rows((Q, LANES)), by_rows((1, H, Q)), whole(segx.shape),
          by_rows((1, 8, LANES)), previous((1, N, DI)), whole(skip.shape)],
         by_rows((Q, DI)), struct((T, DI), F32), [],
-        4_000_000_000, 10 * MIB, "ssd_within",
+        "ssd_within", deps,
     )(act, aux, lt, segx, segr, sout, skip)
 
 
-def ssd_gate(yloc, aux, drow, s_in, act, z, gain):
+def ssd_gate(offs, yloc, aux, drow, s_in, act, z, gain, resid, own, pieces, layer):
     T = yloc.shape[0]
     nc = T // Q
     reads = pl.BlockSpec((Q, N), lambda i: (i, READS.start // N))
     rest = pl.BlockSpec((Q, N), lambda i: (i, READS_REST.start // N))
     return call(
         gate_kernel, nc,
-        [by_rows((Q, DI)), by_rows((Q, LANES)), by_rows((1, 8, DI)), whole((N, DI)), reads,
-         rest, by_rows((Q, DI)), whole(gain.shape)],
-        [by_rows((Q, DI)), by_rows((Q, DI))],
-        [struct((T, DI), F32), struct((T, DI), BF16)],
-        [pltpu.VMEM((Q, DI), F32)],
-        2_000_000_000, 14 * MIB, "ssd_gate",
-    )(yloc, aux, drow, s_in, act, act, z, gain)
-
-
-def gate_back(dout, y, z, gain, act, aux, drow):
+        [SCALARS, by_rows((Q, DI)), by_rows((Q, LANES)), by_rows((1, 8, DI)), whole((N, DI)), reads,
+         rest, by_rows((Q, DI)), whole(gain.shape), whole((T, D)),
+         pl.BlockSpec((1, DI // 2, D), lambda i: (layer, 0, 0))] + [whole(p.shape) for p in pieces],
+        [by_rows((Q, DI)), whole((T, DI // 2)), whole((T, DI // 2)), whole((T, D))],
+        [struct((T, DI), F32), struct((T, DI // 2), BF16), struct((T, DI // 2), BF16), struct((T, D), F32)],
+        [pltpu.VMEM((Q, DI), F32), pltpu.VMEM((T, DI), BF16)],
+        "ssd_gate",
+    )(offs, yloc, aux, drow, s_in, act, act, z, gain, resid, own, *pieces)
+
+
+def gate_back(offs, grad, y, z, gain, act, aux, drow, own, pieces, layer, deps=()):
     T = y.shape[0]
     nc = T // Q
     reads = pl.BlockSpec((Q, N), lambda i: (nc - 1 - i, READS.start // N))
     return call(
         gate_back_kernel, nc,
-        [by_rows((Q, DI), nc), by_rows((Q, DI), nc), by_rows((Q, DI), nc), whole(gain.shape), reads,
-         by_rows((Q, LANES), nc), by_rows((1, 8, DI), nc)],
-        [by_rows((Q, DI), nc)] * 3 + [whole((8, DI)), by_rows((1, N, DI), nc),
-         whole((N, DI)), by_rows((1, 8, DI), nc)],
-        [struct((T, DI), BF16)] * 3 + [struct((8, DI), F32), struct((nc, N, DI), BF16),
-         struct((N, DI), BF16), struct((nc, 8, DI), F32)],
+        [SCALARS, whole((T, D)), by_rows((Q, DI), nc), by_rows((Q, DI), nc), whole(gain.shape), reads,
+         by_rows((Q, LANES), nc), by_rows((1, 8, DI), nc),
+         pl.BlockSpec((1, DI // 2, D), lambda i: (layer, 0, 0))] + [whole(p.shape) for p in pieces],
+        [by_rows((Q, DI), nc)] * 2 + [by_rows((Q, DI // 2), nc)] * 2 + [whole((8, DI)), by_rows((1, N, DI), nc),
+         whole((N, DI)), by_rows((1, 8, DI), nc), whole((T, D))],
+        [struct((T, DI), BF16)] * 2 + [struct((T, DI // 2), BF16)] * 2
+        + [struct((8, DI), F32), struct((nc, N, DI), BF16),
+         struct((N, DI), BF16), struct((nc, 8, DI), F32), struct((T, D), BF16)],
         [pltpu.VMEM((Q, DI), F32), pltpu.VMEM((N, DI), F32), pltpu.VMEM((8, DI), F32),
-         pltpu.VMEM((Q, DI), BF16)],
-        3_000_000_000, 18 * MIB, "gate_back",
-    )(dout, y, z, gain, act, aux, drow)
-
-
-def within_back(act, aux, lt, segx, segr, dy, rest, sout, drow, s_in, zloc):
+         pltpu.VMEM((Q, DI), BF16), pltpu.VMEM((T, DI), F32), pltpu.VMEM((Q, DI), BF16)],
+        "gate_back", deps,
+    )(offs, grad, y, z, gain, act, aux, drow, own, *pieces)
+
+
+def within_back(act, aux, lt, segx, segr, dy, rest, sout, drow, s_in, zloc, deps=()):
     T = act.shape[0]
     nc = T // Q
     return call(
@@ -524,31 +918,30 @@
         [by_rows((Q, DI)), by_rows((Q, 2 * N))],
         [struct((T, DI), F32), struct((T, 2 * N), F32)],
         [pltpu.VMEM((Q, DI), BF16)] * 5,
-        8_000_000_000, 16 * MIB, "within_back",
+        "within_back", deps,
     )(act, aux, lt, segx, segr, dy, rest, sout, drow, s_in, zloc)
 
 
-def ssd_last(act, aux, slope, u, s4, rim, segx, taps, heads, skip, oh, dy, y, dxs, dbc, sout, drow, s_in,
-             zloc, dsuf, zdev):
+def ssd_last(offs, act, aux, slope, us, rim, segx, taps, heads, skip, oh, copies, dy, y, dxs, dbc, sout, drow, s_in,
+             zloc, dsuf, zdev, deps=()):
     T = act.shape[0]
     nc = T // Q
     return call(
         last_kernel, nc,
-        [by_rows((Q, ACT), nc), by_rows((Q, LANES), nc), by_rows((Q, CH), nc), by_rows((Q, CH), nc),
-         by_rows((Q, LANES), nc), whole((8, CH)), whole(segx.shape), whole(taps.shape),
-         whole(heads.shape), whole(skip.shape), whole(oh.shape), by_rows((Q, DI), nc),
+        [SCALARS, by_rows((Q, ACT), nc), by_rows((Q, LANES), nc), by_rows((Q, CH), nc), by_rows((Q, US), nc),
+         whole((8, CH)), whole(segx.shape), whole(taps.shape),
+         whole(heads.shape), whole(skip.shape), whole(oh.shape), whole(copies.shape), by_rows((Q, DI), nc),
          by_rows((Q, DI), nc), by_rows((Q, DI), nc), by_rows((Q, 2 * N), nc), by_rows((1, N, DI), nc),
          by_rows((1, 8, DI), nc), whole((N, DI)), by_rows((1, N, DI), nc), by_rows((1, 8, DI), nc),
          whole((N, DI))],
-        [by_rows((Q, CH), nc), by_rows((Q, LANES), nc), whole((8, CH)), whole((8, CH)), whole((40, CH)),
+        [by_rows((Q, HALF), nc)] * 2 + [whole((8, CH)), whole((8, CH)), whole((40, CH)),
          whole((24, LANES))],
-        [struct((T, CH), BF16), struct((T, LANES), BF16), struct((8, CH), F32), struct((8, CH), BF16),
+        [struct((T, HALF), BF16)] * 2 + [struct((8, CH), F32), struct((8, CH), BF16),
          struct((40, CH), F32), struct((24, LANES), F32)],
-        [pltpu.VMEM((Q + 8, CH), F32), pltpu.VMEM((Q, DI), BF16), pltpu.VMEM((Q, DI), BF16),
-         pltpu.VMEM((Q, DI), BF16), pltpu.VMEM((Q, DI), BF16), pltpu.VMEM((Q, DI), BF16),
-         pltpu.VMEM((8, DI), F32), pltpu.VMEM((8, DI), F32)],
-        6_000_000_000, 24 * MIB, "ssd_last",
-    )(act, aux, slope, u, s4, rim, segx, taps, heads, skip, oh, dy, y, dxs, dbc, sout, drow, s_in,
+        [pltpu.VMEM((Q, CH), BF16), pltpu.VMEM((Q + 8, CH), F32)] + [pltpu.VMEM((Q, DI), BF16)] * 5
+        + [pltpu.VMEM((8, DI), F32), pltpu.VMEM((8, DI), F32)],
+        "ssd_last", deps,
+    )(offs, act, aux, slope, us, rim, segx, taps, heads, skip, oh, copies, dy, y, dxs, dbc, sout, drow, s_in,
       zloc, dsuf, zdev)
 
 
@@ -614,13 +1007,9 @@
     return value
 
 
-def fetch_peer(own, core, earlier=None):
-    rows = own.shape[0] // 2
-    part = lax.dynamic_slice_in_dim(own, core * rows, rows, 0)
-    if earlier is not None:
-        part = after(part, earlier)
+def fetch(part):
     got = swap(part, "fsdp")
-    return ordered(core, got, swap(got, "core"), 0), got
+    return got, swap(got, "core")
 
 
 def carry_forward(core, msg):
@@ -683,27 +1072,11 @@
     return out
 
 
-def sum_shards(partial, fsdp):
-    mine, other = halves(partial, fsdp, 0)
-    total = mine + swap(other.astype(BF16), "fsdp").astype(F32)
-    steps = levels()
-    for axis, bit in steps:
-        which = (lax.axis_index(axis) // bit) % 2
-        mine, other = halves(total, which, 0)
-        total = mine + flip(other.astype(BF16), axis, bit).astype(F32)
-    total = total.astype(BF16)
-    for axis, bit in reversed(steps):
-        which = (lax.axis_index(axis) // bit) % 2
-        total = ordered(which, total, flip(total, axis, bit), 0)
-    return total
-
-
-def sum_small(packed):
-    packed = packed + swap(packed, "core")
-    packed = packed + swap(packed, "fsdp")
-    for axis, bit in levels():
-        packed = packed + flip(packed, axis, bit)
-    return packed
+def following(value, *others):
+    for other in others:
+        mark = other[0, 0]
+        value = jnp.where(mark != mark, jnp.zeros_like(value), value)
+    return value
 
 
 def local(
@@ -722,6 +1095,7 @@
 ):
     rows = tokens.shape[1]
     T = 2 * rows
+    rep = lax.axis_index("rep")
     fsdp = lax.axis_index("fsdp")
     core = lax.axis_index("core")
     me = lax.axis_index(CTX)
@@ -764,92 +1138,154 @@
         == lax.broadcasted_iota(jnp.int32, (LANES, DI), 0)
     ).astype(BF16)
 
+    copies = (
+        lax.broadcasted_iota(jnp.int32, (H, LANES), 0) == lax.broadcasted_iota(jnp.int32, (H, LANES), 1) % H
+    ).astype(BF16)
+
     seq = (me >= half).astype(jnp.int32)
     padded = jnp.pad(segments, ((0, 0), (8, 8)), constant_values=-1)
     seg_line = lax.dynamic_slice(padded, (seq, (me % half) * T), (1, T + 16))[0].astype(F32)
     segx = jnp.broadcast_to(seg_line[:, None], (T + 16, LANES))
     segr = jnp.broadcast_to(seg_line[8 : 8 + T].reshape(T // Q, 1, Q), (T // Q, 8, Q))
 
-    weights = []
-    earlier = None
+    expand_t = jnp.swapaxes(expand_weight, 1, 2)
+    quarter = D // 4
+
+    def offsets(size):
+        start, away = fsdp * size, (1 - fsdp) * size
+        zero = jnp.zeros_like(core)
+        return jnp.stack(
+            [start, away + core * (size // 2), away + (1 - core) * (size // 2), zero, zero, zero, rep, core]
+        ).astype(jnp.int32)
+
+    offs, wide_offs = offsets(D // 2), offsets(DI // 2)
+
+    def take_lanes(layer, start, rows, deps):
+        size = 512
+        return call(
+            functools.partial(take_kernel, True), -(-rows // size),
+            [SCALARS, pl.BlockSpec((1, size, D // 2), lambda i: (layer, start // size + i, 0))],
+            by_rows((size, quarter)), struct((rows, quarter), BF16), [], "take", deps,
+        )(offs, expand_t)
+
+    def take_rows(layer, deps):
+        return call(
+            functools.partial(take_kernel, False), 1,
+            [SCALARS, pl.BlockSpec((1, DI // 2, D), lambda i: (layer, 0, 0))],
+            whole((DI // 4, D)), struct((DI // 4, D), BF16), [], "take", deps,
+        )(offs, reduce_weight)
+
+    first_taken = take_lanes(0, DI, US, ())
+
+    def fetch_layer(layer, after_near=(), after_far=(), after_rows=()):
+        near = first_taken if layer == 0 else take_lanes(layer, DI, US, after_near)
+        far = take_lanes(layer, 0, DI, after_far + (near,))
+        rows_of = take_rows(layer, after_rows + (far,))
+        return fetch(near), fetch(far), fetch(rows_of)
+
+    weights = [fetch_layer(0)]
+
+    resid = gather_tokens(following(tokens, first_taken)).astype(F32)
+    grad = gather_tokens(cotangent).astype(F32)
+    saved, out_both = [], ()
     for layer in range(LAYERS):
-        expand_peer, earlier = fetch_peer(expand_weight[layer], core, earlier)
-        reduce_peer, earlier = fetch_peer(reduce_weight[layer], core, earlier)
-        weights.append(
-            (ordered(fsdp, expand_weight[layer], expand_peer, 0),
-             ordered(fsdp, reduce_weight[layer], reduce_peer, 0))
-        )
-
-    resid = gather_tokens(tokens).astype(F32)
-    saved = []
-    for layer in range(LAYERS):
-        expand, reduce = weights[layer]
-        normed = (resid * rms_parts(resid) * norm_all[layer]).astype(BF16)
-        mixed = dot_nn(normed, expand).astype(BF16)
-        z, u, s = mixed[:, :DI], mixed[:, DI : DI + CH], mixed[:, DI + CH :]
-        s4 = jnp.tile(s, (1, LANES // H))
-        rim = next_piece(u[T - 8 :])
+        near, far, rows_of = weights[layer]
+        us, normed = expand_first(offs, resid, norm_all[layer][None], expand_t, near, layer)
+        rim = us[T - 8 :, :CH]
+        rim = next_piece(following(rim, far[0]) if layer else rim)
         taps, heads = taps_all[layer], heads_all[layer]
         skip = skip_rows[layer][None]
-        act, slope, aux, lt, drow, sout, msg = ssd_front(u, s4, rim, segx, taps, heads, hot_t)
-        s_in, decays = carry_forward(core, msg)
-        yloc = ssd_within(act, aux, lt, segx, segr, sout, skip)
+        act, slope, aux, lt, drow, sout, msg = ssd_front(us, rim, segx, taps, heads, hot_t, copies, out_both[1:])
+        z = expand_rest(offs, normed, expand_t, far, layer, (act,))
+        s_in, decays = carry_forward(core, following(msg, rows_of[0]) if layer else msg)
+        normed_both = normed, swap(normed, "core")
+        within_deps = (normed_both[1], grad) if layer else normed_both[1:]
+        yloc = ssd_within(act, aux, lt, segx, segr, sout, skip, within_deps)
+        if layer + 1 < LAYERS:
+            weights.append(fetch_layer(layer + 1, (us,), (act,), (yloc,)))
         gain = gate_all[layer][None]
-        y, out_in = ssd_gate(yloc, aux, drow, s_in, act, z, gain)
-        normed_both = jnp.concatenate([normed, swap(normed, "core")], axis=0)
-        out_both = jnp.concatenate([out_in, swap(out_in, "core")], axis=0)
-        saved.append((resid, normed_both, z, u, s4, rim, act, slope, aux, lt, drow, sout, s_in, decays, y, out_both))
-        resid = resid + dot_nn(out_in, reduce)
+        y, out_mine, out_other, resid_next = ssd_gate(
+            wide_offs, yloc, aux, drow, s_in, act, z, gain, resid, reduce_weight, rows_of, layer
+        )
+        out_both = out_mine, swap(out_other, "core")
+        saved.append((resid, normed_both, z, us, rim, act, slope, aux, lt, drow, sout, s_in, decays, y, out_both))
+        resid = resid_next
     layer_out = scatter_tokens(resid.astype(BF16))
 
-    grad = gather_tokens(cotangent).astype(F32)
-    expand_z, expand_u, reduce_g, small = [None] * 2, [None] * 2, [None] * 2, [None] * 2
+    small = [None] * LAYERS
+    far_sums, near_sums, pending = {}, {}, ()
+
     for layer in reversed(range(LAYERS)):
-        expand, reduce = weights[layer]
-        (resid_in, normed_both, z, u, s4, rim, act, slope, aux, lt, drow, sout, s_in, decays, y, out_both) = saved[layer]
+        near, far, rows_of = weights[layer]
+        (resid_in, normed_both, z, us, rim, act, slope, aux, lt, drow, sout, s_in, decays, y, out_both) = saved[layer]
         taps, heads = taps_all[layer], heads_all[layer]
         skip = skip_rows[layer][None]
         gain = gate_all[layer][None]
-        grad_low = grad.astype(BF16)
-        dout = dot_nt(grad_low, reduce)
-        low_mine, low_other = halves(grad_low, core, 1)
-        low_both = jnp.concatenate([low_mine, swap(low_other, "core")], axis=0)
-        reduce_g[layer] = sum_shards(dot_tn(out_both, low_both), fsdp)
-        dy, dy_rest, dz, ggrad, zloc, gmsg, dsuf = gate_back(dout, y, z, gain, act, aux, drow)
-        zdev = carry_backward(core, gmsg, decays)
-        dz_mine, dz_other = halves(dz, core, 1)
-        dz_both = jnp.concatenate([dz_mine, swap(dz_other, "core")], axis=0)
-        expand_z[layer] = sum_shards(dot_tn(normed_both, dz_both), fsdp)
-        dxs, dbc = within_back(act, aux, lt, segx, segr, dy, dy_rest, sout, drow, s_in, zloc)
-        du, ds, tail, rimout, tgrad, hgrad = ssd_last(
-            act, aux, slope, u, s4, rim, segx, taps, heads, skip, hot, dy, y, dxs, dbc, sout, drow, s_in,
-            zloc, dsuf, zdev
+        first = layer == 0
+        dy, dy_rest, dzm, dzo, ggrad, zloc, gmsg, dsuf, grad_low = gate_back(
+            wide_offs, grad, y, z, gain, act, aux, drow, reduce_weight, rows_of, layer, pending
         )
+        arrived = near_sums[1].cross((gmsg,)) if first else ()
+        zdev = carry_backward(core, following(gmsg, *arrived), decays)
+        far_args = (dzm, swap(dzo, "core"), *normed_both, *out_both, grad_low, swap(grad_low, "core"))
+        far_sums[layer] = Sum(offs, "far_grads", far_grads_kernel, far_args, FAR_MID, arrived)
+        before = (far_sums[layer].own,)
+        if first:
+            before += near_sums[1].meet((zdev,) + before)
+        dxs, dbc = within_back(act, aux, lt, segx, segr, dy, dy_rest, sout, drow, s_in, zloc, before)
+        before = far_sums[layer].cross((dxs,))
+        if first:
+            before += (far_sums[1].mine,) + near_sums[1].reduce((dxs,))
+        dum, duo, tail, rimout, tgrad, hgrad = ssd_last(
+            offs, act, aux, slope, us, rim, segx, taps, heads, skip, hot, copies, dy, y, dxs, dbc, sout, drow, s_in,
+            zloc, dsuf, zdev, before
+        )
+        token = far_sums[layer].meet((dum,)) + ((near_sums[1].mine,) if first else (layer_out[0],))
+        rimout = following(rimout, *token)
         tail = (tail + next_piece(rimout, True).astype(F32)).astype(BF16)
-        du = lax.dynamic_update_slice(du, tail, (T - 8, 0))
-        ds = ds[:, :H]
-        du_mine, du_other = halves(du, core, 1)
-        us_both = jnp.concatenate(
-            [jnp.concatenate([du_mine, ds], axis=1),
-             swap(jnp.concatenate([du_other, ds], axis=1), "core")], axis=0
+        tail_mine, tail_other = halves(tail, core, 1)
+        dum = lax.dynamic_update_slice(dum, tail_mine, (T - 8, 0))
+        duo = lax.dynamic_update_slice(duo, tail_other, (T - 8, 0))
+        near_args = (dum, swap(duo, "core"), *normed_both)
+        grad, ngrad = input_back(
+            offs, dzm, dzo, dum, duo, norm_all[layer][None], resid_in, grad, expand_t, near, far, layer, token
         )
-        expand_u[layer] = sum_shards(dot_tn(normed_both, us_both), fsdp)
-        d_mixed = jnp.concatenate([dz, du, ds], axis=1)
-        d_normed = dot_nt(d_mixed, expand)
-        scale = rms_parts(resid_in)
-        unit = resid_in * scale
-        pulled = d_normed * norm_all[layer]
-        grad = grad + scale * (pulled - unit * jnp.mean(pulled * unit, axis=-1, keepdims=True))
-        norm_grad = jnp.sum(d_normed * unit, axis=0)
+        near_sums[layer] = Sum(offs, "near_grads", near_grads_kernel, near_args, NEAR_MID, (grad,))
+        if not first:
+            pending = far_sums[1].reduce((near_sums[1].own,))
         tgrad = jnp.sum(tgrad.reshape(5, 8, CH), axis=1).reshape(-1)
         hgrad = jnp.sum(hgrad.reshape(3, 8, LANES), axis=1)[:, :H].reshape(-1)
-        small[layer] = jnp.concatenate([tgrad, jnp.sum(ggrad, axis=0), norm_grad, hgrad])
-
-    token_grads = scatter_tokens(grad.astype(BF16))
+        small[layer] = jnp.concatenate([tgrad, jnp.sum(ggrad, axis=0), jnp.sum(ngrad, axis=0), hgrad])
+
     size = small[0].shape[0]
     padded_size = -(-size // 1024) * 1024
-    packed = jnp.pad(jnp.stack(small), ((0, 0), (0, padded_size - size)))
-    packed = sum_small(packed.reshape(-1, LANES)).reshape(LAYERS, padded_size)
+    packed = jnp.pad(jnp.stack(small), ((0, 0), (0, padded_size - size))).reshape(-1, LANES)
+    hops = [("core", 1), ("fsdp", 1)] + levels()
+
+    def hop(packed):
+        axis, bit = hops.pop(0)
+        return packed + flip(packed, axis, bit)
+
+    far_other = swap(far_sums[1].mine, "rep")
+    token = far_sums[0].reduce((near_sums[0].own, far_other))
+    packed = hop(packed)
+    token = near_sums[0].cross(token + (packed,))
+    near_other = swap(near_sums[1].mine, "rep")
+    packed = hop(packed)
+    token = near_sums[0].meet(token + (far_sums[0].mine, near_other, packed))
+    mid = far_sums[0].mine.shape[0] // 2
+    other_a = swap(far_sums[0].mine[:mid], "rep")
+    grads = final_grads(offs, far_sums[1].spread(far_other), near_sums[1].spread(near_other), 1, (), token)
+    packed = hop(packed)
+    token = near_sums[0].reduce(token + (other_a, packed, grads[0]))
+    other_b = swap(far_sums[0].mine[mid:], "rep")
+    packed = hop(packed)
+    token_grads = scatter_tokens(following(grad.astype(BF16), near_sums[0].mine))
+    far_first = far_sums[0].spread(jnp.concatenate([other_a, other_b], axis=0))
+    while hops:
+        packed = hop(packed)
+    grads = final_grads(offs, far_first, near_sums[0].spread(), 0, grads)
+    packed = packed.reshape(LAYERS, padded_size)
 
     def own_half(x):
         return halves(x, fsdp, x.ndim - 1)[0]
@@ -865,20 +1301,11 @@
     decay_grads = own_half(packed[:, at + H : at + 2 * H])
     skip_grads = own_half(packed[:, at + 2 * H : at + 3 * H])
 
-    expand_grads, reduce_grads = [], []
-    for layer in range(LAYERS):
-        zg = ordered(core, expand_z[layer], swap(expand_z[layer], "core"), 1)
-        ug = expand_u[layer]
-        sg = ug[:, CH // 2 :]
-        ug = ug[:, : CH // 2]
-        ug = ordered(core, ug, swap(ug, "core"), 1)
-        expand_grads.append(jnp.concatenate([zg, ug, sg], axis=1).astype(F32))
-        reduce_grads.append(ordered(core, reduce_g[layer], swap(reduce_g[layer], "core"), 1).astype(F32))
     return (
         layer_out,
         token_grads,
-        jnp.stack(expand_grads),
-        jnp.stack(reduce_grads),
+        jnp.swapaxes(grads[0], 1, 2),
+        grads[1],
         tap_grads,
         offset_grads,
         step_grads,

time: 905 us -> 734 us (0.81)
  Pallas kernels: 170 us -> 365 us
  waiting for transfers between devices: 318 us -> 132 us
  matrix products: 105 us -> 0 us
  other arithmetic: 119 us -> 33.3 us
  starting transfers between devices: 87.5 us -> 135 us
  local copies, waits for them, and re-layouts: 91.8 us -> 44.8 us
  between operations: 2.61 us -> 14.2 us
    pallas_call x12 -> x42, Pallas kernels: 170 us -> 365 us  [call(): return lambda *args: run(*args, *deps)]
    dot_general x14 -> x0, matrix products: 105 us -> none  [the longest x4 43.2 us: dot_nt(): lax.dot_general(a, b, (((1,), (1,)), ((), ())), preferred_element_type=F32)]
    ppermute x39 -> x5, waiting for transfers between devices: 148 us -> 48 us  [flip(): return lax.ppermute(value, axis, [(i, i ^ bit) for i in range(size)])]
    ppermute x39 -> x58, waiting for transfers between devices: 139 us -> 52.2 us  [swap(): return lax.ppermute(value, axis, [(0, 1), (1, 0)])]
    all_to_all x0 -> x8, starting transfers between devices: none -> 42 us  [the longest x4 23.8 us: meet(): self.parts = lax.all_to_all(total, 'zz', 0, 0, tiled=True)]
    ppermute x39 -> x58, starting transfers between devices: 24.1 us -> 51.2 us  [swap(): return lax.ppermute(value, axis, [(0, 1), (1, 0)])]
    select_n x25 -> x8, other arithmetic: 29.8 us -> 4.87 us  [the longest x7 4.01 us: following(): value = jnp.where(mark != mark, jnp.zeros_like(value), value)]
    ppermute x39 -> x5, starting transfers between devices: 27.8 us -> 9.86 us  [flip(): return lax.ppermute(value, axis, [(i, i ^ bit) for i in range(size)])]
  transfers between devices with their start and end apart: 94 -> 87, of which waited for: 37 -> 22; matrix products, arithmetic and copies ran while one was open for 28% -> 8% of each run, Pallas kernels for 16% -> 44%
where the time goes in v2:
time: 734 us; the launch traced here: 725 us
  Pallas kernels  365 us (50%)
  starting transfers between devices  135 us (18%)
  waiting for transfers between devices  132 us (18%)
  local copies, waits for them, and re-layouts  44.8 us (6%)
  other arithmetic  33.3 us (5%)
  between operations  14.2 us (2%)
    pallas_call x42, Pallas kernels, call(): return lambda *args: run(*args, *deps)  365 us
    ppermute x58, waiting for transfers between devices, swap(): return lax.ppermute(value, axis, [(0, 1), (1, 0)])  52.2 us
    ppermute x58, starting transfers between devices, swap(): return lax.ppermute(value, axis, [(0, 1), (1, 0)])  51.2 us
    ppermute x5, waiting for transfers between devices, flip(): return lax.ppermute(value, axis, [(i, i ^ bit) for i in range(size)])  48 us
    all_to_all x4, starting transfers between devices, meet(): self.parts = lax.all_to_all(total, 'zz', 0, 0, tiled=True)  23.8 us
    unnamed x153, local copies, waits for them, and re-layouts  19 us
    all_to_all x4, starting transfers between devices, reduce(): self.mine = lax.all_to_all(copies, 'zz', 0, 0, tiled=True)  18.2 us
  transfers between devices with their start and end apart: 87, of which 22 were waited for; matrix products, arithmetic and copies ran while one was open for 8% of the time, Pallas kernels for 44%

profile of v2, /device:TPU:0, one launch (start us, length us, event | category | flops | bytes accessed | tf_op | source)
XLA Modules:
  0.0 725.0 jit_solution(8348878653366443576)
XLA Ops:
  22.7 5.3 collective-permute-start
  36.7 10.1 %collective-permute-done.3.refs_4_.refs_9_ = bf16[2336,256]{1,0:T(8,128)(2,1)} collective-permute-done((bf16[2336,256]{1,0:T(8,128)(2,1)}, bf16[2336,256]{1,0:T(8,128)(2,1)}, u32[]{:S(2)}, u32[]{:S(2)}) %collective-permute-start.3) | collective-permute-done | bytes 1196064 | tf_op jit(solution)/shard_map/ppermute | solution.py:949
  53.5 8.4 %expand_first.2 = (bf16[512,2336]{1,0:T(8,128)(2,1)}, bf16[512,1024]{1,0:T(8,128)(2,1)}) custom-call(s32[8]{0:T(128)} %stack.71.refs_0_, f32[512,1024]{1,0:T(8,128)} %maximum_convert_fusion.refs_1_.refs_9_.refs_6_, f32[1,1024]{1,0:T(1,128)} %get-tuple-element.255.refs_2_.refs_5_, bf16[2,4384,512]{2,1,0:T(8,128)(2,1)} %bitcast.105, ...), custom_call_target="tpu_custom_call" | custom-call | flops 8800000000 | bytes 1000 | tf_op jit(solution)/shard_map/expand_first/pallas_call | solution.py:726
  66.5 13.5 %ssd_front.2 = (bf16[512,2560]{1,0:T(8,128)(2,1)}, bf16[512,2304]{1,0:T(8,128)(2,1)}, f32[512,128]{1,0:T(8,128)}, f32[4,32,128]{2,1,0:T(8,128)}, f32[4,8,2048]{2...) custom-call(bf16[512,2336]{1,0:T(8,128)(2,1)} %get-tuple-element.107.refs_0_.refs_2_.refs_4_, ...), custom_call_target="tpu_custom_call" | custom-call | flops 14300000256 | bytes 1000 | tf_op jit(solution)/shard_map/ssd_front/pallas_call | solution.py:726
  80.1 11.3 %collective-permute-start.7 = (f32[136,2048]{1,0:T(8,128)}, f32[136,2048]{1,0:T(8,128)S(1)}, u32[]{:S(2)}, u32[]{:S(2)}) collective-permute-start(f32[136,2048]{1,0:T(8,128)} %get-tuple-element.114), channel_id=1, source_target_pairs={{0,1},{1,0},{2,3},{3,2},{4,5},{5,4},{6,7},{7,6},{8,9},{9,8},{10,11... | collective-permute-start | bytes 3342344 | tf_op jit(solution)/shard_map/ppermute | solution.py:949
  110.6 6.1 expand_rest.2.refs_7_.refs_3_
  116.8 4.9 collective-permute-done.8
  122.7 10.9 %ssd_within.2.refs_1_.refs_2_ = f32[512,2048]{1,0:T(8,128)} custom-call(bf16[512,2560]{1,0:T(8,128)(2,1)} %get-tuple-element.108.refs_0_.refs_5_.refs_6_.refs_2_.refs_1_, f32[512,128]{1,0:T(8,128)} %get-tuple-element.109.refs_1_.refs_2_.refs_6_, f32[4,32,128]{2,1,0:T(8,128)} %get-tuple-element.110.refs_2_, ...), custom_call_target="tpu_custom_call" | custom-call | flops 12099999744 | bytes 1000 | tf_op jit(solution)/shard_map/ssd_within/pallas_call | solution.py:726
  136.7 15.6 %collective-permute-done.16.refs_3_.refs_11_ = bf16[2048,256]{1,0:T(8,128)(2,1)} collective-permute-done((bf16[2048,256]{1,0:T(8,128)(2,1)}, bf16[2048,256]{1,0:T(8,128)(2,1)}, u32[]{:S(2)}, u32[]{:S(2)}) %collective-permute-start.16) | collective-permute-done | bytes 1048608 | tf_op jit(solution)/shard_map/ppermute | solution.py:949
  156.1 13.5 %ssd_gate.2 = (f32[512,2048]{1,0:T(8,128)}, bf16[512,1024]{1,0:T(8,128)(2,1)}, bf16[512,1024]{1,0:T(8,128)(2,1)}, f32[512,1024]{1,0:T(8,128)}) custom-call(s32[8]{0:T(128)} %stack.67.refs_0_, f32[512,2048]{1,0:T(8,128)} %ssd_within.2.refs_1_.refs_2_, f32[512,128]{1,0:T(8,128)} %get-tuple-element.109.refs_1_.refs_2_.refs_6_, ...), custom_call_target="tpu_custom_call" | custom-call | flops 14300000256 | bytes 1000 | tf_op jit(solution)/shard_map/ssd_gate/pallas_call | solution.py:726
  171.2 8.4 %expand_first.3 = (bf16[512,2336]{1,0:T(8,128)(2,1)}, bf16[512,1024]{1,0:T(8,128)(2,1)}) custom-call(s32[8]{0:T(128)} %stack.71.refs_0_, f32[512,1024]{1,0:T(8,128)} %get-tuple-element.115.refs_1_.refs_9_.refs_6_, f32[1,1024]{1,0:T(1,128)} %get-tuple-element.254.refs_2_.refs_5_, bf16[2,4384,512]{2,1,0:T(8,128)(2,1)} %bitcast.109, ...), custom_call_target="tpu_custom_call" | custom-call | flops 8800000000 | bytes 1000 | tf_op jit(solution)/shard_map/expand_first/pallas_call | solution.py:726
  186.5 13.5 %ssd_front.3 = (bf16[512,2560]{1,0:T(8,128)(2,1)}, bf16[512,2304]{1,0:T(8,128)(2,1)}, f32[512,128]{1,0:T(8,128)}, f32[4,32,128]{2,1,0:T(8,128)}, f32[4,8,2048]{2...) custom-call(bf16[512,2336]{1,0:T(8,128)(2,1)} %get-tuple-element.116.refs_0_.refs_4_, ...), custom_call_target="tpu_custom_call" | custom-call | flops 14300000256 | bytes 1000 | tf_op jit(solution)/shard_map/ssd_front/pallas_call | solution.py:726
  209.3 6.2 expand_rest.3.refs_7_.refs_3_
  215.5 4.9 collective-permute-done.24
  220.4 10.9 %ssd_within.3.refs_1_ = f32[512,2048]{1,0:T(8,128)} custom-call(bf16[512,2560]{1,0:T(8,128)(2,1)} %get-tuple-element.118.refs_0_.refs_5_.refs_6_.refs_1_, f32[512,128]{1,0:T(8,128)} %get-tuple-element.119.refs_1_.refs_2_.refs_6_, f32[4,32,128]{2,1,0:T(8,128)} %get-tuple-element.120.refs_2_, f32[528,128]{1,0:T(8,128)} %broadcast_in_dim.51.refs_2_.refs_3_.refs_6_, ...), custom_call_target="tpu_custom_call" | custom-call | flops 12099999744 | bytes 1000 | tf_op jit(solution)/shard_map/ssd_within/pallas_call | solution.py:726
  232.5 13.6 %ssd_gate.3 = (f32[512,2048]{1,0:T(8,128)}, bf16[512,1024]{1,0:T(8,128)(2,1)}, bf16[512,1024]{1,0:T(8,128)(2,1)}, f32[512,1024]{1,0:T(8,128)}) custom-call(s32[8]{0:T(128)} %stack.67.refs_0_, f32[512,2048]{1,0:T(8,128)} %ssd_within.3.refs_1_, f32[512,128]{1,0:T(8,128)} %get-tuple-element.119.refs_1_.refs_2_.refs_6_, ...), custom_call_target="tpu_custom_call" | custom-call | flops 14300000256 | bytes 1000 | tf_op jit(solution)/shard_map/ssd_gate/pallas_call | solution.py:726
  252.9 15.7 %gate_back.2 = (bf16[512,2048]{1,0:T(8,128)(2,1)}, bf16[512,2048]{1,0:T(8,128)(2,1)}, bf16[512,1024]{1,0:T(8,128)(2,1)}, bf16[512,1024]{1,0:T(8,128)(2,1)}, f32[...) custom-call(s32[8]{0:T(128)} %stack.67.refs_0_, ...), custom_call_target="tpu_custom_call" | custom-call | flops 16499999744 | bytes 1000 | tf_op jit(solution)/shard_map/gate_back/pallas_call | solution.py:726
  271.9 4.6 collective-permute-done.29
  282.5 11.6 %far_grads.2 = (bf16[2048,512]{1,0:T(8,128)(2,1)}, bf16[2048,512]{1,0:T(8,128)(2,1)}, bf16[1024,512]{1,0:T(8,128)(2,1)}, bf16[512,1024]{1,0:T(8,128)(2,1)}) custom-call(s32[8]{0:T(128)} %stack.71.refs_0_, bf16[512,1024]{1,0:T(8,128)(2,1)} %get-tuple-element.128.refs_1_, bf16[512,1024]{1,0:T(8,128)(2,1)} %copy-done.61, ...), custom_call_target="tpu_custom_call" | custom-call | flops 13200000000 | bytes 1000 | tf_op jit(solution)/shard_map/far_grads/pallas_call | solution.py:726
  296.2 17.7 %within_back.2 = (f32[512,2048]{1,0:T(8,128)}, f32[512,256]{1,0:T(8,128)}) custom-call(bf16[512,2560]{1,0:T(8,128)(2,1)} %get-tuple-element.118.refs_0_.refs_5_.refs_6_.refs_1_, f32[512,128]{1,0:T(8,128)} %get-tuple-element.119.refs_1_.refs_2_.refs_6_, f32[4,32,128]{2,1,0:T(8,128)} %get-tuple-element.120.refs_2_, ...), custom_call_target="tpu_custom_call" | custom-call | flops 18699999232 | bytes 1000 | tf_op jit(solution)/shard_map/within_back/pallas_call | solution.py:726
  316.5 4.6 cross.4
  324.0 24.2 %ssd_last.2 = (bf16[512,1280]{1,0:T(8,128)(2,1)}, bf16[512,1280]{1,0:T(8,128)(2,1)}, f32[8,2304]{1,0:T(8,128)}, bf16[8,2304]{1,0:T(8,128)(2,1)}, f32[40,2304]{1,0:T(8,128)}, /*index=5*/f32[24,128]{1,0:T(8,128)}) custom-call(s32[8]{0:T(128)} %stack.71.refs_0_, bf16[512,2560]{1,0:T(8,128)(2,1)} %get-tuple-element.118.refs_0_.refs_5_.refs_6_.refs_1_, ...), custom_call_target="tpu_custom_call" | custom-call | flops 26400000000 | bytes 1000 | tf_op jit(solution)/shard_map/ssd_last/pallas_call | solution.py:726
  356.1 9.2 %all-to-all-start = ((bf16[4,256,512]{2,1,0:T(8,128)(2,1)}), bf16[4,256,512]{2,1,0:T(8,128)(2,1)S(1)}, u32[]{:S(2)}, u32[]{:S(2)}) async-start(bf16[4,256,512]{2,1,0:T(8,128)(2,1)} %bitcast.130), calls=%async_computation | async-start | bytes 2097152 | tf_op jit(solution)/shard_map/all_to_all | solution.py:817
  367.0 16.4 %input_back.2 = (f32[512,1024]{1,0:T(8,128)}, f32[8,1024]{1,0:T(8,128)}) custom-call(s32[8]{0:T(128)} %stack.71.refs_0_, bf16[512,1024]{1,0:T(8,128)(2,1)} %get-tuple-element.128.refs_1_, bf16[512,1024]{1,0:T(8,128)(2,1)} %get-tuple-element.129.refs_2_, bf16[512,1280]{1,0:T(8,128)(2,1)} %get-tuple-element.249.refs_3_.refs_1_, bf16[512,1280]{1,0:T(8,128)(2,1)} %copy-done.50, ...), custom_call_target="tpu_custom_call" | custom-call | flops 17600000000 | bytes 1000 | tf_op jit(solution)/shard_map/input_back/pallas_call | solution.py:726
  384.5 7.6 %near_grads.2 = (bf16[1280,512]{1,0:T(8,128)(2,1)}, bf16[1280,512]{1,0:T(8,128)(2,1)}, bf16[768,512]{1,0:T(8,128)(2,1)}, bf16[256,1024]{1,0:T(8,128)(2,1)}) custom-call(s32[8]{0:T(128)} %stack.71.refs_0_, bf16[512,1280]{1,0:T(8,128)(2,1)} %get-tuple-element.249.refs_3_.refs_1_, bf16[512,1280]{1,0:T(8,128)(2,1)} %copy-done.51, ...), custom_call_target="tpu_custom_call" | custom-call | flops 6600000000 | bytes 1000 | tf_op jit(solution)/shard_map/near_grads/pallas_call | solution.py:726
  396.5 15.6 %gate_back.3 = (bf16[512,2048]{1,0:T(8,128)(2,1)}, bf16[512,2048]{1,0:T(8,128)(2,1)}, bf16[512,1024]{1,0:T(8,128)(2,1)}, bf16[512,1024]{1,0:T(8,128)(2,1)}, f32[...) custom-call(s32[8]{0:T(128)} %stack.67.refs_0_, ...), custom_call_target="tpu_custom_call" | custom-call | flops 16499999744 | bytes 1000 | tf_op jit(solution)/shard_map/gate_back/pallas_call | solution.py:726
  420.6 5.1 all-to-all-start.1
  430.6 11.5 %far_grads.3 = (bf16[2048,512]{1,0:T(8,128)(2,1)}, bf16[2048,512]{1,0:T(8,128)(2,1)}, bf16[1024,512]{1,0:T(8,128)(2,1)}, bf16[512,1024]{1,0:T(8,128)(2,1)}) custom-call(s32[8]{0:T(128)} %stack.71.refs_0_, bf16[512,1024]{1,0:T(8,128)(2,1)} %get-tuple-element.158.refs_1_, bf16[512,1024]{1,0:T(8,128)(2,1)} %collective-permute-done.41.refs_2_, ...), custom_call_target="tpu_custom_call" | custom-call | flops 13200000000 | bytes 1000 | tf_op jit(solution)/shard_map/far_grads/pallas_call | solution.py:726
  443.3 8.9 %all-to-all-done.1 = bf16[4,256,512]{2,1,0:T(8,128)(2,1)S(1)} async-done(((bf16[4,256,512]{2,1,0:T(8,128)(2,1)}), bf16[4,256,512]{2,1,0:T(8,128)(2,1)S(1)}, u32[]{:S(2)}, u32[]{:S(2)}) %all-to-all-start.1) | async-done | bytes 1048608 | tf_op jit(solution)/shard_map/all_to_all | solution.py:824
  465.5 17.6 %within_back.3 = (f32[512,2048]{1,0:T(8,128)}, f32[512,256]{1,0:T(8,128)}) custom-call(bf16[512,2560]{1,0:T(8,128)(2,1)} %get-tuple-element.108.refs_0_.refs_5_.refs_6_.refs_2_.refs_1_, f32[512,128]{1,0:T(8,128)} %get-tuple-element.109.refs_1_.refs_2_.refs_6_, f32[4,32,128]{2,1,0:T(8,128)} %get-tuple-element.110.refs_2_, ...), custom_call_target="tpu_custom_call" | custom-call | flops 18699999232 | bytes 1000 | tf_op jit(solution)/shard_map/within_back/pallas_call | solution.py:726
  483.2 4.7 cross.6
  492.9 5.1 all-to-all-start.3
  497.9 24.2 %ssd_last.3 = (bf16[512,1280]{1,0:T(8,128)(2,1)}, bf16[512,1280]{1,0:T(8,128)(2,1)}, f32[8,2304]{1,0:T(8,128)}, bf16[8,2304]{1,0:T(8,128)(2,1)}, f32[40,2304]{1,0:T(8,128)}, /*index=5*/f32[24,128]{1,0:T(8,128)}) custom-call(s32[8]{0:T(128)} %stack.71.refs_0_, bf16[512,2560]{1,0:T(8,128)(2,1)} %get-tuple-element.108.refs_0_.refs_5_.refs_6_.refs_2_.refs_1_, ...), custom_call_target="tpu_custom_call" | custom-call | flops 26400000000 | bytes 1000 | tf_op jit(solution)/shard_map/ssd_last/pallas_call | solution.py:726
  532.1 6.0 all-to-all-start.4
  539.0 16.3 %input_back.3 = (f32[512,1024]{1,0:T(8,128)}, f32[8,1024]{1,0:T(8,128)}) custom-call(s32[8]{0:T(128)} %stack.71.refs_0_, bf16[512,1024]{1,0:T(8,128)(2,1)} %get-tuple-element.158.refs_1_, bf16[512,1024]{1,0:T(8,128)(2,1)} %get-tuple-element.159.refs_2_, bf16[512,1280]{1,0:T(8,128)(2,1)} %get-tuple-element.247.refs_3_.refs_1_, ...), custom_call_target="tpu_custom_call" | custom-call | flops 17600000000 | bytes 1000 | tf_op jit(solution)/shard_map/input_back/pallas_call | solution.py:726
  556.2 7.7 %near_grads.3 = (bf16[1280,512]{1,0:T(8,128)(2,1)}, bf16[1280,512]{1,0:T(8,128)(2,1)}, bf16[768,512]{1,0:T(8,128)(2,1)}, bf16[256,1024]{1,0:T(8,128)(2,1)}) custom-call(s32[8]{0:T(128)} %stack.71.refs_0_, bf16[512,1280]{1,0:T(8,128)(2,1)} %get-tuple-element.247.refs_3_.refs_1_, bf16[512,1280]{1,0:T(8,128)(2,1)} %collective-permute-done.54.refs_2_, ...), custom_call_target="tpu_custom_call" | custom-call | flops 6600000000 | bytes 1000 | tf_op jit(solution)/shard_map/near_grads/pallas_call | solution.py:726
  577.9 18.0 %collective-permute-done.62 = f32[240,128]{1,0:T(8,128)S(1)} collective-permute-done((f32[240,128]{1,0:T(8,128)S(1)}, f32[240,128]{1,0:T(8,128)S(1)}, u32[]{:S(2)}, u32[]{:S(2)}) %collective-permute-start.62) | collective-permute-done | bytes 122912 | tf_op jit(solution)/shard_map/ppermute | solution.py:954
  602.1 14.1 %collective-permute-done.64 = f32[240,128]{1,0:T(8,128)S(1)} collective-permute-done((f32[240,128]{1,0:T(8,128)S(1)}, f32[240,128]{1,0:T(8,128)S(1)}, u32[]{:S(2)}, u32[]{:S(2)}) %collective-permute-start.64) | collective-permute-done | bytes 122912 | tf_op jit(solution)/shard_map/ppermute | solution.py:954
  616.7 6.1 collective-permute-done.60.refs_2_
  627.1 4.8 all-to-all-start.6
  634.5 8.3 %final_grads.2 = (f32[2,4384,512]{2,1,0:T(8,128)}, f32[2,1024,1024]{2,1,0:T(8,128)}) custom-call(s32[8]{0:T(128)} %stack.71.refs_0_, bf16[1024,512]{1,0:T(8,128)(2,1)} %bitcast.126, bf16[1024,512]{1,0:T(8,128)(2,1)} %collective-permute-done.57.refs_2_, bf16[1024,512]{1,0:T(8,128)(2,1)} %collective-permute-done.65.refs_3_, ...), custom_call_target="tpu_custom_call" | custom-call | flops 8800000000 | bytes 1000 | tf_op jit(solution)/shard_map/final_grads/pallas_call | solution.py:726
  642.8 5.1 collective-permute-done.63.refs_2_
  658.3 11.1 %collective-permute-done.77 = f32[240,128]{1,0:T(8,128)S(1)} collective-permute-done((f32[240,128]{1,0:T(8,128)S(1)}, f32[240,128]{1,0:T(8,128)S(1)}, u32[]{:S(2)}, u32[]{:S(2)}) %collective-permute-start.77) | collective-permute-done | bytes 122912 | tf_op jit(solution)/shard_map/ppermute | solution.py:954
  669.5 4.6 collective-permute-start.78
  688.1 7.7 %collective-permute-done.71 = bf16[512,512]{1,0:T(8,128)(2,1)} collective-permute-done((bf16[512,512]{1,0:T(8,128)(2,1)}, bf16[512,512]{1,0:T(8,128)(2,1)}, u32[]{:S(2)}, u32[]{:S(2)}) %collective-permute-start.71) | collective-permute-done | bytes 524320 | tf_op jit(solution)/shard_map/ppermute | solution.py:949
  698.6 5.7 collective-permute-start.75
  704.4 4.9 collective-permute-done.74.refs_6_
  716.2 8.3 %final_grads.3 = (f32[2,4384,512]{2,1,0:T(8,128)}, f32[2,1024,1024]{2,1,0:T(8,128)}) custom-call(s32[8]{0:T(128)} %stack.71.refs_0_, bf16[1024,512]{1,0:T(8,128)(2,1)} %bitcast.115, bf16[1024,512]{1,0:T(8,128)(2,1)} %copy-done.6, bf16[1024,512]{1,0:T(8,128)(2,1)} %collective-permute-done.72.refs_3_, ...), custom_call_target="tpu_custom_call", output_to_operand_aliasing={{0}: (9, {}), {1}: (10, {})} | custom-call | flops 8800000000 | bytes 1000 | tf_op jit(solution)/shard_map/final_grads/pallas_call | solution.py:726
  (448 shorter events, 220.5 us)
Async XLA Ops:
  4.3 31.8 %collective-permute-start.2 = (bf16[2,8,1152]{2,0,1:T(2,128)(2,1)S(1)}, bf16[2,8,1152]{2,0,1:T(2,128)(2,1)S(1)}, u32[]{:S(2)}, u32[]{:S(2)}) collective-permute-start(bf16[2,8,1152]{2,0,1:T(2,128)(2,1)S(1)} %constant_dynamic-update-slice_fusion), channel_id=1, source_target_pairs={{0,8},{8,0},{1,9},{9,1},{2,10},{10,2},{3,11},{11,3},{4,12},{12,4},... | collective-permute-start | bytes 110600 | tf_op jit(solution)/shard_map/ppermute | solution.py:949
  8.6 38.9 %collective-permute-start.20 = (bf16[256,1024]{1,0:T(8,128)(2,1)S(1)}, bf16[256,1024]{1,0:T(8,128)(2,1)S(1)}, u32[]{:S(2)}, u32[]{:S(2)}) collective-permute-start(bf16[256,1024]{1,0:T(8,128)(2,1)S(1)} %get-tuple-element.227), channel_id=1, source_target_pairs={{0,0},{1,4},{2,1},{3,5},{4,2},{5,6},{6,3},{7,7},{8,8},{9,12},{10,9... | collective-permute-start | bytes 1572872 | tf_op jit(solution)/shard_map/ppermute | solution.py:978
  9.3 38.8 %collective-permute-start.21 = (bf16[256,1024]{1,0:T(8,128)(2,1)S(1)}, bf16[256,1024]{1,0:T(8,128)(2,1)S(1)}, u32[]{:S(2)}, u32[]{:S(2)}) collective-permute-start(bf16[256,1024]{1,0:T(8,128)(2,1)S(1)} %get-tuple-element.228), channel_id=1, source_target_pairs={{0,4},{1,0},{2,5},{3,1},{4,6},{5,2},{6,7},{7,3},{8,12},{9,8},{10,1... | collective-permute-start | bytes 1572872 | tf_op jit(solution)/shard_map/ppermute | solution.py:979
  18.5 28.2 %collective-permute-start.3 = (bf16[2336,256]{1,0:T(8,128)(2,1)}, bf16[2336,256]{1,0:T(8,128)(2,1)}, u32[]{:S(2)}, u32[]{:S(2)}) collective-permute-start(bf16[2336,256]{1,0:T(8,128)(2,1)} %take.6.refs_2_), channel_id=1, source_target_pairs={{0,8},{8,0},{1,9},{9,1},{2,10},{10,2},{3,11},{11,3},{4,12},{12,4},... | collective-permute-start | bytes 3588104 | tf_op jit(solution)/shard_map/ppermute | solution.py:949
  22.7 26.9 %collective-permute-start = (bf16[256,1024]{1,0:T(8,128)(2,1)}, bf16[256,1024]{1,0:T(8,128)(2,1)}, u32[]{:S(2)}, u32[]{:S(2)}) collective-permute-start(bf16[256,1024]{1,0:T(8,128)(2,1)} %get-tuple-element.231), channel_id=1, source_target_pairs={{0,0},{1,4},{2,1},{3,5},{4,2},{5,6},{6,3},{7,7},{8,8},{9,12},{10,9... | collective-permute-start | bytes 1572872 | tf_op jit(solution)/shard_map/ppermute | solution.py:978
  47.5 48.2 %collective-permute-start.10 = (bf16[2048,256]{1,0:T(8,128)(2,1)S(1)}, bf16[2048,256]{1,0:T(8,128)(2,1)}, u32[]{:S(2)}, u32[]{:S(2)}) collective-permute-start(bf16[2048,256]{1,0:T(8,128)(2,1)S(1)} %copy-done.3), channel_id=1, source_target_pairs={{0,8},{8,0},{1,9},{9,1},{2,10},{10,2},{3,11},{11,3},{4,12},{12,4},... | collective-permute-start | bytes 3145736 | tf_op jit(solution)/shard_map/ppermute | solution.py:949
  48.0 47.6 %collective-permute-start.12 = (bf16[512,1024]{1,0:T(8,128)(2,1)}, bf16[512,1024]{1,0:T(8,128)(2,1)}, u32[]{:S(2)}, u32[]{:S(2)}) collective-permute-start(bf16[512,1024]{1,0:T(8,128)(2,1)} %take.8), channel_id=1, source_target_pairs={{0,8},{8,0},{1,9},{9,1},{2,10},{10,2},{3,11},{11,3},{4,12},{12,4},... | collective-permute-start | bytes 3145736 | tf_op jit(solution)/shard_map/ppermute | solution.py:949
  80.1 24.4 %collective-permute-start.7 = (f32[136,2048]{1,0:T(8,128)}, f32[136,2048]{1,0:T(8,128)S(1)}, u32[]{:S(2)}, u32[]{:S(2)}) collective-permute-start(f32[136,2048]{1,0:T(8,128)} %get-tuple-element.114), channel_id=1, source_target_pairs={{0,1},{1,0},{2,3},{3,2},{4,5},{5,4},{6,7},{7,6},{8,9},{9,8},{10,11... | collective-permute-start | bytes 3342344 | tf_op jit(solution)/shard_map/ppermute | solution.py:949
  95.7 60.5 %collective-permute-start.13 = (bf16[512,1024]{1,0:T(8,128)(2,1)}, bf16[512,1024]{1,0:T(8,128)(2,1)}, u32[]{:S(2)}, u32[]{:S(2)}) collective-permute-start(bf16[512,1024]{1,0:T(8,128)(2,1)} %collective-permute-done.12.refs_11_.refs_9_), channel_id=1, source_target_pairs={{0,1},{1,0},{2,3},{3,2},{4,5},{5,4},{6,7},{7,6},{8,9},{9,8},{10,11... | collective-permute-start | bytes 3145736 | tf_op jit(solution)/shard_map/ppermute | solution.py:949
  96.2 25.5 %collective-permute-start.6 = (bf16[512,1024]{1,0:T(8,128)(2,1)}, bf16[512,1024]{1,0:T(8,128)(2,1)S(1)}, u32[]{:S(2)}, u32[]{:S(2)}) collective-permute-start(bf16[512,1024]{1,0:T(8,128)(2,1)} %get-tuple-element.112.refs_1_.refs_3_), channel_id=1, source_target_pairs={{0,1},{1,0},{2,3},{3,2},{4,5},{5,4},{6,7},{7,6},{8,9},{9,8},{10,11... | collective-permute-start | bytes 3145736 | tf_op jit(solution)/shard_map/ppermute | solution.py:949
  100.4 54.4 %collective-permute-start.14 = (bf16[2336,256]{1,0:T(8,128)(2,1)}, bf16[2336,256]{1,0:T(8,128)(2,1)S(1)}, u32[]{:S(2)}, u32[]{:S(2)}) collective-permute-start(bf16[2336,256]{1,0:T(8,128)(2,1)} %take.9.refs_3_), channel_id=1, source_target_pairs={{0,8},{8,0},{1,9},{9,1},{2,10},{10,2},{3,11},{11,3},{4,12},{12,4},... | collective-permute-start | bytes 3588104 | tf_op jit(solution)/shard_map/ppermute | solution.py:949
  104.5 47.7 %collective-permute-start.16 = (bf16[2048,256]{1,0:T(8,128)(2,1)}, bf16[2048,256]{1,0:T(8,128)(2,1)}, u32[]{:S(2)}, u32[]{:S(2)}) collective-permute-start(bf16[2048,256]{1,0:T(8,128)(2,1)} %take.10.refs_3_), channel_id=1, source_target_pairs={{0,8},{8,0},{1,9},{9,1},{2,10},{10,2},{3,11},{11,3},{4,12},{12,4},... | collective-permute-start | bytes 3145736 | tf_op jit(solution)/shard_map/ppermute | solution.py:949
  121.7 33.2 %collective-permute-start.9 = (f32[64,2048]{1,0:T(8,128)S(1)}, f32[64,2048]{1,0:T(8,128)S(1)}, u32[]{:S(2)}, u32[]{:S(2)}) collective-permute-start(f32[64,2048]{1,0:T(8,128)S(1)} %collective-permute-done.8), channel_id=1, source_target_pairs={{0,1},{1,0},{2,3},{3,2},{4,5},{5,4},{6,7},{7,6},{8,9},{9,8},{10,11... | collective-permute-start | bytes 1572872 | tf_op jit(solution)/shard_map/ppermute | solution.py:949
  136.2 46.9 %collective-permute-start.22 = (bf16[512,1024]{1,0:T(8,128)(2,1)}, bf16[512,1024]{1,0:T(8,128)(2,1)}, u32[]{:S(2)}, u32[]{:S(2)}) collective-permute-start(bf16[512,1024]{1,0:T(8,128)(2,1)} %take.11), channel_id=1, source_target_pairs={{0,8},{8,0},{1,9},{9,1},{2,10},{10,2},{3,11},{11,3},{4,12},{12,4},... | collective-permute-start | bytes 3145736 | tf_op jit(solution)/shard_map/ppermute | solution.py:949
  205.6 26.9 %collective-permute-start.27 = (bf16[512,1024]{1,0:T(8,128)(2,1)}, bf16[512,1024]{1,0:T(8,128)(2,1)}, u32[]{:S(2)}, u32[]{:S(2)}) collective-permute-start(bf16[512,1024]{1,0:T(8,128)(2,1)} %collective-permute-done.22.refs_11_.refs_9_), channel_id=1, source_target_pairs={{0,1},{1,0},{2,3},{3,2},{4,5},{5,4},{6,7},{7,6},{8,9},{9,8},{10,11... | collective-permute-start | bytes 3145736 | tf_op jit(solution)/shard_map/ppermute | solution.py:949
  248.0 21.2 %collective-permute-start.28 = (bf16[256,1024]{1,0:T(8,128)(2,1)S(1)}, bf16[256,1024]{1,0:T(8,128)(2,1)S(1)}, u32[]{:S(2)}, u32[]{:S(2)}) collective-permute-start(bf16[256,1024]{1,0:T(8,128)(2,1)S(1)} %get-tuple-element.223), channel_id=1, source_target_pairs={{0,0},{4,1},{1,2},{5,3},{2,4},{6,5},{3,6},{7,7},{8,8},{12,9},{9,10... | collective-permute-start | bytes 1572872 | tf_op jit(solution)/shard_map/ppermute | solution.py:990
  248.7 27.9 %collective-permute-start.29 = (bf16[256,1024]{1,0:T(8,128)(2,1)S(1)}, bf16[256,1024]{1,0:T(8,128)(2,1)S(1)}, u32[]{:S(2)}, u32[]{:S(2)}) collective-permute-start(bf16[256,1024]{1,0:T(8,128)(2,1)S(1)} %get-tuple-element.224), channel_id=1, source_target_pairs={{4,0},{0,1},{5,2},{1,3},{6,4},{2,5},{7,6},{3,7},{12,8},{8,9},{13,1... | collective-permute-start | bytes 1572872 | tf_op jit(solution)/shard_map/ppermute | solution.py:991
  252.5 28.7 %collective-permute-start.31 = (bf16[512,1024]{1,0:T(8,128)(2,1)S(1)}, bf16[512,1024]{1,0:T(8,128)(2,1)S(1)}, u32[]{:S(2)}, u32[]{:S(2)}) collective-permute-start(bf16[512,1024]{1,0:T(8,128)(2,1)S(1)} %copy-done.59), channel_id=1, source_target_pairs={{0,1},{1,0},{2,3},{3,2},{4,5},{5,4},{6,7},{7,6},{8,9},{9,8},{10,11... | collective-permute-start | bytes 3145736 | tf_op jit(solution)/shard_map/ppermute | solution.py:949
  279.5 34.3 %collective-permute-start.34 = (bf16[128,2048]{1,0:T(8,128)(2,1)S(1)}, bf16[128,2048]{1,0:T(8,128)(2,1)S(1)}, u32[]{:S(2)}, u32[]{:S(2)}) collective-permute-start(bf16[128,2048]{1,0:T(8,128)(2,1)S(1)} %fusion.1), channel_id=1, source_target_pairs={{2,0},{6,4},{3,1},{7,5},{10,8},{14,12},{11,9},{15,13},{18,16},{22,... | collective-permute-start | bytes 1572872 | tf_op jit(solution)/shard_map/ppermute | solution.py:1050
  294.1 21.1 %collective-permute-start.35 = (bf16[1024,512]{1,0:T(8,128)(2,1)}, bf16[1024,512]{1,0:T(8,128)(2,1)S(1)}, u32[]{:S(2)}, u32[]{:S(2)}) collective-permute-start(bf16[1024,512]{1,0:T(8,128)(2,1)} %get-tuple-element.143), channel_id=1, source_target_pairs={{0,8},{8,0},{1,9},{9,1},{2,10},{10,2},{3,11},{11,3},{4,12},{12,4},... | collective-permute-start | bytes 3145736 | tf_op jit(solution)/shard_map/ppermute | solution.py:949
  294.7 20.7 %collective-permute-start.36 = (bf16[512,1024]{1,0:T(8,128)(2,1)}, bf16[512,1024]{1,0:T(8,128)(2,1)S(1)}, u32[]{:S(2)}, u32[]{:S(2)}) collective-permute-start(bf16[512,1024]{1,0:T(8,128)(2,1)} %get-tuple-element.144), channel_id=1, source_target_pairs={{0,16},{16,0},{1,17},{17,1},{2,18},{18,2},{3,19},{19,3},{4,20},{20... | collective-permute-start | bytes 3145736 | tf_op jit(solution)/shard_map/ppermute | solution.py:949
  321.1 27.1 %collective-permute-start.38 = (bf16[512,512]{1,0:T(8,128)(2,1)}, bf16[512,512]{1,0:T(8,128)(2,1)S(1)}, u32[]{:S(2)}, u32[]{:S(2)}) collective-permute-start(bf16[512,512]{1,0:T(8,128)(2,1)} %get-tuple-element.149), channel_id=1, source_target_pairs={{0,8},{8,0},{1,9},{9,1},{2,10},{10,2},{3,11},{11,3},{4,12},{12,4},... | collective-permute-start | bytes 1572872 | tf_op jit(solution)/shard_map/ppermute | solution.py:949
  322.5 25.7 %collective-permute-start.37 = (bf16[512,512]{1,0:T(8,128)(2,1)}, bf16[512,512]{1,0:T(8,128)(2,1)S(1)}, u32[]{:S(2)}, u32[]{:S(2)}) collective-permute-start(bf16[512,512]{1,0:T(8,128)(2,1)} %get-tuple-element.145.refs_22_), channel_id=1, source_target_pairs={{0,16},{16,0},{1,17},{17,1},{2,18},{18,2},{3,19},{19,3},{4,20},{20... | collective-permute-start | bytes 1572872 | tf_op jit(solution)/shard_map/ppermute | solution.py:949
  356.1 37.1 %all-to-all-start = ((bf16[4,256,512]{2,1,0:T(8,128)(2,1)}), bf16[4,256,512]{2,1,0:T(8,128)(2,1)S(1)}, u32[]{:S(2)}, u32[]{:S(2)}) async-start(bf16[4,256,512]{2,1,0:T(8,128)(2,1)} %bitcast.130), calls=%async_computation | async-start | bytes 2097152 | tf_op jit(solution)/shard_map/all_to_all | solution.py:817
  392.1 20.6 %collective-permute-start.44 = (bf16[256,1024]{1,0:T(8,128)(2,1)}, bf16[256,1024]{1,0:T(8,128)(2,1)S(1)}, u32[]{:S(2)}, u32[]{:S(2)}) collective-permute-start(bf16[256,1024]{1,0:T(8,128)(2,1)} %get-tuple-element.164), channel_id=1, source_target_pairs={{0,16},{16,0},{1,17},{17,1},{2,18},{18,2},{3,19},{19,3},{4,20},{20... | collective-permute-start | bytes 1572872 | tf_op jit(solution)/shard_map/ppermute | solution.py:949
  420.6 31.6 %all-to-all-start.1 = ((bf16[4,256,512]{2,1,0:T(8,128)(2,1)}), bf16[4,256,512]{2,1,0:T(8,128)(2,1)S(1)}, u32[]{:S(2)}, u32[]{:S(2)}) async-start(bf16[4,256,512]{2,1,0:T(8,128)(2,1)} %bitcast.45), calls=%async_computation.1 | async-start | bytes 2097152 | tf_op jit(solution)/shard_map/all_to_all | solution.py:824
  425.8 33.6 %collective-permute-start.45 = (bf16[384,512]{1,0:T(8,128)(2,1)}, bf16[384,512]{1,0:T(8,128)(2,1)}, u32[]{:S(2)}, u32[]{:S(2)}) collective-permute-start(bf16[384,512]{1,0:T(8,128)(2,1)} %get-tuple-element.166.refs_9_), channel_id=1, source_target_pairs={{0,16},{16,0},{1,17},{17,1},{2,18},{18,2},{3,19},{19,3},{4,20},{20... | collective-permute-start | bytes 1179656 | tf_op jit(solution)/shard_map/ppermute | solution.py:949
  427.3 32.1 %collective-permute-start.46 = (bf16[256,512]{1,0:T(8,128)(2,1)S(1)}, bf16[256,512]{1,0:T(8,128)(2,1)}, u32[]{:S(2)}, u32[]{:S(2)}) collective-permute-start(bf16[256,512]{1,0:T(8,128)(2,1)S(1)} %copy-done.69), channel_id=1, source_target_pairs={{0,8},{8,0},{1,9},{9,1},{2,10},{10,2},{3,11},{11,3},{4,12},{12,4},... | collective-permute-start | bytes 786440 | tf_op jit(solution)/shard_map/ppermute | solution.py:949
  429.1 27.7 %collective-permute-start.48 = (bf16[128,2048]{1,0:T(8,128)(2,1)S(1)}, bf16[128,2048]{1,0:T(8,128)(2,1)S(1)}, u32[]{:S(2)}, u32[]{:S(2)}) collective-permute-start(bf16[128,2048]{1,0:T(8,128)(2,1)S(1)} %fusion.4), channel_id=1, source_target_pairs={{2,0},{6,4},{3,1},{7,5},{10,8},{14,12},{11,9},{15,13},{18,16},{22,... | collective-permute-start | bytes 1572872 | tf_op jit(solution)/shard_map/ppermute | solution.py:1050
  442.2 41.0 %collective-permute-start.49 = (bf16[1024,512]{1,0:T(8,128)(2,1)}, bf16[1024,512]{1,0:T(8,128)(2,1)}, u32[]{:S(2)}, u32[]{:S(2)}) collective-permute-start(bf16[1024,512]{1,0:T(8,128)(2,1)} %get-tuple-element.174), channel_id=1, source_target_pairs={{0,8},{8,0},{1,9},{9,1},{2,10},{10,2},{3,11},{11,3},{4,12},{12,4},... | collective-permute-start | bytes 3145736 | tf_op jit(solution)/shard_map/ppermute | solution.py:949
  442.7 40.4 %collective-permute-start.50 = (bf16[512,1024]{1,0:T(8,128)(2,1)}, bf16[512,1024]{1,0:T(8,128)(2,1)}, u32[]{:S(2)}, u32[]{:S(2)}) collective-permute-start(bf16[512,1024]{1,0:T(8,128)(2,1)} %get-tuple-element.175), channel_id=1, source_target_pairs={{0,16},{16,0},{1,17},{17,1},{2,18},{18,2},{3,19},{19,3},{4,20},{20... | collective-permute-start | bytes 3145736 | tf_op jit(solution)/shard_map/ppermute | solution.py:949
  456.8 107.1 %collective-permute-start.57 = (bf16[1024,512]{1,0:T(8,128)(2,1)S(1)}, bf16[1024,512]{1,0:T(8,128)(2,1)}, u32[]{:S(2)}, u32[]{:S(2)}) collective-permute-start(bf16[1024,512]{1,0:T(8,128)(2,1)S(1)} %bitcast.124), channel_id=1, source_target_pairs={{0,16},{16,0},{1,17},{17,1},{2,18},{18,2},{3,19},{19,3},{4,20},{20... | collective-permute-start | bytes 3145736 | tf_op jit(solution)/shard_map/ppermute | solution.py:949
  461.8 28.2 %all-to-all-start.2 = ((bf16[4,160,512]{2,1,0:T(8,128)(2,1)}), bf16[4,160,512]{2,1,0:T(8,128)(2,1)S(1)}, u32[]{:S(2)}, u32[]{:S(2)}) async-start(bf16[4,160,512]{2,1,0:T(8,128)(2,1)} %bitcast.137), calls=%async_computation.2 | async-start | bytes 1310720 | tf_op jit(solution)/shard_map/all_to_all | solution.py:817
  487.9 35.3 %collective-permute-start.52 = (bf16[512,512]{1,0:T(8,128)(2,1)}, bf16[512,512]{1,0:T(8,128)(2,1)}, u32[]{:S(2)}, u32[]{:S(2)}) collective-permute-start(bf16[512,512]{1,0:T(8,128)(2,1)} %get-tuple-element.180), channel_id=1, source_target_pairs={{0,8},{8,0},{1,9},{9,1},{2,10},{10,2},{3,11},{11,3},{4,12},{12,4},... | collective-permute-start | bytes 1572872 | tf_op jit(solution)/shard_map/ppermute | solution.py:949
  489.4 33.8 %collective-permute-start.51 = (bf16[512,512]{1,0:T(8,128)(2,1)}, bf16[512,512]{1,0:T(8,128)(2,1)}, u32[]{:S(2)}, u32[]{:S(2)}) collective-permute-start(bf16[512,512]{1,0:T(8,128)(2,1)} %get-tuple-element.176.refs_22_), channel_id=1, source_target_pairs={{0,16},{16,0},{1,17},{17,1},{2,18},{18,2},{3,19},{19,3},{4,20},{20... | collective-permute-start | bytes 1572872 | tf_op jit(solution)/shard_map/ppermute | solution.py:949
  492.9 35.9 %all-to-all-start.3 = ((bf16[4,160,512]{2,1,0:T(8,128)(2,1)}), bf16[4,160,512]{2,1,0:T(8,128)(2,1)S(1)}, u32[]{:S(2)}, u32[]{:S(2)}) async-start(bf16[4,160,512]{2,1,0:T(8,128)(2,1)} %bitcast.136), calls=%async_computation.3 | async-start | bytes 1310720 | tf_op jit(solution)/shard_map/all_to_all | solution.py:824
  532.1 32.4 %all-to-all-start.4 = ((bf16[4,256,512]{2,1,0:T(8,128)(2,1)}), bf16[4,256,512]{2,1,0:T(8,128)(2,1)S(1)}, u32[]{:S(2)}, u32[]{:S(2)}) async-start(bf16[4,256,512]{2,1,0:T(8,128)(2,1)} %bitcast.129), calls=%async_computation.4 | async-start | bytes 2097152 | tf_op jit(solution)/shard_map/all_to_all | solution.py:817
  567.8 55.8 %all-to-all-start.5 = ((bf16[4,256,512]{2,1,0:T(8,128)(2,1)}), bf16[4,256,512]{2,1,0:T(8,128)(2,1)S(1)}, u32[]{:S(2)}, u32[]{:S(2)}) async-start(bf16[4,256,512]{2,1,0:T(8,128)(2,1)} %bitcast.128), calls=%async_computation.5 | async-start | bytes 2097152 | tf_op jit(solution)/shard_map/all_to_all | solution.py:824
  572.2 24.3 %collective-permute-start.56 = (bf16[256,1024]{1,0:T(8,128)(2,1)}, bf16[256,1024]{1,0:T(8,128)(2,1)}, u32[]{:S(2)}, u32[]{:S(2)}) collective-permute-start(bf16[256,1024]{1,0:T(8,128)(2,1)} %get-tuple-element.187), channel_id=1, source_target_pairs={{0,16},{16,0},{1,17},{17,1},{2,18},{18,2},{3,19},{19,3},{4,20},{20... | collective-permute-start | bytes 1572872 | tf_op jit(solution)/shard_map/ppermute | solution.py:949
  573.7 24.4 %collective-permute-start.55 = (bf16[768,512]{1,0:T(8,128)(2,1)}, bf16[768,512]{1,0:T(8,128)(2,1)}, u32[]{:S(2)}, u32[]{:S(2)}) collective-permute-start(bf16[768,512]{1,0:T(8,128)(2,1)} %get-tuple-element.186), channel_id=1, source_target_pairs={{0,8},{8,0},{1,9},{9,1},{2,10},{10,2},{3,11},{11,3},{4,12},{12,4},... | collective-permute-start | bytes 2359304 | tf_op jit(solution)/shard_map/ppermute | solution.py:949
  577.4 57.0 %collective-permute-start.65 = (bf16[1024,512]{1,0:T(8,128)(2,1)S(1)}, bf16[1024,512]{1,0:T(8,128)(2,1)}, u32[]{:S(2)}, u32[]{:S(2)}) collective-permute-start(bf16[1024,512]{1,0:T(8,128)(2,1)S(1)} %bitcast.127), channel_id=1, source_target_pairs={{0,1},{1,0},{2,3},{3,2},{4,5},{5,4},{6,7},{7,6},{8,9},{9,8},{10,11... | collective-permute-start | bytes 3145736 | tf_op jit(solution)/shard_map/ppermute | solution.py:949
  577.4 57.0 %collective-permute-start.66 = (bf16[1024,512]{1,0:T(8,128)(2,1)}, bf16[1024,512]{1,0:T(8,128)(2,1)}, u32[]{:S(2)}, u32[]{:S(2)}) collective-permute-start(bf16[1024,512]{1,0:T(8,128)(2,1)} %collective-permute-done.57.refs_2_), channel_id=1, source_target_pairs={{0,1},{1,0},{2,3},{3,2},{4,5},{5,4},{6,7},{7,6},{8,9},{9,8},{10,11... | collective-permute-start | bytes 3145736 | tf_op jit(solution)/shard_map/ppermute | solution.py:949
  595.9 20.8 %collective-permute-start.61 = (bf16[640,512]{1,0:T(8,128)(2,1)S(1)}, bf16[640,512]{1,0:T(8,128)(2,1)}, u32[]{:S(2)}, u32[]{:S(2)}) collective-permute-start(bf16[640,512]{1,0:T(8,128)(2,1)S(1)} %bitcast.134), channel_id=1, source_target_pairs={{0,16},{16,0},{1,17},{17,1},{2,18},{18,2},{3,19},{19,3},{4,20},{20... | collective-permute-start | bytes 1966088 | tf_op jit(solution)/shard_map/ppermute | solution.py:949
  601.6 22.0 %collective-permute-start.59 = (bf16[384,512]{1,0:T(8,128)(2,1)}, bf16[384,512]{1,0:T(8,128)(2,1)S(1)}, u32[]{:S(2)}, u32[]{:S(2)}) collective-permute-start(bf16[384,512]{1,0:T(8,128)(2,1)} %get-tuple-element.197.refs_3_), channel_id=1, source_target_pairs={{0,16},{16,0},{1,17},{17,1},{2,18},{18,2},{3,19},{19,3},{4,20},{20... | collective-permute-start | bytes 1179656 | tf_op jit(solution)/shard_map/ppermute | solution.py:949
  627.1 22.7 %all-to-all-start.6 = ((bf16[4,160,512]{2,1,0:T(8,128)(2,1)}), bf16[4,160,512]{2,1,0:T(8,128)(2,1)S(1)}, u32[]{:S(2)}, u32[]{:S(2)}) async-start(bf16[4,160,512]{2,1,0:T(8,128)(2,1)} %bitcast.118), calls=%async_computation.6 | async-start | bytes 1310720 | tf_op jit(solution)/shard_map/all_to_all | solution.py:817
  652.7 28.5 %all-to-all-start.7 = ((bf16[4,160,512]{2,1,0:T(8,128)(2,1)}), bf16[4,160,512]{2,1,0:T(8,128)(2,1)S(1)}, u32[]{:S(2)}, u32[]{:S(2)}) async-start(bf16[4,160,512]{2,1,0:T(8,128)(2,1)} %bitcast.117), calls=%async_computation.7 | async-start | bytes 1310720 | tf_op jit(solution)/shard_map/all_to_all | solution.py:824
  680.7 35.5 %collective-permute-start.72 = (bf16[1024,512]{1,0:T(8,128)(2,1)S(1)}, bf16[1024,512]{1,0:T(8,128)(2,1)}, u32[]{:S(2)}, u32[]{:S(2)}) collective-permute-start(bf16[1024,512]{1,0:T(8,128)(2,1)S(1)} %bitcast.116), channel_id=1, source_target_pairs={{0,1},{1,0},{2,3},{3,2},{4,5},{5,4},{6,7},{7,6},{8,9},{9,8},{10,11... | collective-permute-start | bytes 3145736 | tf_op jit(solution)/shard_map/ppermute | solution.py:949
  681.7 27.5 %collective-permute-start.74 = (bf16[640,512]{1,0:T(8,128)(2,1)S(1)}, bf16[640,512]{1,0:T(8,128)(2,1)S(1)}, u32[]{:S(2)}, u32[]{:S(2)}) collective-permute-start(bf16[640,512]{1,0:T(8,128)(2,1)S(1)} %bitcast.120), channel_id=1, source_target_pairs={{0,16},{16,0},{1,17},{17,1},{2,18},{18,2},{3,19},{19,3},{4,20},{20... | collective-permute-start | bytes 1966088 | tf_op jit(solution)/shard_map/ppermute | solution.py:949
  (114 other events, 1141.9 us)

commit v3 on v2

--- a/solution.py
+++ b/solution.py
@@ -361,7 +361,7 @@
     offs_ref, act_ref, aux_ref, slope_ref, us_ref, rim_ref, segx_ref, taps_ref, heads_ref, skip_ref,
     oh_ref, copies_ref, dy_ref, y_ref, dxs_ref, dbc_ref, sout_ref, drow_ref, sin_ref, zloc_ref, dsuf_ref, zdev_ref,
     dum_ref, duo_ref, tail_ref, rimout_ref, tgrad_ref, hgrad_ref,
-    dubuf, dbuf, qhigh, qrest, vhigh, vrest, ebuf, sums, skips,
+    dubuf, dbuf, qhigh, qrest, vbuf, ebuf, sums, skips,
 ):
     i = pl.program_id(0)
     count = pl.num_programs(0)
@@ -393,11 +393,11 @@
         skip = skip_ref[0:1, cols]
         dbuf[0:Q, cols] = (step * dxs + skip * dy) * slope_ref[:, cols].astype(F32)
         qhigh[:, cols], qrest[:, cols] = two_parts(dy * (y_ref[:, cols] - skip * values) - scaled * dxs)
-        vhigh[:, cols], vrest[:, cols] = two_parts(values * dxs)
+        vbuf[:, cols] = (values * dxs).astype(BF16)
         skips[:, cols] += fold_rows(values * dy)
         arrived = zloc_ref[0, :, cols].astype(F32) + dsuf_ref[0, 0:1, cols] * zdev_ref[:, cols].astype(F32)
         leaving = sout_ref[0, :, cols] + drow_ref[0, 2:3, cols] * sin_ref[:, cols]
-        sums[:, cols] = fold_rows(arrived * leaving)
+        sums[:, cols] = jnp.sum((arrived * leaving).reshape(N // 16, 16, LANES), axis=0)
     d_keys = dbc_ref[:, 0:N] + dot_nt(ebuf[...], zdev_ref[...])
     dbuf[0:Q, DI : DI + N] = d_keys * slope_ref[:, DI : DI + N].astype(F32)
     dbuf[0:Q, DI + N :] = dbc_ref[:, N:] * slope_ref[:, DI + N :].astype(F32)
@@ -408,18 +408,20 @@
         high, rest = two_parts(x)
         return dot_nn(high, hot) + dot_nn(rest, hot)
 
-    d_logs = dot_nn(qhigh[...], hot) + dot_nn(qrest[...], hot)
-    d_last = jnp.sum(by_head(sums[...]), axis=0, keepdims=True)
+    stacked = jnp.concatenate([qhigh[...], qrest[...], vbuf[...], *two_parts(sums[...])], axis=0)
+    head_sums = dot_nn(stacked, hot)
+    d_logs = head_sums[:Q] + head_sums[Q : 2 * Q]
+    d_last = jnp.sum(head_sums[3 * Q :], axis=0, keepdims=True)
     rows = lax.broadcasted_iota(jnp.int32, (Q, Q), 0)
     lane = lax.broadcasted_iota(jnp.int32, (Q, Q), 1)
     d_decay = dot_full((rows <= lane).astype(F32), d_logs) + d_last
     raw = dot_nn(us_ref[:, CH:], copies_ref[...]) + heads_ref[0:1, :]
     step = jnp.maximum(raw, 0.0) + jnp.log1p(jnp.exp(-jnp.abs(raw)))
-    d_step = dot_nn(vhigh[...], hot) + dot_nn(vrest[...], hot) - heads_ref[1:2, :] * d_decay
+    d_step = head_sums[2 * Q : 3 * Q] - heads_ref[1:2, :] * d_decay
     d_raw = d_step / (1.0 + jnp.exp(-raw))
-    d_raw = jnp.where(lane < H, d_raw, 0.0).astype(BF16)
-    dum_ref[:, CH // 2 :] = d_raw
-    duo_ref[:, CH // 2 :] = d_raw
+    d_raw = jnp.where(lane < H, d_raw, 0.0)
+    dum_ref[:, CH // 2 :] = d_raw.astype(BF16)
+    duo_ref[:, CH // 2 :] = d_raw.astype(BF16)
     hgrad_ref[0:8, :] += fold_rows(d_raw)
     hgrad_ref[8:16, :] += fold_rows(-(step * d_decay))
 
@@ -646,34 +648,48 @@
         out_ref[k * rows : (k + 1) * rows, :] = total
 
 
-def final_kernel(layer, count, offs_ref, *others):
-    far, near = others[:count], others[count : 2 * count]
-    expand_ref, reduce_ref, zbuf, ubuf, sbuf, rbuf, sems = others[-7:]
-    core, rep, zs, us, rs = offs_ref[7], offs_ref[6], DI // 2, CH // 2, DI // 4
+def placed(offs_ref, parts, mid, buf, k):
+    for h, part in enumerate(parts):
+        at = offs_ref[6] if h == 0 else 1 - offs_ref[6]
+        size = mid // 2
+        buf[k, rows_at(at, size), :] = part[:size, :].astype(F32)
+        buf[k, rows_at(at, part.shape[0] - size, mid), :] = part[size:, :].astype(F32)
+
+
+def send_all(layer, sems, moves):
     copies = []
-
-    def put(src, ref, start, size):
+    for src, ref, start, size in moves:
         copy = pltpu.make_async_copy(src, ref.at[layer, pl.ds(start, size)], sems.at[len(copies)])
         copy.start()
         copies.append(copy)
-
+    for copy in copies:
+        copy.wait()
+
+
+def far_final_kernel(layer, offs_ref, *others):
+    expand_ref, reduce_ref, zbuf, rbuf, sems = others[-5:]
+    core, zs, rs = offs_ref[7], DI // 2, DI // 4
+    moves = []
     for k in range(2):
         which = core if k == 0 else 1 - core
-        for h in range(2):
-            at = rep if h == 0 else 1 - rep
-            for buf, part, mid in ((zbuf, far[2 * k + h], FAR_MID), (ubuf, near[2 * k + h], NEAR_MID)):
-                size = mid // 2
-                buf[k, rows_at(at, size), :] = part[:size, :].astype(F32)
-                buf[k, rows_at(at, part.shape[0] - size, mid), :] = part[size:, :].astype(F32)
+        placed(offs_ref, others[2 * k : 2 * k + 2], FAR_MID, zbuf, k)
         for q in range(2):
             rbuf[k, :, 512 * q : 512 * (q + 1)] = zbuf[k, zs + rs * q : zs + rs * (q + 1), :]
-        put(rbuf.at[k], reduce_ref, pl.multiple_of(which * rs, LANES), rs)
-        put(zbuf.at[k, pl.ds(0, zs)], expand_ref, pl.multiple_of(which * zs, LANES), zs)
-        put(ubuf.at[k, pl.ds(0, us)], expand_ref, pl.multiple_of(DI + which * us, LANES), us)
-    sbuf[...] = ubuf[0, us : us + H, :]
-    put(sbuf, expand_ref, DI + CH, H)
-    for copy in copies:
-        copy.wait()
+        moves.append((rbuf.at[k], reduce_ref, pl.multiple_of(which * rs, LANES), rs))
+        moves.append((zbuf.at[k, pl.ds(0, zs)], expand_ref, pl.multiple_of(which * zs, LANES), zs))
+    send_all(layer, sems, moves)
+
+
+def near_final_kernel(layer, offs_ref, *others):
+    expand_ref, ubuf, sems = others[-3:]
+    core, us = offs_ref[7], CH // 2
+    moves = []
+    for k in range(2):
+        which = core if k == 0 else 1 - core
+        placed(offs_ref, others[2 * k : 2 * k + 2], NEAR_MID, ubuf, k)
+        moves.append((ubuf.at[k, pl.ds(0, us)], expand_ref, pl.multiple_of(DI + which * us, LANES), us))
+    moves.append((ubuf.at[0, pl.ds(us, H)], expand_ref, DI + CH, H))
+    send_all(layer, sems, moves)
 
 
 def whole(shape):
@@ -697,7 +713,7 @@
 COST = {
     "expand_first": 8, "ssd_front": 13, "expand_rest": 6, "ssd_within": 11, "ssd_gate": 13, "gate_back": 15,
     "within_back": 17, "ssd_last": 24, "input_back": 16, "far_grads": 12, "near_grads": 6, "take": 1, "cross": 4, "meet": 3, "reduce_parts": 2,
-    "final_grads": 8,
+    "far_final": 6, "near_final": 4,
 }
 
 
@@ -769,18 +785,25 @@
     )(offs, dzm, dzo, dum, duo, gain, resid, grad, own, *near, *far)
 
 
-def final_grads(offs, far, near, layer, held, deps=()):
-    n = 1 + len(far) + len(near)
+def far_final(offs, parts, layer, held, deps=()):
+    n = 1 + len(parts)
     return call(
-        functools.partial(final_kernel, layer, len(far)), 1,
-        [SCALARS] + [whole(p.shape) for p in (*far, *near)] + [ANYWHERE] * len(held),
-        [ANYWHERE, ANYWHERE],
+        functools.partial(far_final_kernel, layer), 1,
+        [SCALARS] + [whole(p.shape) for p in parts] + [ANYWHERE] * len(held), [ANYWHERE, ANYWHERE],
         [struct((LAYERS, E, D // 2), F32), struct((LAYERS, DI // 2, D), F32)],
-        [pltpu.VMEM((2, DI, D // 2), F32), pltpu.VMEM((2, HALF, D // 2), F32),
-         pltpu.VMEM((H, D // 2), F32), pltpu.VMEM((2, DI // 4, D), F32), pltpu.SemaphoreType.DMA((7,))],
-        "final_grads", deps,
-        aliases={n + k: k for k in range(len(held))},
-    )(offs, *far, *near, *held)
+        [pltpu.VMEM((2, DI, D // 2), F32), pltpu.VMEM((2, DI // 4, D), F32), pltpu.SemaphoreType.DMA((4,))],
+        "far_final", deps, aliases={n + k: k for k in range(len(held))},
+    )(offs, *parts, *held)
+
+
+def near_final(offs, parts, layer, held, deps=()):
+    n = 1 + len(parts)
+    return call(
+        functools.partial(near_final_kernel, layer), 1,
+        [SCALARS] + [whole(p.shape) for p in parts] + [ANYWHERE], ANYWHERE, struct((LAYERS, E, D // 2), F32),
+        [pltpu.VMEM((2, HALF, D // 2), F32), pltpu.SemaphoreType.DMA((3,))],
+        "near_final", deps, aliases={n: 0},
+    )(offs, *parts, held)
 
 
 class Sum:
@@ -938,8 +961,8 @@
          whole((24, LANES))],
         [struct((T, HALF), BF16)] * 2 + [struct((8, CH), F32), struct((8, CH), BF16),
          struct((40, CH), F32), struct((24, LANES), F32)],
-        [pltpu.VMEM((Q, CH), BF16), pltpu.VMEM((Q + 8, CH), F32)] + [pltpu.VMEM((Q, DI), BF16)] * 5
-        + [pltpu.VMEM((8, DI), F32), pltpu.VMEM((8, DI), F32)],
+        [pltpu.VMEM((Q, CH), BF16), pltpu.VMEM((Q + 8, CH), F32)] + [pltpu.VMEM((Q, DI), BF16)] * 4
+        + [pltpu.VMEM((16, DI), F32), pltpu.VMEM((8, DI), F32)],
         "ssd_last", deps,
     )(offs, act, aux, slope, us, rim, segx, taps, heads, skip, oh, copies, dy, y, dxs, dbc, sout, drow, s_in,
       zloc, dsuf, zdev)
@@ -1105,12 +1128,33 @@
     def pad(x, width):
         return jnp.pad(x, ((0, 0), (0, 0), (0, width - x.shape[-1])))
 
+    expand_t = jnp.swapaxes(expand_weight, 1, 2)
+    quarter = D // 4
+
+    def offsets(size):
+        start, away = fsdp * size, (1 - fsdp) * size
+        zero = jnp.zeros_like(core)
+        return jnp.stack(
+            [start, away + core * (size // 2), away + (1 - core) * (size // 2), zero, zero, zero, rep, core]
+        ).astype(jnp.int32)
+
+    offs, wide_offs = offsets(D // 2), offsets(DI // 2)
+
+    def take_lanes(layer, start, rows, deps):
+        size = 512
+        return call(
+            functools.partial(take_kernel, True), -(-rows // size),
+            [SCALARS, pl.BlockSpec((1, size, D // 2), lambda i: (layer, start // size + i, 0))],
+            by_rows((size, quarter)), struct((rows, quarter), BF16), [], "take", deps,
+        )(offs, expand_t)
+
+    first_taken = take_lanes(0, DI, US, ())
     heads_packed = jnp.concatenate([step_bias, decay_rate, skip_gain], axis=-1)
     own = jnp.concatenate(
         [filter_taps, filter_offset[:, None], pad(norm_gain[:, None], CH // 2),
          pad(gate_gain[:, None], CH // 2), pad(heads_packed[:, None], CH // 2)], axis=1
     )
-    other = swap(own, "fsdp")
+    other = swap(following(own, first_taken), "fsdp")
     lead = fsdp == 0
     low_half = jnp.where(lead, own, other).astype(F32)
     high_half = jnp.where(lead, other, own).astype(F32)
@@ -1148,26 +1192,6 @@
     segx = jnp.broadcast_to(seg_line[:, None], (T + 16, LANES))
     segr = jnp.broadcast_to(seg_line[8 : 8 + T].reshape(T // Q, 1, Q), (T // Q, 8, Q))
 
-    expand_t = jnp.swapaxes(expand_weight, 1, 2)
-    quarter = D // 4
-
-    def offsets(size):
-        start, away = fsdp * size, (1 - fsdp) * size
-        zero = jnp.zeros_like(core)
-        return jnp.stack(
-            [start, away + core * (size // 2), away + (1 - core) * (size // 2), zero, zero, zero, rep, core]
-        ).astype(jnp.int32)
-
-    offs, wide_offs = offsets(D // 2), offsets(DI // 2)
-
-    def take_lanes(layer, start, rows, deps):
-        size = 512
-        return call(
-            functools.partial(take_kernel, True), -(-rows // size),
-            [SCALARS, pl.BlockSpec((1, size, D // 2), lambda i: (layer, start // size + i, 0))],
-            by_rows((size, quarter)), struct((rows, quarter), BF16), [], "take", deps,
-        )(offs, expand_t)
-
     def take_rows(layer, deps):
         return call(
             functools.partial(take_kernel, False), 1,
@@ -1175,34 +1199,37 @@
             whole((DI // 4, D)), struct((DI // 4, D), BF16), [], "take", deps,
         )(offs, reduce_weight)
 
-    first_taken = take_lanes(0, DI, US, ())
-
-    def fetch_layer(layer, after_near=(), after_far=(), after_rows=()):
-        near = first_taken if layer == 0 else take_lanes(layer, DI, US, after_near)
+
+    def fetch_layer(layer, near, after_far=(), after_rows=()):
         far = take_lanes(layer, 0, DI, after_far + (near,))
         rows_of = take_rows(layer, after_rows + (far,))
-        return fetch(near), fetch(far), fetch(rows_of)
-
-    weights = [fetch_layer(0)]
+        return fetch(far), fetch(rows_of)
+
+    weights = [(fetch(first_taken),) + fetch_layer(0, first_taken)]
 
     resid = gather_tokens(following(tokens, first_taken)).astype(F32)
-    grad = gather_tokens(cotangent).astype(F32)
     saved, out_both = [], ()
     for layer in range(LAYERS):
         near, far, rows_of = weights[layer]
         us, normed = expand_first(offs, resid, norm_all[layer][None], expand_t, near, layer)
         rim = us[T - 8 :, :CH]
-        rim = next_piece(following(rim, far[0]) if layer else rim)
+        rim = next_piece(following(rim, far_cotangent) if layer else rim)
         taps, heads = taps_all[layer], heads_all[layer]
         skip = skip_rows[layer][None]
-        act, slope, aux, lt, drow, sout, msg = ssd_front(us, rim, segx, taps, heads, hot_t, copies, out_both[1:])
+        next_taken = (take_lanes(layer + 1, DI, US, (us,)),) if layer + 1 < LAYERS else ()
+        act, slope, aux, lt, drow, sout, msg = ssd_front(us, rim, segx, taps, heads, hot_t, copies, out_both[1:] + next_taken)
         z = expand_rest(offs, normed, expand_t, far, layer, (act,))
-        s_in, decays = carry_forward(core, following(msg, rows_of[0]) if layer else msg)
+        s_in, decays = carry_forward(core, following(msg, far[0]) if layer else msg)
         normed_both = normed, swap(normed, "core")
-        within_deps = (normed_both[1], grad) if layer else normed_both[1:]
+        within_deps = normed_both[1:]
+        if layer == 0:
+            far_cotangent = gather_tokens(following(cotangent, s_in))
+            grad = far_cotangent.astype(F32)
+        else:
+            within_deps += (rows_of[0],)
         yloc = ssd_within(act, aux, lt, segx, segr, sout, skip, within_deps)
         if layer + 1 < LAYERS:
-            weights.append(fetch_layer(layer + 1, (us,), (act,), (yloc,)))
+            weights.append((fetch(next_taken[0]),) + fetch_layer(layer + 1, next_taken[0], (act,), (yloc,)))
         gain = gate_all[layer][None]
         y, out_mine, out_other, resid_next = ssd_gate(
             wide_offs, yloc, aux, drow, s_in, act, z, gain, resid, reduce_weight, rows_of, layer
@@ -1226,7 +1253,9 @@
             wide_offs, grad, y, z, gain, act, aux, drow, reduce_weight, rows_of, layer, pending
         )
         arrived = near_sums[1].cross((gmsg,)) if first else ()
-        zdev = carry_backward(core, following(gmsg, *arrived), decays)
+        if first:
+            gmsg = following(gmsg, *arrived, far_sums[1].mine)
+        zdev = carry_backward(core, gmsg, decays)
         far_args = (dzm, swap(dzo, "core"), *normed_both, *out_both, grad_low, swap(grad_low, "core"))
         far_sums[layer] = Sum(offs, "far_grads", far_grads_kernel, far_args, FAR_MID, arrived)
         before = (far_sums[layer].own,)
@@ -1240,19 +1269,24 @@
             offs, act, aux, slope, us, rim, segx, taps, heads, skip, hot, copies, dy, y, dxs, dbc, sout, drow, s_in,
             zloc, dsuf, zdev, before
         )
-        token = far_sums[layer].meet((dum,)) + ((near_sums[1].mine,) if first else (layer_out[0],))
+        token = (near_sums[1].mine,) if first else far_sums[1].meet((dum,)) + (layer_out[0],)
         rimout = following(rimout, *token)
         tail = (tail + next_piece(rimout, True).astype(F32)).astype(BF16)
         tail_mine, tail_other = halves(tail, core, 1)
         dum = lax.dynamic_update_slice(dum, tail_mine, (T - 8, 0))
         duo = lax.dynamic_update_slice(duo, tail_other, (T - 8, 0))
         near_args = (dum, swap(duo, "core"), *normed_both)
+        if first:
+            token = far_sums[0].meet(near_args[1:2])
+            near_sums[0] = Sum(offs, "near_grads", near_grads_kernel, near_args, NEAR_MID, token)
+            token = (near_sums[0].own,)
         grad, ngrad = input_back(
             offs, dzm, dzo, dum, duo, norm_all[layer][None], resid_in, grad, expand_t, near, far, layer, token
         )
-        near_sums[layer] = Sum(offs, "near_grads", near_grads_kernel, near_args, NEAR_MID, (grad,))
         if not first:
-            pending = far_sums[1].reduce((near_sums[1].own,))
+            token = far_sums[1].reduce((grad,))
+            near_sums[1] = Sum(offs, "near_grads", near_grads_kernel, near_args, NEAR_MID, token)
+            pending = (near_sums[1].own,)
         tgrad = jnp.sum(tgrad.reshape(5, 8, CH), axis=1).reshape(-1)
         hgrad = jnp.sum(hgrad.reshape(3, 8, LANES), axis=1)[:, :H].reshape(-1)
         small[layer] = jnp.concatenate([tgrad, jnp.sum(ggrad, axis=0), jnp.sum(ngrad, axis=0), hgrad])
@@ -1260,31 +1294,32 @@
     size = small[0].shape[0]
     padded_size = -(-size // 1024) * 1024
     packed = jnp.pad(jnp.stack(small), ((0, 0), (0, padded_size - size))).reshape(-1, LANES)
-    hops = [("core", 1), ("fsdp", 1)] + levels()
+    hops = [("core", 1)] + levels() + [("fsdp", 1)]
 
     def hop(packed):
         axis, bit = hops.pop(0)
         return packed + flip(packed, axis, bit)
 
     far_other = swap(far_sums[1].mine, "rep")
-    token = far_sums[0].reduce((near_sums[0].own, far_other))
+    token = far_sums[0].reduce((grad, far_other))
     packed = hop(packed)
     token = near_sums[0].cross(token + (packed,))
     near_other = swap(near_sums[1].mine, "rep")
     packed = hop(packed)
     token = near_sums[0].meet(token + (far_sums[0].mine, near_other, packed))
-    mid = far_sums[0].mine.shape[0] // 2
-    other_a = swap(far_sums[0].mine[:mid], "rep")
-    grads = final_grads(offs, far_sums[1].spread(far_other), near_sums[1].spread(near_other), 1, (), token)
+    first_other = swap(far_sums[0].mine, "rep")
+    expand_sum, reduce_sum = far_final(offs, far_sums[1].spread(far_other), 1, (), token)
+    expand_sum = near_final(offs, near_sums[1].spread(near_other), 1, expand_sum)
     packed = hop(packed)
-    token = near_sums[0].reduce(token + (other_a, packed, grads[0]))
-    other_b = swap(far_sums[0].mine[mid:], "rep")
+    token = near_sums[0].reduce(token + (first_other, packed, expand_sum))
     packed = hop(packed)
+    expand_sum, reduce_sum = far_final(
+        offs, far_sums[0].spread(first_other), 0, (expand_sum, reduce_sum), token + (packed,)
+    )
     token_grads = scatter_tokens(following(grad.astype(BF16), near_sums[0].mine))
-    far_first = far_sums[0].spread(jnp.concatenate([other_a, other_b], axis=0))
     while hops:
         packed = hop(packed)
-    grads = final_grads(offs, far_first, near_sums[0].spread(), 0, grads)
+    expand_sum = near_final(offs, near_sums[0].spread(), 0, expand_sum)
     packed = packed.reshape(LAYERS, padded_size)
 
     def own_half(x):
@@ -1304,8 +1339,8 @@
     return (
         layer_out,
         token_grads,
-        jnp.swapaxes(grads[0], 1, 2),
-        grads[1],
+        jnp.swapaxes(expand_sum, 1, 2),
+        reduce_sum,
         tap_grads,
         offset_grads,
         step_grads,

time: 734 us -> 703 us (0.958)
  waiting for transfers between devices: 132 us -> 110 us
    ppermute x5, waiting for transfers between devices: 48 us -> 17 us  [flip(): return lax.ppermute(value, axis, [(i, i ^ bit) for i in range(size)])]
    all_to_all x4, waiting for transfers between devices: 2.47 us -> 14.4 us  [meet(): self.parts = lax.all_to_all(total, 'zz', 0, 0, tiled=True)]
    ppermute x58 -> x57, waiting for transfers between devices: 52.2 us -> 40.4 us  [swap(): return lax.ppermute(value, axis, [(0, 1), (1, 0)])]
    ppermute x58 -> x57, starting transfers between devices: 51.2 us -> 46.8 us  [swap(): return lax.ppermute(value, axis, [(0, 1), (1, 0)])]
    pallas_call x42 -> x44, Pallas kernels: 365 us -> 367 us  [call(): return lambda *args: run(*args, *deps)]
    unnamed x153 -> x164, local copies, waits for them, and re-layouts: 19 us -> 20.8 us
  transfers between devices with their start and end apart: 87 -> 86, of which waited for: 22 -> 23; matrix products, arithmetic and copies ran while one was open for 8% -> 6% of each run, Pallas kernels for 44% -> 48%
where the time goes in v3:
time: 703 us; the launch traced here: 693 us
  Pallas kernels  367 us (52%)
  starting transfers between devices  131 us (19%)
  waiting for transfers between devices  110 us (16%)
  local copies, waits for them, and re-layouts  41.8 us (6%)
  other arithmetic  28.1 us (4%)
  between operations  15.7 us (2%)
    pallas_call x44, Pallas kernels, call(): return lambda *args: run(*args, *deps)  367 us
    ppermute x57, starting transfers between devices, swap(): return lax.ppermute(value, axis, [(0, 1), (1, 0)])  46.8 us
    ppermute x57, waiting for transfers between devices, swap(): return lax.ppermute(value, axis, [(0, 1), (1, 0)])  40.4 us
    all_to_all x4, starting transfers between devices, meet(): self.parts = lax.all_to_all(total, 'zz', 0, 0, tiled=True)  23.6 us
    unnamed x164, local copies, waits for them, and re-layouts  20.8 us
    all_to_all x4, starting transfers between devices, reduce(): self.mine = lax.all_to_all(copies, 'zz', 0, 0, tiled=True)  18.1 us
    ppermute x5, waiting for transfers between devices, flip(): return lax.ppermute(value, axis, [(i, i ^ bit) for i in range(size)])  17 us
    all_to_all x4, waiting for transfers between devices, meet(): self.parts = lax.all_to_all(total, 'zz', 0, 0, tiled=True)  14.4 us
  transfers between devices with their start and end apart: 86, of which 23 were waited for; matrix products, arithmetic and copies ran while one was open for 6% of the time, Pallas kernels for 48%

profile of v3, /device:TPU:0, one launch (start us, length us, event | category | flops | bytes accessed | tf_op | source)
XLA Modules:
  0.0 692.7 jit_solution(15158247927802591045)
XLA Ops:
  1.4 4.3 take.6.refs_2_
  12.4 4.8 collective-permute-start.1
  26.8 10.0 %collective-permute-done.2 = bf16[2,8,1152]{2,0,1:T(2,128)(2,1)S(1)} collective-permute-done((bf16[2,8,1152]{2,0,1:T(2,128)(2,1)S(1)}, bf16[2,8,1152]{2,0,1:T(2,128)(2,1)S(1)}, u32[]{:S(2)}, u32[]{:S(2)}) %collective-permute-start.2) | collective-permute-done | bytes 36896 | tf_op jit(solution)/shard_map/ppermute | solution.py:972
  43.1 8.4 %expand_first.2 = (bf16[512,2336]{1,0:T(8,128)(2,1)}, bf16[512,1024]{1,0:T(8,128)(2,1)}) custom-call(s32[8]{0:T(128)} %stack.71.refs_0_, f32[512,1024]{1,0:T(8,128)} %maximum_convert_fusion.refs_1_.refs_9_.refs_6_, f32[1,1024]{1,0:T(1,128)} %get-tuple-element.253.refs_2_.refs_5_, bf16[2,4384,512]{2,1,0:T(8,128)(2,1)} %bitcast.105, ...), custom_call_target="tpu_custom_call" | custom-call | flops 8800000000 | bytes 1000 | tf_op jit(solution)/shard_map/expand_first/pallas_call | solution.py:742
  59.8 13.6 %ssd_front.2 = (bf16[512,2560]{1,0:T(8,128)(2,1)}, bf16[512,2304]{1,0:T(8,128)(2,1)}, f32[512,128]{1,0:T(8,128)}, f32[4,32,128]{2,1,0:T(8,128)}, f32[4,8,2048]{2...) custom-call(bf16[512,2336]{1,0:T(8,128)(2,1)} %get-tuple-element.107.refs_2_.refs_0_.refs_4_, ...), custom_call_target="tpu_custom_call" | custom-call | flops 14300000256 | bytes 1000 | tf_op jit(solution)/shard_map/ssd_front/pallas_call | solution.py:742
  91.8 6.2 expand_rest.2.refs_7_.refs_3_
  97.9 5.3 collective-permute-done.8
  103.9 10.9 %ssd_within.2.refs_1_.refs_2_ = f32[512,2048]{1,0:T(8,128)} custom-call(bf16[512,2560]{1,0:T(8,128)(2,1)} %get-tuple-element.108.refs_0_.refs_5_.refs_6_.refs_2_.refs_1_, f32[512,128]{1,0:T(8,128)} %get-tuple-element.109.refs_1_.refs_2_.refs_6_, f32[4,32,128]{2,1,0:T(8,128)} %get-tuple-element.110.refs_2_, ...), custom_call_target="tpu_custom_call" | custom-call | flops 12099999744 | bytes 1000 | tf_op jit(solution)/shard_map/ssd_within/pallas_call | solution.py:742
  121.1 13.5 %ssd_gate.2 = (f32[512,2048]{1,0:T(8,128)}, bf16[512,1024]{1,0:T(8,128)(2,1)}, bf16[512,1024]{1,0:T(8,128)(2,1)}, f32[512,1024]{1,0:T(8,128)}) custom-call(s32[8]{0:T(128)} %stack.67.refs_0_, f32[512,2048]{1,0:T(8,128)} %ssd_within.2.refs_1_.refs_2_, f32[512,128]{1,0:T(8,128)} %get-tuple-element.109.refs_1_.refs_2_.refs_6_, ...), custom_call_target="tpu_custom_call" | custom-call | flops 14300000256 | bytes 1000 | tf_op jit(solution)/shard_map/ssd_gate/pallas_call | solution.py:742
  139.5 8.4 %expand_first.3 = (bf16[512,2336]{1,0:T(8,128)(2,1)}, bf16[512,1024]{1,0:T(8,128)(2,1)}) custom-call(s32[8]{0:T(128)} %stack.71.refs_0_, f32[512,1024]{1,0:T(8,128)} %get-tuple-element.115.refs_1_.refs_9_.refs_6_, f32[1,1024]{1,0:T(1,128)} %get-tuple-element.252.refs_2_.refs_5_, bf16[2,4384,512]{2,1,0:T(8,128)(2,1)} %bitcast.109, ...), custom_call_target="tpu_custom_call" | custom-call | flops 8800000000 | bytes 1000 | tf_op jit(solution)/shard_map/expand_first/pallas_call | solution.py:742
  160.3 13.5 %ssd_front.3 = (bf16[512,2560]{1,0:T(8,128)(2,1)}, bf16[512,2304]{1,0:T(8,128)(2,1)}, f32[512,128]{1,0:T(8,128)}, f32[4,32,128]{2,1,0:T(8,128)}, f32[4,8,2048]{2...) custom-call(bf16[512,2336]{1,0:T(8,128)(2,1)} %get-tuple-element.116.refs_0_.refs_4_, ...), custom_call_target="tpu_custom_call" | custom-call | flops 14300000256 | bytes 1000 | tf_op jit(solution)/shard_map/ssd_front/pallas_call | solution.py:742
  184.8 6.2 expand_rest.3.refs_7_.refs_3_
  191.0 5.2 collective-permute-done.24
  197.2 10.9 %ssd_within.3.refs_1_ = f32[512,2048]{1,0:T(8,128)} custom-call(bf16[512,2560]{1,0:T(8,128)(2,1)} %get-tuple-element.118.refs_0_.refs_5_.refs_6_.refs_1_, f32[512,128]{1,0:T(8,128)} %get-tuple-element.119.refs_1_.refs_2_.refs_6_, f32[4,32,128]{2,1,0:T(8,128)} %get-tuple-element.120.refs_2_, f32[528,128]{1,0:T(8,128)} %broadcast_in_dim.48.refs_2_.refs_3_.refs_6_, ...), custom_call_target="tpu_custom_call" | custom-call | flops 12099999744 | bytes 1000 | tf_op jit(solution)/shard_map/ssd_within/pallas_call | solution.py:742
  209.2 13.6 %ssd_gate.3 = (f32[512,2048]{1,0:T(8,128)}, bf16[512,1024]{1,0:T(8,128)(2,1)}, bf16[512,1024]{1,0:T(8,128)(2,1)}, f32[512,1024]{1,0:T(8,128)}) custom-call(s32[8]{0:T(128)} %stack.67.refs_0_, f32[512,2048]{1,0:T(8,128)} %ssd_within.3.refs_1_, f32[512,128]{1,0:T(8,128)} %get-tuple-element.119.refs_1_.refs_2_.refs_6_, ...), custom_call_target="tpu_custom_call" | custom-call | flops 14300000256 | bytes 1000 | tf_op jit(solution)/shard_map/ssd_gate/pallas_call | solution.py:742
  229.4 15.7 %gate_back.2 = (bf16[512,2048]{1,0:T(8,128)(2,1)}, bf16[512,2048]{1,0:T(8,128)(2,1)}, bf16[512,1024]{1,0:T(8,128)(2,1)}, bf16[512,1024]{1,0:T(8,128)(2,1)}, f32[...) custom-call(s32[8]{0:T(128)} %stack.67.refs_0_, ...), custom_call_target="tpu_custom_call" | custom-call | flops 16499999744 | bytes 1000 | tf_op jit(solution)/shard_map/gate_back/pallas_call | solution.py:742
  248.6 4.7 collective-permute-done.29
  259.6 11.6 %far_grads.2 = (bf16[2048,512]{1,0:T(8,128)(2,1)}, bf16[2048,512]{1,0:T(8,128)(2,1)}, bf16[1024,512]{1,0:T(8,128)(2,1)}, bf16[512,1024]{1,0:T(8,128)(2,1)}) custom-call(s32[8]{0:T(128)} %stack.71.refs_0_, bf16[512,1024]{1,0:T(8,128)(2,1)} %get-tuple-element.128.refs_1_, bf16[512,1024]{1,0:T(8,128)(2,1)} %copy-done.62, ...), custom_call_target="tpu_custom_call" | custom-call | flops 13200000000 | bytes 1000 | tf_op jit(solution)/shard_map/far_grads/pallas_call | solution.py:742
  274.3 17.6 %within_back.2 = (f32[512,2048]{1,0:T(8,128)}, f32[512,256]{1,0:T(8,128)}) custom-call(bf16[512,2560]{1,0:T(8,128)(2,1)} %get-tuple-element.118.refs_0_.refs_5_.refs_6_.refs_1_, f32[512,128]{1,0:T(8,128)} %get-tuple-element.119.refs_1_.refs_2_.refs_6_, f32[4,32,128]{2,1,0:T(8,128)} %get-tuple-element.120.refs_2_, ...), custom_call_target="tpu_custom_call" | custom-call | flops 18699999232 | bytes 1000 | tf_op jit(solution)/shard_map/within_back/pallas_call | solution.py:742
  294.4 4.6 cross.4
  301.0 22.6 %ssd_last.2 = (bf16[512,1280]{1,0:T(8,128)(2,1)}, bf16[512,1280]{1,0:T(8,128)(2,1)}, f32[8,2304]{1,0:T(8,128)}, bf16[8,2304]{1,0:T(8,128)(2,1)}, f32[40,2304]{1,0:T(8,128)}, /*index=5*/f32[24,128]{1,0:T(8,128)}) custom-call(s32[8]{0:T(128)} %stack.71.refs_0_, bf16[512,2560]{1,0:T(8,128)(2,1)} %get-tuple-element.118.refs_0_.refs_5_.refs_6_.refs_1_, ...), custom_call_target="tpu_custom_call" | custom-call | flops 26400000000 | bytes 1000 | tf_op jit(solution)/shard_map/ssd_last/pallas_call | solution.py:742
  331.5 9.2 %all-to-all-start = ((bf16[4,256,512]{2,1,0:T(8,128)(2,1)}), bf16[4,256,512]{2,1,0:T(8,128)(2,1)S(1)}, u32[]{:S(2)}, u32[]{:S(2)}) async-start(bf16[4,256,512]{2,1,0:T(8,128)(2,1)} %bitcast.126), calls=%async_computation | async-start | bytes 2097152 | tf_op jit(solution)/shard_map/all_to_all | solution.py:840
  342.4 16.4 %input_back.2 = (f32[512,1024]{1,0:T(8,128)}, f32[8,1024]{1,0:T(8,128)}) custom-call(s32[8]{0:T(128)} %stack.71.refs_0_, bf16[512,1024]{1,0:T(8,128)(2,1)} %get-tuple-element.128.refs_1_, bf16[512,1024]{1,0:T(8,128)(2,1)} %get-tuple-element.129.refs_2_, bf16[512,1280]{1,0:T(8,128)(2,1)} %get-tuple-element.247.refs_3_.refs_1_, bf16[512,1280]{1,0:T(8,128)(2,1)} %copy-done.53, ...), custom_call_target="tpu_custom_call" | custom-call | flops 17600000000 | bytes 1000 | tf_op jit(solution)/shard_map/input_back/pallas_call | solution.py:742
  358.9 8.2 %all-to-all-done.refs_0_ = bf16[4,256,512]{2,1,0:T(8,128)(2,1)S(1)} async-done(((bf16[4,256,512]{2,1,0:T(8,128)(2,1)}), bf16[4,256,512]{2,1,0:T(8,128)(2,1)S(1)}, u32[]{:S(2)}, u32[]{:S(2)}) %all-to-all-start) | async-done | bytes 1048608 | tf_op jit(solution)/shard_map/all_to_all | solution.py:840
  370.4 4.2 all-to-all-start.1
  374.7 7.6 %near_grads.2 = (bf16[1280,512]{1,0:T(8,128)(2,1)}, bf16[1280,512]{1,0:T(8,128)(2,1)}, bf16[768,512]{1,0:T(8,128)(2,1)}, bf16[256,1024]{1,0:T(8,128)(2,1)}) custom-call(s32[8]{0:T(128)} %stack.71.refs_0_, bf16[512,1280]{1,0:T(8,128)(2,1)} %get-tuple-element.247.refs_3_.refs_1_, bf16[512,1280]{1,0:T(8,128)(2,1)} %collective-permute-done.40.refs_2_, ...), custom_call_target="tpu_custom_call" | custom-call | flops 6600000000 | bytes 1000 | tf_op jit(solution)/shard_map/near_grads/pallas_call | solution.py:742
  384.4 15.7 %gate_back.3 = (bf16[512,2048]{1,0:T(8,128)(2,1)}, bf16[512,2048]{1,0:T(8,128)(2,1)}, bf16[512,1024]{1,0:T(8,128)(2,1)}, bf16[512,1024]{1,0:T(8,128)(2,1)}, f32[...) custom-call(s32[8]{0:T(128)} %stack.67.refs_0_, ...), custom_call_target="tpu_custom_call" | custom-call | flops 16499999744 | bytes 1000 | tf_op jit(solution)/shard_map/gate_back/pallas_call | solution.py:742
  417.5 11.5 %far_grads.3 = (bf16[2048,512]{1,0:T(8,128)(2,1)}, bf16[2048,512]{1,0:T(8,128)(2,1)}, bf16[1024,512]{1,0:T(8,128)(2,1)}, bf16[512,1024]{1,0:T(8,128)(2,1)}) custom-call(s32[8]{0:T(128)} %stack.71.refs_0_, bf16[512,1024]{1,0:T(8,128)(2,1)} %get-tuple-element.158.refs_1_, bf16[512,1024]{1,0:T(8,128)(2,1)} %copy-done.59, ...), custom_call_target="tpu_custom_call" | custom-call | flops 13200000000 | bytes 1000 | tf_op jit(solution)/shard_map/far_grads/pallas_call | solution.py:742
  435.3 5.9 all-to-all-start.2
  441.3 17.7 %within_back.3 = (f32[512,2048]{1,0:T(8,128)}, f32[512,256]{1,0:T(8,128)}) custom-call(bf16[512,2560]{1,0:T(8,128)(2,1)} %get-tuple-element.108.refs_0_.refs_5_.refs_6_.refs_2_.refs_1_, f32[512,128]{1,0:T(8,128)} %get-tuple-element.109.refs_1_.refs_2_.refs_6_, f32[4,32,128]{2,1,0:T(8,128)} %get-tuple-element.110.refs_2_, ...), custom_call_target="tpu_custom_call" | custom-call | flops 18699999232 | bytes 1000 | tf_op jit(solution)/shard_map/within_back/pallas_call | solution.py:742
  460.3 4.7 cross.6
  467.9 5.1 all-to-all-start.3
  473.0 22.8 %ssd_last.3 = (bf16[512,1280]{1,0:T(8,128)(2,1)}, bf16[512,1280]{1,0:T(8,128)(2,1)}, f32[8,2304]{1,0:T(8,128)}, bf16[8,2304]{1,0:T(8,128)(2,1)}, f32[40,2304]{1,0:T(8,128)}, /*index=5*/f32[24,128]{1,0:T(8,128)}) custom-call(s32[8]{0:T(128)} %stack.71.refs_0_, bf16[512,2560]{1,0:T(8,128)(2,1)} %get-tuple-element.108.refs_0_.refs_5_.refs_6_.refs_2_.refs_1_, ...), custom_call_target="tpu_custom_call" | custom-call | flops 26400000000 | bytes 1000 | tf_op jit(solution)/shard_map/ssd_last/pallas_call | solution.py:742
  510.9 9.3 %collective-permute-done.54.refs_2_ = bf16[512,512]{1,0:T(8,128)(2,1)} collective-permute-done((bf16[512,512]{1,0:T(8,128)(2,1)S(1)}, bf16[512,512]{1,0:T(8,128)(2,1)}, u32[]{:S(2)}, u32[]{:S(2)}) %collective-permute-start.54) | collective-permute-done | bytes 524320 | tf_op jit(solution)/shard_map/ppermute | solution.py:972
  528.3 7.6 %near_grads.3 = (bf16[1280,512]{1,0:T(8,128)(2,1)}, bf16[1280,512]{1,0:T(8,128)(2,1)}, bf16[768,512]{1,0:T(8,128)(2,1)}, bf16[256,1024]{1,0:T(8,128)(2,1)}) custom-call(s32[8]{0:T(128)} %stack.71.refs_0_, bf16[512,1280]{1,0:T(8,128)(2,1)} %get-tuple-element.245.refs_1_.refs_3_, bf16[512,1280]{1,0:T(8,128)(2,1)} %collective-permute-done.52.refs_3_.refs_2_, ...), custom_call_target="tpu_custom_call" | custom-call | flops 6600000000 | bytes 1000 | tf_op jit(solution)/shard_map/near_grads/pallas_call | solution.py:742
  536.0 16.3 %input_back.3 = (f32[512,1024]{1,0:T(8,128)}, f32[8,1024]{1,0:T(8,128)}) custom-call(s32[8]{0:T(128)} %stack.71.refs_0_, bf16[512,1024]{1,0:T(8,128)(2,1)} %get-tuple-element.158.refs_1_, bf16[512,1024]{1,0:T(8,128)(2,1)} %get-tuple-element.159.refs_2_, bf16[512,1280]{1,0:T(8,128)(2,1)} %get-tuple-element.245.refs_1_.refs_3_, ...), custom_call_target="tpu_custom_call" | custom-call | flops 17600000000 | bytes 1000 | tf_op jit(solution)/shard_map/input_back/pallas_call | solution.py:742
  558.8 5.1 all-to-all-start.5
  566.5 4.5 collective-permute-done.62
  573.6 7.7 %collective-permute-done.64 = f32[240,128]{1,0:T(8,128)S(1)} collective-permute-done((f32[240,128]{1,0:T(8,128)S(1)}, f32[240,128]{1,0:T(8,128)S(1)}, u32[]{:S(2)}, u32[]{:S(2)}) %collective-permute-start.64) | collective-permute-done | bytes 122912 | tf_op jit(solution)/shard_map/ppermute | solution.py:977
  582.8 5.9 collective-permute-start.76
  608.6 4.6 all-to-all-start.6
  613.2 6.4 far_final.2
  619.6 4.2 near_final.2.refs_4_.refs_5_
  623.8 6.2 all-to-all-done.6.refs_0_
  641.9 12.5 %all-to-all-done.7 = bf16[4,160,512]{2,1,0:T(8,128)(2,1)S(1)} async-done(((bf16[4,160,512]{2,1,0:T(8,128)(2,1)}), bf16[4,160,512]{2,1,0:T(8,128)(2,1)S(1)}, u32[]{:S(2)}, u32[]{:S(2)}) %all-to-all-start.7) | async-done | bytes 655392 | tf_op jit(solution)/shard_map/all_to_all | solution.py:847
  662.6 7.5 %collective-permute-done.71.refs_2_ = bf16[640,512]{1,0:T(8,128)(2,1)S(1)} collective-permute-done((bf16[640,512]{1,0:T(8,128)(2,1)S(1)}, bf16[640,512]{1,0:T(8,128)(2,1)S(1)}, u32[]{:S(2)}, u32[]{:S(2)}) %collective-permute-start.71) | collective-permute-done | bytes 655392 | tf_op jit(solution)/shard_map/ppermute | solution.py:972
  671.2 6.4 far_final.3
  677.6 8.2 %collective-permute-done.70 = bf16[256,1024]{1,0:T(8,128)(2,1)S(1)} collective-permute-done((bf16[256,1024]{1,0:T(8,128)(2,1)S(1)}, bf16[256,1024]{1,0:T(8,128)(2,1)S(1)}, u32[]{:S(2)}, u32[]{:S(2)}) %collective-permute-start.70) | collective-permute-done | bytes 524320 | tf_op jit(solution)/shard_map/ppermute | solution.py:1014
  (459 shorter events, 223.9 us)
Async XLA Ops:
  5.7 33.7 %collective-permute-start.3 = (bf16[2336,256]{1,0:T(8,128)(2,1)}, bf16[2336,256]{1,0:T(8,128)(2,1)}, u32[]{:S(2)}, u32[]{:S(2)}) collective-permute-start(bf16[2336,256]{1,0:T(8,128)(2,1)} %take.6.refs_2_), channel_id=1, source_target_pairs={{0,8},{8,0},{1,9},{9,1},{2,10},{10,2},{3,11},{11,3},{4,12},{12,4},... | collective-permute-start | bytes 3588104 | tf_op jit(solution)/shard_map/ppermute | solution.py:972
  11.5 25.4 %collective-permute-start.2 = (bf16[2,8,1152]{2,0,1:T(2,128)(2,1)S(1)}, bf16[2,8,1152]{2,0,1:T(2,128)(2,1)S(1)}, u32[]{:S(2)}, u32[]{:S(2)}) collective-permute-start(bf16[2,8,1152]{2,0,1:T(2,128)(2,1)S(1)} %broadcast_select_fusion.16), channel_id=1, source_target_pairs={{0,8},{8,0},{1,9},{9,1},{2,10},{10,2},{3,11},{11,3},{4,12},{12,4},... | collective-permute-start | bytes 110600 | tf_op jit(solution)/shard_map/ppermute | solution.py:972
  11.7 29.8 %collective-permute-start = (bf16[256,1024]{1,0:T(8,128)(2,1)S(1)}, bf16[256,1024]{1,0:T(8,128)(2,1)S(1)}, u32[]{:S(2)}, u32[]{:S(2)}) collective-permute-start(bf16[256,1024]{1,0:T(8,128)(2,1)S(1)} %get-tuple-element.229), channel_id=1, source_target_pairs={{0,0},{1,4},{2,1},{3,5},{4,2},{5,6},{6,3},{7,7},{8,8},{9,12},{10,9... | collective-permute-start | bytes 1572872 | tf_op jit(solution)/shard_map/ppermute | solution.py:1001
  12.4 29.1 %collective-permute-start.1 = (bf16[256,1024]{1,0:T(8,128)(2,1)S(1)}, bf16[256,1024]{1,0:T(8,128)(2,1)S(1)}, u32[]{:S(2)}, u32[]{:S(2)}) collective-permute-start(bf16[256,1024]{1,0:T(8,128)(2,1)S(1)} %get-tuple-element.230), channel_id=1, source_target_pairs={{0,4},{1,0},{2,5},{3,1},{4,6},{5,2},{6,7},{7,3},{8,12},{9,8},{10,1... | collective-permute-start | bytes 1572872 | tf_op jit(solution)/shard_map/ppermute | solution.py:1002
  20.8 60.2 %collective-permute-start.10 = (bf16[2048,256]{1,0:T(8,128)(2,1)}, bf16[2048,256]{1,0:T(8,128)(2,1)}, u32[]{:S(2)}, u32[]{:S(2)}) collective-permute-start(bf16[2048,256]{1,0:T(8,128)(2,1)} %take.8.refs_2_), channel_id=1, source_target_pairs={{0,8},{8,0},{1,9},{9,1},{2,10},{10,2},{3,11},{11,3},{4,12},{12,4},... | collective-permute-start | bytes 3145736 | tf_op jit(solution)/shard_map/ppermute | solution.py:972
  36.8 44.2 %collective-permute-start.12 = (bf16[512,1024]{1,0:T(8,128)(2,1)}, bf16[512,1024]{1,0:T(8,128)(2,1)}, u32[]{:S(2)}, u32[]{:S(2)}) collective-permute-start(bf16[512,1024]{1,0:T(8,128)(2,1)} %take.9), channel_id=1, source_target_pairs={{0,8},{8,0},{1,9},{9,1},{2,10},{10,2},{3,11},{11,3},{4,12},{12,4},... | collective-permute-start | bytes 3145736 | tf_op jit(solution)/shard_map/ppermute | solution.py:972
  81.0 40.0 %collective-permute-start.13 = (bf16[512,1024]{1,0:T(8,128)(2,1)}, bf16[512,1024]{1,0:T(8,128)(2,1)}, u32[]{:S(2)}, u32[]{:S(2)}) collective-permute-start(bf16[512,1024]{1,0:T(8,128)(2,1)} %collective-permute-done.12.refs_11_.refs_9_), channel_id=1, source_target_pairs={{0,1},{1,0},{2,3},{3,2},{4,5},{5,4},{6,7},{7,6},{8,9},{9,8},{10,11... | collective-permute-start | bytes 3145736 | tf_op jit(solution)/shard_map/ppermute | solution.py:972
  81.6 33.2 %collective-permute-start.14 = (bf16[2336,256]{1,0:T(8,128)(2,1)S(1)}, bf16[2336,256]{1,0:T(8,128)(2,1)}, u32[]{:S(2)}, u32[]{:S(2)}) collective-permute-start(bf16[2336,256]{1,0:T(8,128)(2,1)S(1)} %copy-done), channel_id=1, source_target_pairs={{0,8},{8,0},{1,9},{9,1},{2,10},{10,2},{3,11},{11,3},{4,12},{12,4},... | collective-permute-start | bytes 3588104 | tf_op jit(solution)/shard_map/ppermute | solution.py:972
  83.3 20.0 %collective-permute-start.6 = (bf16[512,1024]{1,0:T(8,128)(2,1)}, bf16[512,1024]{1,0:T(8,128)(2,1)}, u32[]{:S(2)}, u32[]{:S(2)}) collective-permute-start(bf16[512,1024]{1,0:T(8,128)(2,1)} %get-tuple-element.112.refs_1_.refs_3_), channel_id=1, source_target_pairs={{0,1},{1,0},{2,3},{3,2},{4,5},{5,4},{6,7},{7,6},{8,9},{9,8},{10,11... | collective-permute-start | bytes 3145736 | tf_op jit(solution)/shard_map/ppermute | solution.py:972
  87.0 69.8 %collective-permute-start.22 = (bf16[2048,256]{1,0:T(8,128)(2,1)}, bf16[2048,256]{1,0:T(8,128)(2,1)}, u32[]{:S(2)}, u32[]{:S(2)}) collective-permute-start(bf16[2048,256]{1,0:T(8,128)(2,1)} %take.10.refs_3_), channel_id=1, source_target_pairs={{0,8},{8,0},{1,9},{9,1},{2,10},{10,2},{3,11},{11,3},{4,12},{12,4},... | collective-permute-start | bytes 3145736 | tf_op jit(solution)/shard_map/ppermute | solution.py:972
  114.7 23.7 %collective-permute-start.15 = (bf16[2336,256]{1,0:T(8,128)(2,1)}, bf16[2336,256]{1,0:T(8,128)(2,1)S(1)}, u32[]{:S(2)}, u32[]{:S(2)}) collective-permute-start(bf16[2336,256]{1,0:T(8,128)(2,1)} %collective-permute-done.14.refs_4_.refs_9_), channel_id=1, source_target_pairs={{0,1},{1,0},{2,3},{3,2},{4,5},{5,4},{6,7},{7,6},{8,9},{9,8},{10,11... | collective-permute-start | bytes 3588104 | tf_op jit(solution)/shard_map/ppermute | solution.py:972
  117.6 30.4 %collective-permute-start.17 = (bf16[256,1024]{1,0:T(8,128)(2,1)S(1)}, bf16[256,1024]{1,0:T(8,128)(2,1)S(1)}, u32[]{:S(2)}, u32[]{:S(2)}) collective-permute-start(bf16[256,1024]{1,0:T(8,128)(2,1)S(1)} %get-tuple-element.225), channel_id=1, source_target_pairs={{0,4},{1,0},{2,5},{3,1},{4,6},{5,2},{6,7},{7,3},{8,12},{9,8},{10,1... | collective-permute-start | bytes 1572872 | tf_op jit(solution)/shard_map/ppermute | solution.py:1002
  120.2 27.8 %collective-permute-start.16 = (bf16[256,1024]{1,0:T(8,128)(2,1)S(1)}, bf16[256,1024]{1,0:T(8,128)(2,1)S(1)}, u32[]{:S(2)}, u32[]{:S(2)}) collective-permute-start(bf16[256,1024]{1,0:T(8,128)(2,1)S(1)} %get-tuple-element.226), channel_id=1, source_target_pairs={{0,0},{1,4},{2,1},{3,5},{4,2},{5,6},{6,3},{7,7},{8,8},{9,12},{10,9... | collective-permute-start | bytes 1572872 | tf_op jit(solution)/shard_map/ppermute | solution.py:1001
  134.6 24.7 %collective-permute-start.19 = (bf16[512,1024]{1,0:T(8,128)(2,1)}, bf16[512,1024]{1,0:T(8,128)(2,1)S(1)}, u32[]{:S(2)}, u32[]{:S(2)}) collective-permute-start(bf16[512,1024]{1,0:T(8,128)(2,1)} %get-tuple-element.117), channel_id=1, source_target_pairs={{0,1},{1,0},{2,3},{3,2},{4,5},{5,4},{6,7},{7,6},{8,9},{9,8},{10,11... | collective-permute-start | bytes 3145736 | tf_op jit(solution)/shard_map/ppermute | solution.py:972
  155.3 25.4 %collective-permute-start.21 = (bf16[512,1024]{1,0:T(8,128)(2,1)}, bf16[512,1024]{1,0:T(8,128)(2,1)}, u32[]{:S(2)}, u32[]{:S(2)}) collective-permute-start(bf16[512,1024]{1,0:T(8,128)(2,1)} %take.11), channel_id=1, source_target_pairs={{0,8},{8,0},{1,9},{9,1},{2,10},{10,2},{3,11},{11,3},{4,12},{12,4},... | collective-permute-start | bytes 3145736 | tf_op jit(solution)/shard_map/ppermute | solution.py:972
  180.7 28.6 %collective-permute-start.27 = (bf16[512,1024]{1,0:T(8,128)(2,1)}, bf16[512,1024]{1,0:T(8,128)(2,1)}, u32[]{:S(2)}, u32[]{:S(2)}) collective-permute-start(bf16[512,1024]{1,0:T(8,128)(2,1)} %collective-permute-done.21.refs_8_.refs_11_.refs_9_), channel_id=1, source_target_pairs={{0,1},{1,0},{2,3},{3,2},{4,5},{5,4},{6,7},{7,6},{8,9},{9,8},{10,11... | collective-permute-start | bytes 3145736 | tf_op jit(solution)/shard_map/ppermute | solution.py:972
  224.7 21.0 %collective-permute-start.28 = (bf16[256,1024]{1,0:T(8,128)(2,1)S(1)}, bf16[256,1024]{1,0:T(8,128)(2,1)S(1)}, u32[]{:S(2)}, u32[]{:S(2)}) collective-permute-start(bf16[256,1024]{1,0:T(8,128)(2,1)S(1)} %get-tuple-element.223), channel_id=1, source_target_pairs={{0,0},{4,1},{1,2},{5,3},{2,4},{6,5},{3,6},{7,7},{8,8},{12,9},{9,10... | collective-permute-start | bytes 1572872 | tf_op jit(solution)/shard_map/ppermute | solution.py:1013
  225.4 27.9 %collective-permute-start.29 = (bf16[256,1024]{1,0:T(8,128)(2,1)S(1)}, bf16[256,1024]{1,0:T(8,128)(2,1)S(1)}, u32[]{:S(2)}, u32[]{:S(2)}) collective-permute-start(bf16[256,1024]{1,0:T(8,128)(2,1)S(1)} %get-tuple-element.224), channel_id=1, source_target_pairs={{4,0},{0,1},{5,2},{1,3},{6,4},{2,5},{7,6},{3,7},{12,8},{8,9},{13,1... | collective-permute-start | bytes 1572872 | tf_op jit(solution)/shard_map/ppermute | solution.py:1014
  229.3 28.7 %collective-permute-start.31 = (bf16[512,1024]{1,0:T(8,128)(2,1)S(1)}, bf16[512,1024]{1,0:T(8,128)(2,1)S(1)}, u32[]{:S(2)}, u32[]{:S(2)}) collective-permute-start(bf16[512,1024]{1,0:T(8,128)(2,1)S(1)} %copy-done.57), channel_id=1, source_target_pairs={{0,1},{1,0},{2,3},{3,2},{4,5},{5,4},{6,7},{7,6},{8,9},{9,8},{10,11... | collective-permute-start | bytes 3145736 | tf_op jit(solution)/shard_map/ppermute | solution.py:972
  256.3 35.7 %collective-permute-start.34 = (bf16[128,2048]{1,0:T(8,128)(2,1)S(1)}, bf16[128,2048]{1,0:T(8,128)(2,1)S(1)}, u32[]{:S(2)}, u32[]{:S(2)}) collective-permute-start(bf16[128,2048]{1,0:T(8,128)(2,1)S(1)} %fusion.1), channel_id=1, source_target_pairs={{2,0},{6,4},{3,1},{7,5},{10,8},{14,12},{11,9},{15,13},{18,16},{22,... | collective-permute-start | bytes 1572872 | tf_op jit(solution)/shard_map/ppermute | solution.py:1073
  271.2 21.8 %collective-permute-start.35 = (bf16[1024,512]{1,0:T(8,128)(2,1)}, bf16[1024,512]{1,0:T(8,128)(2,1)S(1)}, u32[]{:S(2)}, u32[]{:S(2)}) collective-permute-start(bf16[1024,512]{1,0:T(8,128)(2,1)} %get-tuple-element.143), channel_id=1, source_target_pairs={{0,8},{8,0},{1,9},{9,1},{2,10},{10,2},{3,11},{11,3},{4,12},{12,4},... | collective-permute-start | bytes 3145736 | tf_op jit(solution)/shard_map/ppermute | solution.py:972
  272.8 20.5 %collective-permute-start.36 = (bf16[512,1024]{1,0:T(8,128)(2,1)}, bf16[512,1024]{1,0:T(8,128)(2,1)S(1)}, u32[]{:S(2)}, u32[]{:S(2)}) collective-permute-start(bf16[512,1024]{1,0:T(8,128)(2,1)} %get-tuple-element.144), channel_id=1, source_target_pairs={{0,16},{16,0},{1,17},{17,1},{2,18},{18,2},{3,19},{19,3},{4,20},{20... | collective-permute-start | bytes 3145736 | tf_op jit(solution)/shard_map/ppermute | solution.py:972
  299.0 24.6 %collective-permute-start.38 = (bf16[512,512]{1,0:T(8,128)(2,1)}, bf16[512,512]{1,0:T(8,128)(2,1)S(1)}, u32[]{:S(2)}, u32[]{:S(2)}) collective-permute-start(bf16[512,512]{1,0:T(8,128)(2,1)} %get-tuple-element.149), channel_id=1, source_target_pairs={{0,8},{8,0},{1,9},{9,1},{2,10},{10,2},{3,11},{11,3},{4,12},{12,4},... | collective-permute-start | bytes 1572872 | tf_op jit(solution)/shard_map/ppermute | solution.py:972
  299.5 24.1 %collective-permute-start.37 = (bf16[512,512]{1,0:T(8,128)(2,1)}, bf16[512,512]{1,0:T(8,128)(2,1)S(1)}, u32[]{:S(2)}, u32[]{:S(2)}) collective-permute-start(bf16[512,512]{1,0:T(8,128)(2,1)} %get-tuple-element.145.refs_22_), channel_id=1, source_target_pairs={{0,16},{16,0},{1,17},{17,1},{2,18},{18,2},{3,19},{19,3},{4,20},{20... | collective-permute-start | bytes 1572872 | tf_op jit(solution)/shard_map/ppermute | solution.py:972
  331.5 35.6 %all-to-all-start = ((bf16[4,256,512]{2,1,0:T(8,128)(2,1)}), bf16[4,256,512]{2,1,0:T(8,128)(2,1)S(1)}, u32[]{:S(2)}, u32[]{:S(2)}) async-start(bf16[4,256,512]{2,1,0:T(8,128)(2,1)} %bitcast.126), calls=%async_computation | async-start | bytes 2097152 | tf_op jit(solution)/shard_map/all_to_all | solution.py:840
  341.4 33.3 %collective-permute-start.40 = (bf16[512,1280]{1,0:T(8,128)(2,1)S(1)}, bf16[512,1280]{1,0:T(8,128)(2,1)}, u32[]{:S(2)}, u32[]{:S(2)}) collective-permute-start(bf16[512,1280]{1,0:T(8,128)(2,1)S(1)} %get-tuple-element.246.refs_4_), channel_id=1, source_target_pairs={{0,1},{1,0},{2,3},{3,2},{4,5},{5,4},{6,7},{7,6},{8,9},{9,8},{10,11... | collective-permute-start | bytes 3932168 | tf_op jit(solution)/shard_map/ppermute | solution.py:972
  370.4 38.2 %all-to-all-start.1 = ((bf16[4,256,512]{2,1,0:T(8,128)(2,1)}), bf16[4,256,512]{2,1,0:T(8,128)(2,1)}, u32[]{:S(2)}, u32[]{:S(2)}) async-start(bf16[4,256,512]{2,1,0:T(8,128)(2,1)} %bitcast.125), calls=%async_computation.1 | async-start | bytes 2097152 | tf_op jit(solution)/shard_map/all_to_all | solution.py:847
  411.2 20.8 %collective-permute-start.45 = (bf16[384,512]{1,0:T(8,128)(2,1)}, bf16[384,512]{1,0:T(8,128)(2,1)S(1)}, u32[]{:S(2)}, u32[]{:S(2)}) collective-permute-start(bf16[384,512]{1,0:T(8,128)(2,1)} %get-tuple-element.166.refs_9_), channel_id=1, source_target_pairs={{0,16},{16,0},{1,17},{17,1},{2,18},{18,2},{3,19},{19,3},{4,20},{20... | collective-permute-start | bytes 1179656 | tf_op jit(solution)/shard_map/ppermute | solution.py:972
  412.8 19.3 %collective-permute-start.46 = (bf16[256,512]{1,0:T(8,128)(2,1)}, bf16[256,512]{1,0:T(8,128)(2,1)S(1)}, u32[]{:S(2)}, u32[]{:S(2)}) collective-permute-start(bf16[256,512]{1,0:T(8,128)(2,1)} %get-tuple-element.169), channel_id=1, source_target_pairs={{0,8},{8,0},{1,9},{9,1},{2,10},{10,2},{3,11},{11,3},{4,12},{12,4},... | collective-permute-start | bytes 786440 | tf_op jit(solution)/shard_map/ppermute | solution.py:972
  429.0 29.9 %collective-permute-start.49 = (bf16[1024,512]{1,0:T(8,128)(2,1)}, bf16[1024,512]{1,0:T(8,128)(2,1)S(1)}, u32[]{:S(2)}, u32[]{:S(2)}) collective-permute-start(bf16[1024,512]{1,0:T(8,128)(2,1)} %get-tuple-element.174), channel_id=1, source_target_pairs={{0,8},{8,0},{1,9},{9,1},{2,10},{10,2},{3,11},{11,3},{4,12},{12,4},... | collective-permute-start | bytes 3145736 | tf_op jit(solution)/shard_map/ppermute | solution.py:972
  429.6 29.4 %collective-permute-start.50 = (bf16[512,1024]{1,0:T(8,128)(2,1)}, bf16[512,1024]{1,0:T(8,128)(2,1)S(1)}, u32[]{:S(2)}, u32[]{:S(2)}) collective-permute-start(bf16[512,1024]{1,0:T(8,128)(2,1)} %get-tuple-element.175), channel_id=1, source_target_pairs={{0,16},{16,0},{1,17},{17,1},{2,18},{18,2},{3,19},{19,3},{4,20},{20... | collective-permute-start | bytes 3145736 | tf_op jit(solution)/shard_map/ppermute | solution.py:972
  435.3 29.6 %all-to-all-start.2 = ((bf16[4,160,512]{2,1,0:T(8,128)(2,1)}), bf16[4,160,512]{2,1,0:T(8,128)(2,1)S(1)}, u32[]{:S(2)}, u32[]{:S(2)}) async-start(bf16[4,160,512]{2,1,0:T(8,128)(2,1)} %bitcast.129), calls=%async_computation.2 | async-start | bytes 1310720 | tf_op jit(solution)/shard_map/all_to_all | solution.py:840
  467.9 27.9 %all-to-all-start.3 = ((bf16[4,160,512]{2,1,0:T(8,128)(2,1)}), bf16[4,160,512]{2,1,0:T(8,128)(2,1)S(1)}, u32[]{:S(2)}, u32[]{:S(2)}) async-start(bf16[4,160,512]{2,1,0:T(8,128)(2,1)} %bitcast.128), calls=%async_computation.3 | async-start | bytes 1310720 | tf_op jit(solution)/shard_map/all_to_all | solution.py:847
  508.4 47.1 %collective-permute-start.57 = (bf16[1024,512]{1,0:T(8,128)(2,1)}, bf16[1024,512]{1,0:T(8,128)(2,1)}, u32[]{:S(2)}, u32[]{:S(2)}) collective-permute-start(bf16[1024,512]{1,0:T(8,128)(2,1)} %bitcast.46.refs_23_.refs_1_), channel_id=1, source_target_pairs={{0,16},{16,0},{1,17},{17,1},{2,18},{18,2},{3,19},{19,3},{4,20},{20... | collective-permute-start | bytes 3145736 | tf_op jit(solution)/shard_map/ppermute | solution.py:972
  524.4 31.0 %all-to-all-start.4 = ((bf16[4,256,512]{2,1,0:T(8,128)(2,1)}), bf16[4,256,512]{2,1,0:T(8,128)(2,1)S(1)}, u32[]{:S(2)}, u32[]{:S(2)}) async-start(bf16[4,256,512]{2,1,0:T(8,128)(2,1)} %bitcast.127), calls=%async_computation.4 | async-start | bytes 2097152 | tf_op jit(solution)/shard_map/all_to_all | solution.py:840
  553.1 29.6 %collective-permute-start.56 = (bf16[256,1024]{1,0:T(8,128)(2,1)}, bf16[256,1024]{1,0:T(8,128)(2,1)}, u32[]{:S(2)}, u32[]{:S(2)}) collective-permute-start(bf16[256,1024]{1,0:T(8,128)(2,1)} %get-tuple-element.186), channel_id=1, source_target_pairs={{0,16},{16,0},{1,17},{17,1},{2,18},{18,2},{3,19},{19,3},{4,20},{20... | collective-permute-start | bytes 1572872 | tf_op jit(solution)/shard_map/ppermute | solution.py:972
  554.1 34.6 %collective-permute-start.55 = (bf16[768,512]{1,0:T(8,128)(2,1)}, bf16[768,512]{1,0:T(8,128)(2,1)}, u32[]{:S(2)}, u32[]{:S(2)}) collective-permute-start(bf16[768,512]{1,0:T(8,128)(2,1)} %get-tuple-element.185), channel_id=1, source_target_pairs={{0,8},{8,0},{1,9},{9,1},{2,10},{10,2},{3,11},{11,3},{4,12},{12,4},... | collective-permute-start | bytes 2359304 | tf_op jit(solution)/shard_map/ppermute | solution.py:972
  558.8 45.6 %all-to-all-start.5 = ((bf16[4,256,512]{2,1,0:T(8,128)(2,1)}), bf16[4,256,512]{2,1,0:T(8,128)(2,1)}, u32[]{:S(2)}, u32[]{:S(2)}) async-start(bf16[4,256,512]{2,1,0:T(8,128)(2,1)} %bitcast.124), calls=%async_computation.5 | async-start | bytes 2097152 | tf_op jit(solution)/shard_map/all_to_all | solution.py:847
  573.1 40.1 %collective-permute-start.67 = (bf16[1024,512]{1,0:T(8,128)(2,1)}, bf16[1024,512]{1,0:T(8,128)(2,1)}, u32[]{:S(2)}, u32[]{:S(2)}) collective-permute-start(bf16[1024,512]{1,0:T(8,128)(2,1)} %bitcast.46.refs_23_.refs_1_), channel_id=1, source_target_pairs={{0,1},{1,0},{2,3},{3,2},{4,5},{5,4},{6,7},{7,6},{8,9},{9,8},{10,11... | collective-permute-start | bytes 3145736 | tf_op jit(solution)/shard_map/ppermute | solution.py:972
  573.1 40.1 %collective-permute-start.68 = (bf16[1024,512]{1,0:T(8,128)(2,1)}, bf16[1024,512]{1,0:T(8,128)(2,1)}, u32[]{:S(2)}, u32[]{:S(2)}) collective-permute-start(bf16[1024,512]{1,0:T(8,128)(2,1)} %collective-permute-done.57.refs_2_), channel_id=1, source_target_pairs={{0,1},{1,0},{2,3},{3,2},{4,5},{5,4},{6,7},{7,6},{8,9},{9,8},{10,11... | collective-permute-start | bytes 3145736 | tf_op jit(solution)/shard_map/ppermute | solution.py:972
  600.4 19.2 %collective-permute-start.65 = (bf16[640,512]{1,0:T(8,128)(2,1)S(1)}, bf16[640,512]{1,0:T(8,128)(2,1)}, u32[]{:S(2)}, u32[]{:S(2)}) collective-permute-start(bf16[640,512]{1,0:T(8,128)(2,1)S(1)} %bitcast.117), channel_id=1, source_target_pairs={{0,1},{1,0},{2,3},{3,2},{4,5},{5,4},{6,7},{7,6},{8,9},{9,8},{10,11... | collective-permute-start | bytes 1966088 | tf_op jit(solution)/shard_map/ppermute | solution.py:972
  604.4 25.8 %collective-permute-start.63 = (bf16[1024,512]{1,0:T(8,128)(2,1)}, bf16[1024,512]{1,0:T(8,128)(2,1)S(1)}, u32[]{:S(2)}, u32[]{:S(2)}) collective-permute-start(bf16[1024,512]{1,0:T(8,128)(2,1)} %bitcast.59.refs_4_.refs_1_), channel_id=1, source_target_pairs={{0,16},{16,0},{1,17},{17,1},{2,18},{18,2},{3,19},{19,3},{4,20},{20... | collective-permute-start | bytes 3145736 | tf_op jit(solution)/shard_map/ppermute | solution.py:972
  608.6 21.4 %all-to-all-start.6 = ((bf16[4,160,512]{2,1,0:T(8,128)(2,1)}), bf16[4,160,512]{2,1,0:T(8,128)(2,1)S(1)}, u32[]{:S(2)}, u32[]{:S(2)}) async-start(bf16[4,160,512]{2,1,0:T(8,128)(2,1)} %bitcast.114), calls=%async_computation.6 | async-start | bytes 1310720 | tf_op jit(solution)/shard_map/all_to_all | solution.py:840
  633.9 20.5 %all-to-all-start.7 = ((bf16[4,160,512]{2,1,0:T(8,128)(2,1)}), bf16[4,160,512]{2,1,0:T(8,128)(2,1)S(1)}, u32[]{:S(2)}, u32[]{:S(2)}) async-start(bf16[4,160,512]{2,1,0:T(8,128)(2,1)} %bitcast.113), calls=%async_computation.7 | async-start | bytes 1310720 | tf_op jit(solution)/shard_map/all_to_all | solution.py:847
  639.4 21.4 %collective-permute-start.74 = (bf16[1024,512]{1,0:T(8,128)(2,1)}, bf16[1024,512]{1,0:T(8,128)(2,1)S(1)}, u32[]{:S(2)}, u32[]{:S(2)}) collective-permute-start(bf16[1024,512]{1,0:T(8,128)(2,1)} %bitcast.59.refs_4_.refs_1_), channel_id=1, source_target_pairs={{0,1},{1,0},{2,3},{3,2},{4,5},{5,4},{6,7},{7,6},{8,9},{9,8},{10,11... | collective-permute-start | bytes 3145736 | tf_op jit(solution)/shard_map/ppermute | solution.py:972
  639.5 30.7 %collective-permute-start.75 = (bf16[1024,512]{1,0:T(8,128)(2,1)}, bf16[1024,512]{1,0:T(8,128)(2,1)S(1)}, u32[]{:S(2)}, u32[]{:S(2)}) collective-permute-start(bf16[1024,512]{1,0:T(8,128)(2,1)} %copy-done.2), channel_id=1, source_target_pairs={{0,1},{1,0},{2,3},{3,2},{4,5},{5,4},{6,7},{7,6},{8,9},{9,8},{10,11... | collective-permute-start | bytes 3145736 | tf_op jit(solution)/shard_map/ppermute | solution.py:972
  657.0 29.9 %collective-permute-start.72 = (bf16[640,512]{1,0:T(8,128)(2,1)S(1)}, bf16[640,512]{1,0:T(8,128)(2,1)S(1)}, u32[]{:S(2)}, u32[]{:S(2)}) collective-permute-start(bf16[640,512]{1,0:T(8,128)(2,1)S(1)} %bitcast.121), channel_id=1, source_target_pairs={{0,1},{1,0},{2,3},{3,2},{4,5},{5,4},{6,7},{7,6},{8,9},{9,8},{10,11... | collective-permute-start | bytes 1966088 | tf_op jit(solution)/shard_map/ppermute | solution.py:972
  660.8 24.9 %collective-permute-start.70 = (bf16[256,1024]{1,0:T(8,128)(2,1)S(1)}, bf16[256,1024]{1,0:T(8,128)(2,1)S(1)}, u32[]{:S(2)}, u32[]{:S(2)}) collective-permute-start(bf16[256,1024]{1,0:T(8,128)(2,1)S(1)} %get-tuple-element.218), channel_id=1, source_target_pairs={{4,0},{0,1},{5,2},{1,3},{6,4},{2,5},{7,6},{3,7},{12,8},{8,9},{13,1... | collective-permute-start | bytes 1572872 | tf_op jit(solution)/shard_map/ppermute | solution.py:1014
  (117 other events, 1246.3 us)
